TPU v7x, 32 devices: a whole 2x2x4 slice. The times are simulated.
32 devices in a mesh: grp: 2 (over y), gx: 8 (over z, x), gy: 2 (over core).
Axes of the slice: x: 2, y: 2, z: 4, core: 2. Of those that a mesh axis runs over, the one named last changes fastest.
Arguments:
- tokens: bfloat16 [2, 16, 8192], P(None, ('grp', 'gx'), 'gy'), parts along dimension 1, may hold values from -2000 to 2000, as said below
- norm_gain: float32 [8192], P('gy'), may hold values from 0.1 to 1.9
- gate_weight: bfloat16 [8192, 26624], P('gy', 'gx'), may hold values from -0.0625 to 0.0625
- up_weight: bfloat16 [8192, 26624], P('gy', 'gx'), may hold values from -0.0625 to 0.0625
- down_weight: bfloat16 [26624, 8192], P('gx', 'gy'), may hold values from -0.0390625 to 0.0390625
Outputs:
- block_out: bfloat16 [2, 16, 8192], P(None, ('grp', 'gx'), 'gy'), parts along dimension 1
There are 2 independent parts, one for each index of `grp`. A program takes and returns all parts, laid end to end along the dimension named above; an argument that names none is the same for every part. Nothing has to cross between parts.
Inputs may be any that keep to these rules, and one draw needn't show every extreme that they name: `tokens`: hidden states of moderate size whose rows and features have unequal scales.
All inputs are finite; a program needn't handle non-finite values.
Results may differ from a plain program's by a relative error of at most 0.0065.
Values may be sent and summed in bfloat16 or wider, within the bound.
No kernel may reach another device: no remote copies, remote signals or barrier semaphores. Data moves between devices by JAX's collectives and lax.ppermute only.
A program may use at most 192 MiB of HBM per device.

v0:
```python
import jax
import jax.numpy as jnp
from jax import lax
from jax.sharding import PartitionSpec as P

D = 8192


epsilon = 1e-05


def project_one(piece, weight):
    return jnp.einsum("srd,du->sru", piece, weight, preferred_element_type=jnp.float32)


def feed_forward(step_block, norm_gain, gate_weight, up_weight, down_weight):
    step_count = step_block.shape[0]
    local_rows = step_block.shape[1]
    half_width = step_block.shape[2]
    unit_count = gate_weight.shape[1]
    gathered = lax.all_gather(step_block, ("gx", "gy"), axis=1, tiled=True)
    groups = lax.axis_size("gx")
    gathered = gathered.reshape(step_count, groups, 2, local_rows, half_width)
    gathered = jnp.transpose(gathered, (0, 1, 3, 2, 4)).reshape(
        step_count, groups * local_rows, 2 * half_width
    )
    widened = gathered.astype(jnp.float32)
    mean_square = jnp.sum(widened * widened, axis=2, keepdims=True) / D
    own_half = lax.dynamic_slice_in_dim(widened, lax.axis_index("gy") * half_width, half_width, 2)
    normed = (own_half * lax.rsqrt(mean_square + epsilon) * norm_gain).astype(jnp.bfloat16)
    gate_up = jnp.concatenate(
        [project_one(normed, gate_weight), project_one(normed, up_weight)], axis=2
    )
    summed = lax.psum(gate_up, "gy")
    hidden = (jax.nn.silu(summed[..., :unit_count]) * summed[..., unit_count:]).astype(jnp.bfloat16)
    row_count = hidden.shape[1]
    flattened = jnp.transpose(hidden, (1, 0, 2)).reshape(row_count * step_count, unit_count)
    per_device = flattened.shape[0] // lax.axis_size("gx")
    own_rows = lax.psum_scatter(
        jnp.dot(flattened, down_weight, preferred_element_type=jnp.float32),
        "gx",
        scatter_dimension=0,
        tiled=True,
    )
    own_rows = own_rows.reshape(per_device // step_count, step_count, half_width)
    return jnp.transpose(own_rows, (1, 0, 2)).astype(jnp.bfloat16)


def body(tokens, norm_gain, gate_weight, up_weight, down_weight):
    return feed_forward(tokens, norm_gain, gate_weight, up_weight, down_weight)


def solution(mesh):
    placed = (P(None, ("grp", "gx"), "gy"), P("gy"), P("gy", "gx"), P("gy", "gx"), P("gx", "gy"))
    return jax.shard_map(
        body, mesh=mesh, in_specs=placed, out_specs=P(None, ("grp", "gx"), "gy"), check_vma=False
    )
```

profile of v0, /device:TPU:0, one launch (start us, length us, event | category | flops | bytes accessed | tf_op | source)
XLA Modules:
  0.0 129.9 jit_solution(8739295010060516610)
XLA Ops:
  6.5 0.0 copy-start
  6.5 0.0 all-reduce.4.cloned.1.call-start
  6.5 24.1 %all_gather.3 = bf16[2,16,4096]{2,0,1:T(2,128)(2,1)S(1)} all-gather(bf16[2,1,4096]{2,0,1:T(2,128)(2,1)} %param.5), channel_id=1, replica_groups=mesh['grp'=2,'gx'=8,'gy'=2] {'gx','gy'}, dimensions={1}, use_global_device_ids=true | all-gather | bytes 278528 | tf_op jit(solution)/shard_map/all_gather | solution.py:21
  30.7 0.4 multiply_reduce_fusion
  31.0 0.2 copy_convert_fusion
  31.2 0.1 copy.16
  31.3 0.1 copy.17
  31.4 0.2 reshape.17
  31.6 0.0 copy-start.1
  31.6 10.7 %fusion = f32[2,8,3328]{2,1,0:T(8,128)S(1)} fusion(bf16[4096,3328]{1,0:T(8,128)(2,1)} %param.8, f32[2,8,8192]{2,1,0:T(8,128)S(1)} %reshape.17, s32[]{:T(128)S(6)} %select_n.3, f32[4096]{0:T(1024)} %param.6, f32[2,8]{1,0:T(2,128)S(1)} %add_rsqrt_fusion), kind=kOutput, calls=%fused_computation | convolution fusion | flops 436404224 | bytes 27755524 | tf_op jit(solution)/shard_map/srd,du->sru/dot_general | solution.py:13
  42.3 0.0 copy-done
  42.3 10.7 %fusion.2 = f32[2,8,3328]{2,1,0:T(8,128)S(1)} fusion(bf16[4096,3328]{1,0:T(8,128)(2,1)} %param.7, f32[2,8,8192]{2,1,0:T(8,128)S(1)} %reshape.17, s32[]{:T(128)S(6)} %select_n.3, f32[4096]{0:T(1024)S(1)} %copy-done, f32[2,8]{1,0:T(2,128)S(1)} %add_rsqrt_fusion), kind=kOutput, calls=%fused_computation.2 | convolution fusion | flops 436404224 | bytes 27755524 | tf_op jit(solution)/shard_map/srd,du->sru/dot_general | solution.py:13
  53.0 0.8 pad_maximum_fusion
  53.8 0.0 all-reduce.4.cloned.1.call-update
  53.8 0.0 copy-done.1
  53.8 0.6 dynamic-slice
  55.1 14.8 %all-reduce.4.cloned.1.call-done = f32[2,8,6656]{2,1,0:T(8,128)} async-done(((f32[2,8,6656]{2,1,0:T(8,128)}), f32[2,8,6656]{2,1,0:T(8,128)}) %all-reduce.4.cloned.1.call-update) | async-done | bytes 426000 | tf_op jit(solution)/shard_map/psum | solution.py:34
  69.8 1.1 fusion.5
  70.9 0.1 copy.14
  71.1 10.6 %fusion.9 = f32[16,4096]{1,0:T(8,128)S(1)} fusion(bf16[16,3328]{1,0:T(8,128)(2,1)S(1)} %reshape.16, bf16[3328,4096]{1,0:T(8,128)(2,1)} %param.9), kind=kOutput, calls=%fused_computation.16 | convolution fusion | flops 436207616 | bytes 27631616 | tf_op jit(solution)/shard_map/dot_general | solution.py:40
  81.7 40.6 %all-reduce.5 = bf16[16,4096]{1,0:T(8,128)(2,1)S(1)} all-reduce(f32[16,4096]{1,0:T(8,128)S(1)} %fusion.9), channel_id=2, replica_groups=mesh['grp'=2,'gx'=8,'gy'=2] {'gx'}, use_global_device_ids=true, to_apply=%region_3.4.clone | all-reduce | flops 65536 | bytes 393216
  122.4 0.6 fusion.6
  (3 shorter events, 0.1 us)
Async XLA Ops:
  6.5 35.8 %copy-start = (f32[4096]{0:T(1024)S(1)}, f32[4096]{0:T(1024)}, u32[]{:S(2)}) copy-start(f32[4096]{0:T(1024)} %param.6) | copy-start | bytes 49156
  6.5 63.3 %all-reduce.4.cloned.1.call-start = ((), (), s32[]{:S(2)}) async-start(), calls=%async_computation | async-start | bytes 851968 | tf_op jit(solution)/shard_map/psum | solution.py:34
  31.6 22.3 %copy-start.1 = (u32[32]{0:T(128)S(1)}, u32[32]{0:T(128)}, u32[]{:S(2)}) copy-start(u32[32]{0:T(128)} %constant.23) | copy-start | bytes 388
Sparse Core Ops, SparseCore 0:
  53.9 15.8 all-reduce.3
where the time goes:
time: 130 us
  blocking collectives  64.8 us (50%)
  matrix products  32 us (25%)
  waiting for transfers between devices  14.8 us (11%)
  between operations  14.1 us (11%)
  other arithmetic  2.43 us (2%)
  local copies, waits for them, and re-layouts  1.69 us (1%)
    unnamed x1, blocking collectives  40.6 us
    all_gather x1, blocking collectives, feed_forward(): gathered = lax.all_gather(step_block, ('gx', 'gy'), axis=1, tiled=True)  24.1 us
    dot_general x2, matrix products, project_one(): jnp.einsum('srd,du->sru', piece, weight, preferred_element_type=jnp.float32)  21.4 us
    psum x1, waiting for transfers between devices, feed_forward(): summed = lax.psum(gate_up, 'gy')  14.8 us
    dot_general x1, matrix products, feed_forward(): jnp.dot(flattened, down_weight, preferred_element_type=jnp.float32)  10.6 us
  transfers between devices with their start and end apart: 1, of which 1 were waited for; matrix products, arithmetic and copies ran while one was open for 0% of the time, Pallas kernels for 0%

commit v1 on v0

v1 whole, which is shorter than its diff:
```python
import functools

import jax
import jax.numpy as jnp
from jax import lax
from jax.experimental import pallas as pl
from jax.experimental.pallas import tpu as pltpu
from jax.sharding import PartitionSpec as P

epsilon = 1e-05
f32, bf16 = jnp.float32, jnp.bfloat16
MiB = 2**20
VMEM = pl.BlockSpec(memory_space=pltpu.VMEM)
HBM = pl.BlockSpec(memory_space=pl.ANY)
Shape = jax.ShapeDtypeStruct

PAD = (512, 1024)
PADS = 32


def call(kernel, outs, *args, pads=(), specs=None, scratch=(), limit=2):
    skip = len(pads)
    specs = specs or [VMEM] * len(args)
    return pl.pallas_call(
        lambda *refs: kernel(*refs[skip:]),
        out_shape=outs,
        in_specs=[VMEM] * skip + specs,
        out_specs=jax.tree.map(lambda _: VMEM, outs),
        scratch_shapes=scratch,
        compiler_params=pltpu.CompilerParams(vmem_limit_bytes=limit * MiB),
    )(*pads, *args)


def empty_kernel(out_ref):
    pass


def squares_kernel(x_ref, sums_ref):
    x = x_ref[...].astype(f32)
    sums_ref[...] = jnp.broadcast_to(jnp.sum(x * x, axis=1, keepdims=True), sums_ref.shape)


def norm_kernel(width, x_ref, own_ref, other_ref, gain_ref, out_ref):
    mean_square = (own_ref[:, :1] + other_ref[:, :1]) / width
    x = x_ref[...].astype(f32)
    out_ref[...] = (x * lax.rsqrt(mean_square + epsilon) * gain_ref[...]).astype(bf16)


def join_kernel(first_ref, second_ref, out_ref):
    rows = first_ref.shape[0]
    out_ref[:rows, :] = first_ref[...]
    out_ref[rows:, :] = second_ref[...]


def project_kernel(x_ref, w_ref, out_ref):
    columns = w_ref.shape[1]
    for c in range(0, columns, 256):
        e = min(c + 256, columns)
        out_ref[:, c:e] = jnp.dot(x_ref[...], w_ref[:, c:e], preferred_element_type=f32)


def down_kernel(chunk, slots, g_ref, g2_ref, u_ref, u2_ref, w_ref, keep_ref, send_ref, acc_ref, h_ref, buf_ref, sems):
    units, width = w_ref.shape
    count = units // chunk

    def copy(k):
        return pltpu.make_async_copy(
            w_ref.at[pl.ds(k * chunk, chunk), :], buf_ref.at[k % slots], sems.at[k % slots]
        )

    for k in range(min(slots, count)):
        copy(k).start()
    v = g_ref[...] + g2_ref[...]
    h_ref[...] = (v / (1.0 + jnp.exp(-v)) * (u_ref[...] + u2_ref[...])).astype(bf16)
    for k in range(count):
        copy(k).wait()
        h = h_ref[:, k * chunk : (k + 1) * chunk]
        for c in range(0, width, 512):
            part = jnp.dot(h, buf_ref[k % slots, :, c : c + 512], preferred_element_type=f32)
            acc_ref[:, c : c + 512] = part if k == 0 else acc_ref[:, c : c + 512] + part
        if k + slots < count:
            copy(k + slots).start()
    rows = keep_ref.shape[0]
    keep_ref[...] = acc_ref[:rows, :]
    send_ref[...] = acc_ref[rows:, :]


def add_kernel(a_ref, b_ref, keep_ref, send_ref):
    rows = keep_ref.shape[0]
    total = a_ref[...] + b_ref[...]
    keep_ref[...] = total[:rows]
    send_ref[...] = total[rows:]


def last_kernel(a_ref, b_ref, out_ref):
    out_ref[...] = (a_ref[...] + b_ref[...]).astype(bf16)


def swap(x, axis, size, mask):
    return lax.ppermute(x, axis, [(i, i ^ mask) for i in range(size)])


def body(tokens, norm_gain, gate_weight, up_weight, down_weight):
    steps, own, half = tokens.shape
    groups, halves = lax.axis_size("gx"), lax.axis_size("gy")
    units = gate_weight.shape[1]
    own_rows = steps * own
    rows = own_rows * groups
    masks = [1 << k for k in range(groups.bit_length() - 1)]
    x = tokens.reshape(own_rows, half)

    pads = (call(empty_kernel, Shape(PAD, f32)),) * PADS
    sums = call(squares_kernel, Shape((own_rows, 128), f32), x, pads=pads)
    held = call(
        functools.partial(norm_kernel, half * halves),
        Shape((own_rows, half), bf16),
        x, sums, swap(sums, "gy", halves, 1), norm_gain.reshape(1, half),
    )
    for mask in reversed(masks):
        held = call(join_kernel, Shape((2 * held.shape[0], half), bf16), held, swap(held, "gx", groups, mask))
    gate = call(project_kernel, Shape((rows, units), f32), held, gate_weight)
    gate_other = swap(gate, "gy", halves, 1)
    up = call(project_kernel, Shape((rows, units), f32), held, up_weight)
    up_other = swap(up, "gy", halves, 1)

    chunk = max(c for c in range(16, 257, 16) if units % c == 0)
    slots = 6
    keep, send = call(
        functools.partial(down_kernel, chunk, slots),
        (Shape((rows // 2, half), f32),) * 2,
        gate, gate_other, up, up_other, down_weight,
        specs=[VMEM] * 4 + [HBM],
        scratch=[
            pltpu.VMEM((rows, half), f32),
            pltpu.VMEM((rows, units), bf16),
            pltpu.VMEM((slots, chunk, half), bf16),
            pltpu.SemaphoreType.DMA((slots,)),
        ],
        limit=42,
    )
    for mask in masks[:-1]:
        part = Shape((keep.shape[0] // 2, half), f32)
        keep, send = call(add_kernel, (part, part), keep, swap(send, "gx", groups, mask))
    out = call(last_kernel, Shape((own_rows, half), bf16), keep, swap(send, "gx", groups, masks[-1]))
    return out.reshape(steps, own, half)


def solution(mesh):
    placed = (P(None, ("grp", "gx"), "gy"), P("gy"), P("gy", "gx"), P("gy", "gx"), P("gx", "gy"))
    return jax.shard_map(
        body, mesh=mesh, in_specs=placed, out_specs=P(None, ("grp", "gx"), "gy"), check_vma=False
    )
```

time: 130 us -> 51.1 us (0.39)
  blocking collectives: 64.8 us -> 0 us
  matrix products: 32 us -> 0 us
  Pallas kernels: 0 us -> 17.7 us
  starting transfers between devices: 0.01 us -> 15.5 us
  between operations: 14.1 us -> 0.24 us
  other arithmetic: 2.43 us -> 0.01 us
  waiting for transfers between devices: 14.8 us -> 16.5 us
    unnamed x1 -> x0, blocking collectives: 40.6 us -> none
    dot_general x3 -> x0, matrix products: 32 us -> none  [the longest x2 21.4 us: project_one(): jnp.einsum('srd,du->sru', piece, weight, preferred_element_type=jnp.float32)]
    all_gather x1 -> x0, blocking collectives: 24.1 us -> none  [feed_forward(): gathered = lax.all_gather(step_block, ('gx', 'gy'), axis=1, tiled=True)]
    pallas_call x0 -> x12, Pallas kernels: none -> 17.7 us  [call(): pl.pallas_call(lambda *refs: kernel(*refs[skip:]), out_shape=outs, in_spe...]
    ppermute x0 -> x9, waiting for transfers between devices: none -> 16.5 us  [swap(): return lax.ppermute(x, axis, [(i, i ^ mask) for i in range(size)])]
    ppermute x0 -> x9, starting transfers between devices: none -> 15.5 us  [swap(): return lax.ppermute(x, axis, [(i, i ^ mask) for i in range(size)])]
    psum x1 -> x0, waiting for transfers between devices: 14.8 us -> none  [feed_forward(): summed = lax.psum(gate_up, 'gy')]
  transfers between devices with their start and end apart: 1 -> 9, of which waited for: 1 -> 9; matrix products, arithmetic and copies ran while one was open for 0% -> 0% of each run, Pallas kernels for 0% -> 0%
where the time goes in v1:
time: 51.1 us; the launch traced here: 50.9 us
  Pallas kernels  17.7 us (35%)
  waiting for transfers between devices  16.5 us (32%)
  starting transfers between devices  15.5 us (30%)
  local copies, waits for them, and re-layouts  0.94 us (2%)
    pallas_call x12, Pallas kernels, call(): pl.pallas_call(lambda *refs: kernel(*refs[skip:]), out_shape=outs, in_spe...  17.7 us
    ppermute x9, waiting for transfers between devices, swap(): return lax.ppermute(x, axis, [(i, i ^ mask) for i in range(size)])  16.5 us
    ppermute x9, starting transfers between devices, swap(): return lax.ppermute(x, axis, [(i, i ^ mask) for i in range(size)])  15.5 us
  transfers between devices with their start and end apart: 9, of which 9 were waited for; matrix products, arithmetic and copies ran while one was open for 0% of the time, Pallas kernels for 0%

profile of v1, /device:TPU:0, one launch (start us, length us, event | category | flops | bytes accessed | tf_op | source)
XLA Modules:
  0.0 50.9 jit_solution(17070747209374475913)
XLA Ops:
  0.0 0.9 %copy-done = bf16[2,1,4096]{2,0,1:T(2,128)(2,1)S(1)} copy-done((bf16[2,1,4096]{2,0,1:T(2,128)(2,1)S(1)}, bf16[2,1,4096]{2,0,1:T(2,128)(2,1)}, u32[]{:S(2)}) %copy-start) | copy-done | bytes 16408
  0.9 0.0 slice-start.4
  0.9 0.0 slice-start.7
  0.9 0.0 slice-start.8
  0.9 0.0 slice-start.9
  0.9 0.0 slice-start.10
  1.0 0.0 slice-start.11
  1.0 0.1 shard_map.56.refs_1_
  1.1 0.5 collective-permute-start
  1.6 0.8 %collective-permute-done.refs_2_ = f32[2,128]{1,0:T(2,128)S(1)} collective-permute-done((f32[2,128]{1,0:T(2,128)S(1)}, f32[2,128]{1,0:T(2,128)S(1)}, u32[]{:S(2)}, u32[]{:S(2)}) %collective-permute-start) | collective-permute-done | bytes 1056 | tf_op jit(solution)/shard_map/ppermute | solution.py:100
  2.4 0.1 shard_map.57.refs_0_
  2.5 4.0 %collective-permute-start.1 = (bf16[2,4096]{1,0:T(2,128)(2,1)S(1)}, bf16[2,4096]{1,0:T(2,128)(2,1)S(1)}, u32[]{:S(2)}, u32[]{:S(2)}) collective-permute-start(bf16[2,4096]{1,0:T(2,128)(2,1)S(1)} %shard_map.57.refs_0_), channel_id=1, source_target_pairs={{0,8},{2,10},{4,12},{6,14},{8,0},{10,2},{12,4},{14,6},{1,9},{3,11}... | collective-permute-start | bytes 49160 | tf_op jit(solution)/shard_map/ppermute | solution.py:100
  6.5 1.7 %collective-permute-done.1.refs_1_ = bf16[2,4096]{1,0:T(2,128)(2,1)S(1)} collective-permute-done((bf16[2,4096]{1,0:T(2,128)(2,1)S(1)}, bf16[2,4096]{1,0:T(2,128)(2,1)S(1)}, u32[]{:S(2)}, u32[]{:S(2)}) %collective-permute-start.1) | collective-permute-done | bytes 16416 | tf_op jit(solution)/shard_map/ppermute | solution.py:100
  8.2 2.0 %collective-permute-start.2 = (bf16[4,4096]{1,0:T(4,128)(2,1)S(1)}, bf16[4,4096]{1,0:T(4,128)(2,1)S(1)}, u32[]{:S(2)}, u32[]{:S(2)}) collective-permute-start(bf16[4,4096]{1,0:T(4,128)(2,1)S(1)} %shard_map.58.refs_0_), channel_id=1, source_target_pairs={{0,4},{2,6},{4,0},{6,2},{8,12},{10,14},{12,8},{14,10},{1,5},{3,7},... | collective-permute-start | bytes 98312 | tf_op jit(solution)/shard_map/ppermute | solution.py:100
  10.2 2.0 %collective-permute-done.2.refs_1_ = bf16[4,4096]{1,0:T(4,128)(2,1)S(1)} collective-permute-done((bf16[4,4096]{1,0:T(4,128)(2,1)S(1)}, bf16[4,4096]{1,0:T(4,128)(2,1)S(1)}, u32[]{:S(2)}, u32[]{:S(2)}) %collective-permute-start.2) | collective-permute-done | bytes 32800 | tf_op jit(solution)/shard_map/ppermute | solution.py:100
  12.2 1.9 %collective-permute-start.3 = (bf16[8,4096]{1,0:T(8,128)(2,1)S(1)}, bf16[8,4096]{1,0:T(8,128)(2,1)S(1)}, u32[]{:S(2)}, u32[]{:S(2)}) collective-permute-start(bf16[8,4096]{1,0:T(8,128)(2,1)S(1)} %shard_map.59.refs_0_), channel_id=1, source_target_pairs={{0,2},{2,0},{4,6},{6,4},{8,10},{10,8},{12,14},{14,12},{1,3},{3,1},... | collective-permute-start | bytes 196616 | tf_op jit(solution)/shard_map/ppermute | solution.py:100
  14.1 2.4 %collective-permute-done.3.refs_1_ = bf16[8,4096]{1,0:T(8,128)(2,1)S(1)} collective-permute-done((bf16[8,4096]{1,0:T(8,128)(2,1)S(1)}, bf16[8,4096]{1,0:T(8,128)(2,1)S(1)}, u32[]{:S(2)}, u32[]{:S(2)}) %collective-permute-start.3) | collective-permute-done | bytes 65568 | tf_op jit(solution)/shard_map/ppermute | solution.py:100
  16.6 0.0 slice-start.12
  16.6 3.6 %shard_map.62.refs_2_ = f32[16,3328]{1,0:T(8,128)S(1)} custom-call(bf16[16,4096]{1,0:T(8,128)(2,1)S(1)} %shard_map.60.refs_0_, bf16[4096,3328]{1,0:T(8,128)(2,1)S(1)} %bitcast.4), custom_call_target="tpu_custom_call" | custom-call | tf_op jit(solution)/shard_map/pallas_call | solution.py:24
  20.3 0.0 slice-done.9
  20.3 3.6 %shard_map.61.refs_0_ = f32[16,3328]{1,0:T(8,128)S(1)} custom-call(bf16[16,4096]{1,0:T(8,128)(2,1)S(1)} %shard_map.60.refs_0_, bf16[4096,3328]{1,0:T(8,128)(2,1)S(1)} %bitcast.6), custom_call_target="tpu_custom_call" | custom-call | tf_op jit(solution)/shard_map/pallas_call | solution.py:24
  24.0 0.5 %collective-permute-start.5 = (f32[16,3328]{1,0:T(8,128)S(1)}, f32[16,3328]{1,0:T(8,128)S(1)}, u32[]{:S(2)}, u32[]{:S(2)}) collective-permute-start(f32[16,3328]{1,0:T(8,128)S(1)} %shard_map.62.refs_2_), channel_id=1, source_target_pairs={{0,1},{1,0},{2,3},{3,2},{4,5},{5,4},{6,7},{7,6},{8,9},{9,8},{10,11... | collective-permute-start | bytes 638984 | tf_op jit(solution)/shard_map/ppermute | solution.py:100
  24.5 1.0 %collective-permute-done.4.refs_1_ = f32[16,3328]{1,0:T(8,128)S(1)} collective-permute-done((f32[16,3328]{1,0:T(8,128)S(1)}, f32[16,3328]{1,0:T(8,128)S(1)}, u32[]{:S(2)}, u32[]{:S(2)}) %collective-permute-start.4) | collective-permute-done | bytes 213024 | tf_op jit(solution)/shard_map/ppermute | solution.py:100
  25.4 0.3 collective-permute-done.5.refs_3_
  25.7 9.5 %shard_map.63 = (f32[8,4096]{1,0:T(8,128)S(1)}, f32[8,4096]{1,0:T(8,128)S(1)}) custom-call(f32[16,3328]{1,0:T(8,128)S(1)} %shard_map.61.refs_0_, f32[16,3328]{1,0:T(8,128)S(1)} %collective-permute-done.4.refs_1_, f32[16,3328]{1,0:T(8,128)S(1)} %shard_map.62.refs_2_, f32[16,3328]{1,0:T(8,128)S(1)} %collective-permute-done.5.refs_3_, bf16[3328,4096]{1,0:T(8,128)(2,1)} %refs_4_.1), custom_call_target="tpu_custom_call" | custom-call | tf_op jit(solution)/shard_map/pallas_call | solution.py:24
  35.2 1.9 %collective-permute-start.6 = (f32[8,4096]{1,0:T(8,128)S(1)}, f32[8,4096]{1,0:T(8,128)S(1)}, u32[]{:S(2)}, u32[]{:S(2)}) collective-permute-start(f32[8,4096]{1,0:T(8,128)S(1)} %get-tuple-element.12), channel_id=1, source_target_pairs={{0,2},{2,0},{4,6},{6,4},{8,10},{10,8},{12,14},{14,12},{1,3},{3,1},... | collective-permute-start | bytes 393224 | tf_op jit(solution)/shard_map/ppermute | solution.py:100
  37.1 3.9 %collective-permute-done.6.refs_1_ = f32[8,4096]{1,0:T(8,128)S(1)} collective-permute-done((f32[8,4096]{1,0:T(8,128)S(1)}, f32[8,4096]{1,0:T(8,128)S(1)}, u32[]{:S(2)}, u32[]{:S(2)}) %collective-permute-start.6) | collective-permute-done | bytes 131104 | tf_op jit(solution)/shard_map/ppermute | solution.py:100
  41.0 1.9 %collective-permute-start.7 = (f32[4,4096]{1,0:T(4,128)S(1)}, f32[4,4096]{1,0:T(4,128)S(1)}, u32[]{:S(2)}, u32[]{:S(2)}) collective-permute-start(f32[4,4096]{1,0:T(4,128)S(1)} %get-tuple-element.14), channel_id=1, source_target_pairs={{0,4},{2,6},{4,0},{6,2},{8,12},{10,14},{12,8},{14,10},{1,5},{3,7},... | collective-permute-start | bytes 196616 | tf_op jit(solution)/shard_map/ppermute | solution.py:100
  42.9 2.4 %collective-permute-done.7.refs_1_ = f32[4,4096]{1,0:T(4,128)S(1)} collective-permute-done((f32[4,4096]{1,0:T(4,128)S(1)}, f32[4,4096]{1,0:T(4,128)S(1)}, u32[]{:S(2)}, u32[]{:S(2)}) %collective-permute-start.7) | collective-permute-done | bytes 65568 | tf_op jit(solution)/shard_map/ppermute | solution.py:100
  45.4 2.9 %collective-permute-start.8 = (f32[2,4096]{1,0:T(2,128)S(1)}, f32[2,4096]{1,0:T(2,128)S(1)}, u32[]{:S(2)}, u32[]{:S(2)}) collective-permute-start(f32[2,4096]{1,0:T(2,128)S(1)} %get-tuple-element.16), channel_id=1, source_target_pairs={{0,8},{2,10},{4,12},{6,14},{8,0},{10,2},{12,4},{14,6},{1,9},{3,11}... | collective-permute-start | bytes 98312 | tf_op jit(solution)/shard_map/ppermute | solution.py:100
  48.3 2.0 %collective-permute-done.8.refs_1_ = f32[2,4096]{1,0:T(2,128)S(1)} collective-permute-done((f32[2,4096]{1,0:T(2,128)S(1)}, f32[2,4096]{1,0:T(2,128)S(1)}, u32[]{:S(2)}, u32[]{:S(2)}) %collective-permute-start.8) | collective-permute-done | bytes 32800 | tf_op jit(solution)/shard_map/ppermute | solution.py:100
  50.2 0.6 %shard_map.66 = bf16[2,4096]{1,0:T(2,128)(2,1)} custom-call(f32[2,4096]{1,0:T(2,128)S(1)} %get-tuple-element.15.refs_0_, f32[2,4096]{1,0:T(2,128)S(1)} %collective-permute-done.8.refs_1_), custom_call_target="tpu_custom_call" | custom-call | tf_op jit(solution)/shard_map/pallas_call | solution.py:24
  (32 shorter events, 0.1 us)
Async XLA Ops:
  0.0 16.5 %slice-start = ((s8[27262976]{0:T(1024)(128)(4,1)}), s8[4194304]{0:T(1024)(128)(4,1)S(1)}, s32[]{:S(2)}) async-start(s8[27262976]{0:T(1024)(128)(4,1)} %bitcast.3), calls=%async_computation | async-start | bytes 8388608
  0.0 0.9 %copy-start = (bf16[2,1,4096]{2,0,1:T(2,128)(2,1)S(1)}, bf16[2,1,4096]{2,0,1:T(2,128)(2,1)}, u32[]{:S(2)}) copy-start(bf16[2,1,4096]{2,0,1:T(2,128)(2,1)} %param.5) | copy-start | bytes 49156
  0.9 1.5 %copy-start.1 = (f32[4096]{0:T(1024)S(1)}, f32[4096]{0:T(1024)}, u32[]{:S(2)}) copy-start(f32[4096]{0:T(1024)} %param.6) | copy-start | bytes 49156
  0.9 15.7 %slice-start.1 = ((s8[27262976]{0:T(1024)(128)(4,1)}), s8[4194304]{0:T(1024)(128)(4,1)S(1)}, s32[]{:S(2)}) async-start(s8[27262976]{0:T(1024)(128)(4,1)} %bitcast.3), calls=%async_computation.1 | async-start | bytes 8388608
  0.9 15.7 %slice-start.2 = ((s8[27262976]{0:T(1024)(128)(4,1)}), s8[4194304]{0:T(1024)(128)(4,1)S(1)}, s32[]{:S(2)}) async-start(s8[27262976]{0:T(1024)(128)(4,1)} %bitcast.3), calls=%async_computation.2 | async-start | bytes 8388608
  0.9 15.7 %slice-start.3 = ((s8[27262976]{0:T(1024)(128)(4,1)}), s8[4194304]{0:T(1024)(128)(4,1)S(1)}, s32[]{:S(2)}) async-start(s8[27262976]{0:T(1024)(128)(4,1)} %bitcast.3), calls=%async_computation.3 | async-start | bytes 8388608
  0.9 15.7 %slice-start.4 = ((s8[27262976]{0:T(1024)(128)(4,1)}), s8[4194304]{0:T(1024)(128)(4,1)S(1)}, s32[]{:S(2)}) async-start(s8[27262976]{0:T(1024)(128)(4,1)} %bitcast.3), calls=%async_computation.4 | async-start | bytes 8388608
  0.9 15.7 %slice-start.5 = ((s8[27262976]{0:T(1024)(128)(4,1)}), s8[4194304]{0:T(1024)(128)(4,1)S(1)}, s32[]{:S(2)}) async-start(s8[27262976]{0:T(1024)(128)(4,1)} %bitcast.3), calls=%async_computation.5 | async-start | bytes 8388608
  0.9 15.7 %slice-start.6 = ((s8[27262976]{0:T(1024)(128)(4,1)}), s8[2097152]{0:T(1024)(128)(4,1)S(1)}, s32[]{:S(2)}) async-start(s8[27262976]{0:T(1024)(128)(4,1)} %bitcast.3), calls=%async_computation.6 | async-start | bytes 4194304
  0.9 19.3 %slice-start.7 = ((s8[27262976]{0:T(1024)(128)(4,1)}), s8[2097152]{0:T(1024)(128)(4,1)S(1)}, s32[]{:S(2)}) async-start(s8[27262976]{0:T(1024)(128)(4,1)} %bitcast.5), calls=%async_computation.7 | async-start | bytes 4194304
  0.9 19.3 %slice-start.8 = ((s8[27262976]{0:T(1024)(128)(4,1)}), s8[4194304]{0:T(1024)(128)(4,1)S(1)}, s32[]{:S(2)}) async-start(s8[27262976]{0:T(1024)(128)(4,1)} %bitcast.5), calls=%async_computation.8 | async-start | bytes 8388608
  0.9 19.3 %slice-start.9 = ((s8[27262976]{0:T(1024)(128)(4,1)}), s8[4194304]{0:T(1024)(128)(4,1)S(1)}, s32[]{:S(2)}) async-start(s8[27262976]{0:T(1024)(128)(4,1)} %bitcast.5), calls=%async_computation.9 | async-start | bytes 8388608
  0.9 19.3 %slice-start.10 = ((s8[27262976]{0:T(1024)(128)(4,1)}), s8[4194304]{0:T(1024)(128)(4,1)S(1)}, s32[]{:S(2)}) async-start(s8[27262976]{0:T(1024)(128)(4,1)} %bitcast.5), calls=%async_computation.10 | async-start | bytes 8388608
  1.0 19.3 %slice-start.11 = ((s8[27262976]{0:T(1024)(128)(4,1)}), s8[4194304]{0:T(1024)(128)(4,1)S(1)}, s32[]{:S(2)}) async-start(s8[27262976]{0:T(1024)(128)(4,1)} %bitcast.5), calls=%async_computation.11 | async-start | bytes 8388608
  1.1 1.3 %collective-permute-start = (f32[2,128]{1,0:T(2,128)S(1)}, f32[2,128]{1,0:T(2,128)S(1)}, u32[]{:S(2)}, u32[]{:S(2)}) collective-permute-start(f32[2,128]{1,0:T(2,128)S(1)} %shard_map.56.refs_1_), channel_id=1, source_target_pairs={{0,1},{1,0},{2,3},{3,2},{4,5},{5,4},{6,7},{7,6},{8,9},{9,8},{10,11... | collective-permute-start | bytes 3080 | tf_op jit(solution)/shard_map/ppermute | solution.py:100
  2.5 5.7 %collective-permute-start.1 = (bf16[2,4096]{1,0:T(2,128)(2,1)S(1)}, bf16[2,4096]{1,0:T(2,128)(2,1)S(1)}, u32[]{:S(2)}, u32[]{:S(2)}) collective-permute-start(bf16[2,4096]{1,0:T(2,128)(2,1)S(1)} %shard_map.57.refs_0_), channel_id=1, source_target_pairs={{0,8},{2,10},{4,12},{6,14},{8,0},{10,2},{12,4},{14,6},{1,9},{3,11}... | collective-permute-start | bytes 49160 | tf_op jit(solution)/shard_map/ppermute | solution.py:100
  8.2 4.0 %collective-permute-start.2 = (bf16[4,4096]{1,0:T(4,128)(2,1)S(1)}, bf16[4,4096]{1,0:T(4,128)(2,1)S(1)}, u32[]{:S(2)}, u32[]{:S(2)}) collective-permute-start(bf16[4,4096]{1,0:T(4,128)(2,1)S(1)} %shard_map.58.refs_0_), channel_id=1, source_target_pairs={{0,4},{2,6},{4,0},{6,2},{8,12},{10,14},{12,8},{14,10},{1,5},{3,7},... | collective-permute-start | bytes 98312 | tf_op jit(solution)/shard_map/ppermute | solution.py:100
  12.2 4.3 %collective-permute-start.3 = (bf16[8,4096]{1,0:T(8,128)(2,1)S(1)}, bf16[8,4096]{1,0:T(8,128)(2,1)S(1)}, u32[]{:S(2)}, u32[]{:S(2)}) collective-permute-start(bf16[8,4096]{1,0:T(8,128)(2,1)S(1)} %shard_map.59.refs_0_), channel_id=1, source_target_pairs={{0,2},{2,0},{4,6},{6,4},{8,10},{10,8},{12,14},{14,12},{1,3},{3,1},... | collective-permute-start | bytes 196616 | tf_op jit(solution)/shard_map/ppermute | solution.py:100
  16.6 3.7 %slice-start.12 = ((s8[27262976]{0:T(1024)(128)(4,1)}), s8[4194304]{0:T(1024)(128)(4,1)S(1)}, s32[]{:S(2)}) async-start(s8[27262976]{0:T(1024)(128)(4,1)} %bitcast.5), calls=%async_computation.12 | async-start | bytes 8388608
  16.6 3.7 %slice-start.13 = ((s8[27262976]{0:T(1024)(128)(4,1)}), s8[4194304]{0:T(1024)(128)(4,1)S(1)}, s32[]{:S(2)}) async-start(s8[27262976]{0:T(1024)(128)(4,1)} %bitcast.5), calls=%async_computation.13 | async-start | bytes 8388608
  23.9 1.5 %collective-permute-start.4 = (f32[16,3328]{1,0:T(8,128)S(1)}, f32[16,3328]{1,0:T(8,128)S(1)}, u32[]{:S(2)}, u32[]{:S(2)}) collective-permute-start(f32[16,3328]{1,0:T(8,128)S(1)} %shard_map.61.refs_0_), channel_id=1, source_target_pairs={{0,1},{1,0},{2,3},{3,2},{4,5},{5,4},{6,7},{7,6},{8,9},{9,8},{10,11... | collective-permute-start | bytes 638984 | tf_op jit(solution)/shard_map/ppermute | solution.py:100
  24.0 1.8 %collective-permute-start.5 = (f32[16,3328]{1,0:T(8,128)S(1)}, f32[16,3328]{1,0:T(8,128)S(1)}, u32[]{:S(2)}, u32[]{:S(2)}) collective-permute-start(f32[16,3328]{1,0:T(8,128)S(1)} %shard_map.62.refs_2_), channel_id=1, source_target_pairs={{0,1},{1,0},{2,3},{3,2},{4,5},{5,4},{6,7},{7,6},{8,9},{9,8},{10,11... | collective-permute-start | bytes 638984 | tf_op jit(solution)/shard_map/ppermute | solution.py:100
  35.2 5.8 %collective-permute-start.6 = (f32[8,4096]{1,0:T(8,128)S(1)}, f32[8,4096]{1,0:T(8,128)S(1)}, u32[]{:S(2)}, u32[]{:S(2)}) collective-permute-start(f32[8,4096]{1,0:T(8,128)S(1)} %get-tuple-element.12), channel_id=1, source_target_pairs={{0,2},{2,0},{4,6},{6,4},{8,10},{10,8},{12,14},{14,12},{1,3},{3,1},... | collective-permute-start | bytes 393224 | tf_op jit(solution)/shard_map/ppermute | solution.py:100
  41.0 4.3 %collective-permute-start.7 = (f32[4,4096]{1,0:T(4,128)S(1)}, f32[4,4096]{1,0:T(4,128)S(1)}, u32[]{:S(2)}, u32[]{:S(2)}) collective-permute-start(f32[4,4096]{1,0:T(4,128)S(1)} %get-tuple-element.14), channel_id=1, source_target_pairs={{0,4},{2,6},{4,0},{6,2},{8,12},{10,14},{12,8},{14,10},{1,5},{3,7},... | collective-permute-start | bytes 196616 | tf_op jit(solution)/shard_map/ppermute | solution.py:100
  45.4 4.9 %collective-permute-start.8 = (f32[2,4096]{1,0:T(2,128)S(1)}, f32[2,4096]{1,0:T(2,128)S(1)}, u32[]{:S(2)}, u32[]{:S(2)}) collective-permute-start(f32[2,4096]{1,0:T(2,128)S(1)} %get-tuple-element.16), channel_id=1, source_target_pairs={{0,8},{2,10},{4,12},{6,14},{8,0},{10,2},{12,4},{14,6},{1,9},{3,11}... | collective-permute-start | bytes 98312 | tf_op jit(solution)/shard_map/ppermute | solution.py:100

commit v2 on v1

v2 whole, which is shorter than its diff:
```python
import functools

import jax
import jax.numpy as jnp
from jax import lax
from jax.experimental import pallas as pl
from jax.experimental.pallas import tpu as pltpu
from jax.sharding import PartitionSpec as P

epsilon = 1e-05
f32, bf16 = jnp.float32, jnp.bfloat16
MiB = 2**20
VMEM = pl.BlockSpec(memory_space=pltpu.VMEM)
HBM = pl.BlockSpec(memory_space=pl.ANY)
Shape = jax.ShapeDtypeStruct

PAD = (512, 1024)
PADS = 48
UP_SHARE, GATE_SHARE = 2, 7


def call(kernel, outs, *args, pads=(), specs=None, scratch=(), limit=2, flops=0):
    skip = len(pads)
    specs = specs or [VMEM] * len(args)
    return pl.pallas_call(
        lambda *refs: kernel(*refs[skip:]),
        out_shape=outs,
        in_specs=[VMEM] * skip + specs,
        out_specs=jax.tree.map(lambda _: VMEM, outs),
        scratch_shapes=scratch,
        cost_estimate=pl.CostEstimate(flops=flops, bytes_accessed=flops // 16, transcendentals=0),
        compiler_params=pltpu.CompilerParams(vmem_limit_bytes=limit * MiB),
    )(*pads, *args)


def empty_kernel(out_ref):
    pass


def squares_kernel(x_ref, sums_ref):
    x = x_ref[...].astype(f32)
    sums_ref[...] = jnp.broadcast_to(jnp.sum(x * x, axis=1, keepdims=True), sums_ref.shape)


def norm_kernel(width, x_ref, own_ref, other_ref, gain_ref, out_ref):
    mean_square = (own_ref[:, :1] + other_ref[:, :1]) / width
    x = x_ref[...].astype(f32)
    out_ref[...] = (x * lax.rsqrt(mean_square + epsilon) * gain_ref[...]).astype(bf16)


def join_kernel(first_ref, second_ref, out_ref):
    rows = first_ref.shape[0]
    out_ref[:rows, :] = first_ref[...]
    out_ref[rows:, :] = second_ref[...]


def project_kernel(ahead, chunk, first, x_ref, w_ref, down_ref, out_ref, *rest):
    copies = []
    if ahead:
        taken_ref, sems = rest
        for k in range(ahead):
            copies.append(
                pltpu.make_async_copy(
                    down_ref.at[pl.ds((first + k) * chunk, chunk), :],
                    taken_ref.at[pl.ds(k * chunk, chunk), :],
                    sems.at[k],
                )
            )
            copies[-1].start()
    columns = w_ref.shape[1]
    for c in range(0, columns, 256):
        e = min(c + 256, columns)
        out_ref[:, c:e] = jnp.dot(x_ref[...], w_ref[:, c:e], preferred_element_type=f32)
    for copy in copies:
        copy.wait()


def down_kernel(chunk, counts, g_ref, g2_ref, u_ref, u2_ref, w_ref, *rest):
    taken, (keep_ref, send_ref, acc_ref, h_ref, buf_ref, sems) = rest[:-6], rest[-6:]
    width = w_ref.shape[1]
    before = sum(counts[:-1])
    copies = []
    for k in range(counts[-1]):
        copies.append(
            pltpu.make_async_copy(w_ref.at[pl.ds((before + k) * chunk, chunk), :], buf_ref.at[k], sems.at[k])
        )
        copies[-1].start()
    v = g_ref[...] + g2_ref[...]
    h_ref[...] = (v / (1.0 + jnp.exp(-v)) * (u_ref[...] + u2_ref[...])).astype(bf16)
    k = 0
    for ref, count in zip((*taken, buf_ref), [n for n in counts if n]):
        for j in range(count):
            if ref is buf_ref:
                copies[j].wait()
                place = (j, slice(None))
            else:
                place = (slice(j * chunk, (j + 1) * chunk),)
            h = h_ref[:, k * chunk : (k + 1) * chunk]
            for c in range(0, width, 512):
                part = jnp.dot(h, ref[(*place, slice(c, c + 512))], preferred_element_type=f32)
                acc_ref[:, c : c + 512] = part if k == 0 else acc_ref[:, c : c + 512] + part
            k += 1
    rows = keep_ref.shape[0]
    keep_ref[...] = acc_ref[:rows, :]
    send_ref[...] = acc_ref[rows:, :].astype(send_ref.dtype)


def add_kernel(a_ref, b_ref, keep_ref, send_ref):
    rows = keep_ref.shape[0]
    total = a_ref[...] + b_ref[...].astype(f32)
    keep_ref[...] = total[:rows]
    send_ref[...] = total[rows:].astype(send_ref.dtype)


def last_kernel(a_ref, b_ref, out_ref):
    out_ref[...] = (a_ref[...] + b_ref[...].astype(f32)).astype(bf16)


def swap(x, axis, size, mask):
    return lax.ppermute(x, axis, [(i, i ^ mask) for i in range(size)])


def body(tokens, norm_gain, gate_weight, up_weight, down_weight):
    steps, own, half = tokens.shape
    groups, halves = lax.axis_size("gx"), lax.axis_size("gy")
    units = gate_weight.shape[1]
    own_rows = steps * own
    rows = own_rows * groups
    masks = [1 << k for k in range(groups.bit_length() - 1)]
    x = tokens.reshape(own_rows, half)

    pads = (call(empty_kernel, Shape(PAD, f32)),) * PADS
    sums = call(squares_kernel, Shape((own_rows, 128), f32), x, pads=pads)
    held = call(
        functools.partial(norm_kernel, half * halves),
        Shape((own_rows, half), bf16),
        x, sums, swap(sums, "gy", halves, 1), norm_gain.reshape(1, half),
    )
    for mask in reversed(masks):
        held = call(join_kernel, Shape((2 * held.shape[0], half), bf16), held, swap(held, "gx", groups, mask))
    chunk = max(c for c in range(16, 257, 16) if units % c == 0)
    count = units // chunk
    counts = (count * UP_SHARE // 13, count * GATE_SHARE // 13)
    counts = (*counts, count - sum(counts))

    def project(weight, first, ahead):
        outs = [Shape((rows, units), f32)]
        scratch = []
        if ahead:
            outs.append(Shape((ahead * chunk, half), bf16))
            scratch.append(pltpu.SemaphoreType.DMA((ahead,)))
        return call(
            functools.partial(project_kernel, ahead, chunk, first),
            outs, held, weight, down_weight,
            specs=[VMEM, VMEM, HBM], scratch=scratch, flops=2 * rows * weight.size,
        )

    up, *taken_up = project(up_weight, 0, counts[0])
    up_other = swap(up, "gy", halves, 1)
    gate, *taken_gate = project(gate_weight, counts[0], counts[1])
    gate_other = swap(gate, "gy", halves, 1)
    taken = (*taken_up, *taken_gate)
    keep, send = call(
        functools.partial(down_kernel, chunk, counts),
        (Shape((rows // 2, half), f32), Shape((rows // 2, half), bf16)),
        gate, gate_other, up, up_other, down_weight, *taken,
        specs=[VMEM] * 4 + [HBM] + [VMEM] * len(taken),
        scratch=[
            pltpu.VMEM((rows, half), f32),
            pltpu.VMEM((rows, units), bf16),
            pltpu.VMEM((counts[-1], chunk, half), bf16),
            pltpu.SemaphoreType.DMA((counts[-1],)),
        ],
        limit=11, flops=2 * rows * down_weight.size,
    )
    for mask in masks[:-1]:
        parts = (Shape((keep.shape[0] // 2, half), f32), Shape((keep.shape[0] // 2, half), bf16))
        keep, send = call(add_kernel, parts, keep, swap(send, "gx", groups, mask))
    out = call(last_kernel, Shape((own_rows, half), bf16), keep, swap(send, "gx", groups, masks[-1]))
    return out.reshape(steps, own, half)


def solution(mesh):
    placed = (P(None, ("grp", "gx"), "gy"), P("gy"), P("gy", "gx"), P("gy", "gx"), P("gx", "gy"))
    return jax.shard_map(
        body, mesh=mesh, in_specs=placed, out_specs=P(None, ("grp", "gx"), "gy"), check_vma=False
    )
```

time: 51.1 us -> 49.9 us (0.977)
  waiting for transfers between devices: 16.5 us -> 14.6 us
  local copies, waits for them, and re-layouts: 0.94 us -> 1.85 us
    ppermute x9, waiting for transfers between devices: 16.5 us -> 14.6 us  [swap(): return lax.ppermute(x, axis, [(i, i ^ mask) for i in range(size)])]
    unnamed x32, local copies, waits for them, and re-layouts: 0.94 us -> 1.85 us
  transfers between devices with their start and end apart: 9 -> 9, of which waited for: 9 -> 8; matrix products, arithmetic and copies ran while one was open for 0% -> 0% of each run, Pallas kernels for 0% -> 14%
where the time goes in v2:
time: 49.9 us; the launch traced here: 49.7 us
  Pallas kernels  17.7 us (35%)
  starting transfers between devices  15.3 us (31%)
  waiting for transfers between devices  14.6 us (29%)
  local copies, waits for them, and re-layouts  1.85 us (4%)
    pallas_call x12, Pallas kernels, call(): pl.pallas_call(lambda *refs: kernel(*refs[skip:]), out_shape=outs, in_spe...  17.7 us
    ppermute x9, starting transfers between devices, swap(): return lax.ppermute(x, axis, [(i, i ^ mask) for i in range(size)])  15.3 us
    ppermute x9, waiting for transfers between devices, swap(): return lax.ppermute(x, axis, [(i, i ^ mask) for i in range(size)])  14.6 us
    unnamed x32, local copies, waits for them, and re-layouts  1.85 us
  transfers between devices with their start and end apart: 9, of which 8 were waited for; matrix products, arithmetic and copies ran while one was open for 0% of the time, Pallas kernels for 14%

profile of v2, /device:TPU:0, one launch (start us, length us, event | category | flops | bytes accessed | tf_op | source)
XLA Modules:
  0.0 49.7 jit_solution(16781480298406935040)
XLA Ops:
  0.0 0.9 %copy-done = bf16[2,1,4096]{2,0,1:T(2,128)(2,1)S(1)} copy-done((bf16[2,1,4096]{2,0,1:T(2,128)(2,1)S(1)}, bf16[2,1,4096]{2,0,1:T(2,128)(2,1)}, u32[]{:S(2)}) %copy-start) | copy-done | bytes 16408
  0.9 0.0 slice-start.4
  0.9 0.0 slice-start.7
  0.9 0.0 slice-start.8
  0.9 0.0 slice-start.9
  0.9 0.0 slice-start.10
  1.0 0.0 slice-start.11
  1.0 0.1 shard_map.56.refs_1_
  1.1 0.5 collective-permute-start
  1.6 0.8 %collective-permute-done.refs_2_ = f32[2,128]{1,0:T(2,128)S(1)} collective-permute-done((f32[2,128]{1,0:T(2,128)S(1)}, f32[2,128]{1,0:T(2,128)S(1)}, u32[]{:S(2)}, u32[]{:S(2)}) %collective-permute-start) | collective-permute-done | bytes 1056 | tf_op jit(solution)/shard_map/ppermute | solution.py:120
  2.4 0.1 shard_map.57.refs_0_
  2.5 4.0 %collective-permute-start.1 = (bf16[2,4096]{1,0:T(2,128)(2,1)S(1)}, bf16[2,4096]{1,0:T(2,128)(2,1)S(1)}, u32[]{:S(2)}, u32[]{:S(2)}) collective-permute-start(bf16[2,4096]{1,0:T(2,128)(2,1)S(1)} %shard_map.57.refs_0_), channel_id=1, source_target_pairs={{0,8},{2,10},{4,12},{6,14},{8,0},{10,2},{12,4},{14,6},{1,9},{3,11}... | collective-permute-start | bytes 49160 | tf_op jit(solution)/shard_map/ppermute | solution.py:120
  6.5 1.7 %collective-permute-done.1.refs_1_ = bf16[2,4096]{1,0:T(2,128)(2,1)S(1)} collective-permute-done((bf16[2,4096]{1,0:T(2,128)(2,1)S(1)}, bf16[2,4096]{1,0:T(2,128)(2,1)S(1)}, u32[]{:S(2)}, u32[]{:S(2)}) %collective-permute-start.1) | collective-permute-done | bytes 16416 | tf_op jit(solution)/shard_map/ppermute | solution.py:120
  8.2 2.0 %collective-permute-start.2 = (bf16[4,4096]{1,0:T(4,128)(2,1)S(1)}, bf16[4,4096]{1,0:T(4,128)(2,1)S(1)}, u32[]{:S(2)}, u32[]{:S(2)}) collective-permute-start(bf16[4,4096]{1,0:T(4,128)(2,1)S(1)} %shard_map.58.refs_0_), channel_id=1, source_target_pairs={{0,4},{2,6},{4,0},{6,2},{8,12},{10,14},{12,8},{14,10},{1,5},{3,7},... | collective-permute-start | bytes 98312 | tf_op jit(solution)/shard_map/ppermute | solution.py:120
  10.2 2.0 %collective-permute-done.2.refs_1_ = bf16[4,4096]{1,0:T(4,128)(2,1)S(1)} collective-permute-done((bf16[4,4096]{1,0:T(4,128)(2,1)S(1)}, bf16[4,4096]{1,0:T(4,128)(2,1)S(1)}, u32[]{:S(2)}, u32[]{:S(2)}) %collective-permute-start.2) | collective-permute-done | bytes 32800 | tf_op jit(solution)/shard_map/ppermute | solution.py:120
  12.2 1.9 %collective-permute-start.3 = (bf16[8,4096]{1,0:T(8,128)(2,1)S(1)}, bf16[8,4096]{1,0:T(8,128)(2,1)S(1)}, u32[]{:S(2)}, u32[]{:S(2)}) collective-permute-start(bf16[8,4096]{1,0:T(8,128)(2,1)S(1)} %shard_map.59.refs_0_), channel_id=1, source_target_pairs={{0,2},{2,0},{4,6},{6,4},{8,10},{10,8},{12,14},{14,12},{1,3},{3,1},... | collective-permute-start | bytes 196616 | tf_op jit(solution)/shard_map/ppermute | solution.py:120
  14.1 2.4 %collective-permute-done.3.refs_1_ = bf16[8,4096]{1,0:T(8,128)(2,1)S(1)} collective-permute-done((bf16[8,4096]{1,0:T(8,128)(2,1)S(1)}, bf16[8,4096]{1,0:T(8,128)(2,1)S(1)}, u32[]{:S(2)}, u32[]{:S(2)}) %collective-permute-start.3) | collective-permute-done | bytes 65568 | tf_op jit(solution)/shard_map/ppermute | solution.py:120
  16.6 0.0 slice-start.12
  16.6 3.7 %shard_map.62 = (f32[16,3328]{1,0:T(8,128)S(1)}, bf16[512,4096]{1,0:T(8,128)(2,1)S(1)}) custom-call(bf16[16,4096]{1,0:T(8,128)(2,1)S(1)} %shard_map.60.refs_0_, bf16[4096,3328]{1,0:T(8,128)(2,1)S(1)} %bitcast.4, bf16[3328,4096]{1,0:T(8,128)(2,1)} %refs_4_.1), custom_call_target="tpu_custom_call" | custom-call | flops 436207616 | bytes 27262976 | tf_op jit(solution)/shard_map/pallas_call | solution.py:25
  20.3 0.1 collective-permute-start.5
  20.4 0.9 %slice-done.13 = s8[4194304]{0:T(1024)(128)(4,1)S(1)} async-done(((s8[27262976]{0:T(1024)(128)(4,1)}), s8[4194304]{0:T(1024)(128)(4,1)S(1)}, s32[]{:S(2)}) %slice-start.13) | async-done | bytes 4194328
  21.4 7.0 %shard_map.61 = (f32[16,3328]{1,0:T(8,128)S(1)}, bf16[1792,4096]{1,0:T(8,128)(2,1)S(1)}) custom-call(bf16[16,4096]{1,0:T(8,128)(2,1)S(1)} %shard_map.60.refs_0_, bf16[4096,3328]{1,0:T(8,128)(2,1)S(1)} %bitcast.6, bf16[3328,4096]{1,0:T(8,128)(2,1)} %refs_4_.1), custom_call_target="tpu_custom_call" | custom-call | flops 436207616 | bytes 27262976 | tf_op jit(solution)/shard_map/pallas_call | solution.py:25
  28.4 0.1 collective-permute-start.4
  28.5 1.4 %collective-permute-done.4.refs_1_ = f32[16,3328]{1,0:T(8,128)S(1)} collective-permute-done((f32[16,3328]{1,0:T(8,128)S(1)}, f32[16,3328]{1,0:T(8,128)S(1)}, u32[]{:S(2)}, u32[]{:S(2)}) %collective-permute-start.4) | collective-permute-done | bytes 213024 | tf_op jit(solution)/shard_map/ppermute | solution.py:120
  29.9 6.1 %shard_map.63 = (f32[8,4096]{1,0:T(8,128)S(1)}, bf16[8,4096]{1,0:T(8,128)(2,1)S(1)}) custom-call(f32[16,3328]{1,0:T(8,128)S(1)} %get-tuple-element.15.refs_0_, f32[16,3328]{1,0:T(8,128)S(1)} %collective-permute-done.4.refs_1_, f32[16,3328]{1,0:T(8,128)S(1)} %get-tuple-element.16.refs_2_, f32[16,3328]{1,0:T(8,128)S(1)} %collective-permute-done.5.refs_3_, ...), custom_call_target="tpu_custom_call" | custom-call | flops 436207616 | bytes 27262976 | tf_op jit(solution)/shard_map/pallas_call | solution.py:25
  36.0 1.9 %collective-permute-start.6 = (bf16[8,4096]{1,0:T(8,128)(2,1)S(1)}, bf16[8,4096]{1,0:T(8,128)(2,1)S(1)}, u32[]{:S(2)}, u32[]{:S(2)}) collective-permute-start(bf16[8,4096]{1,0:T(8,128)(2,1)S(1)} %get-tuple-element.20), channel_id=1, source_target_pairs={{0,2},{2,0},{4,6},{6,4},{8,10},{10,8},{12,14},{14,12},{1,3},{3,1},... | collective-permute-start | bytes 196616 | tf_op jit(solution)/shard_map/ppermute | solution.py:120
  37.9 2.4 %collective-permute-done.6.refs_1_ = bf16[8,4096]{1,0:T(8,128)(2,1)S(1)} collective-permute-done((bf16[8,4096]{1,0:T(8,128)(2,1)S(1)}, bf16[8,4096]{1,0:T(8,128)(2,1)S(1)}, u32[]{:S(2)}, u32[]{:S(2)}) %collective-permute-start.6) | collective-permute-done | bytes 65568 | tf_op jit(solution)/shard_map/ppermute | solution.py:120
  40.3 2.0 %collective-permute-start.7 = (bf16[4,4096]{1,0:T(4,128)(2,1)S(1)}, bf16[4,4096]{1,0:T(4,128)(2,1)S(1)}, u32[]{:S(2)}, u32[]{:S(2)}) collective-permute-start(bf16[4,4096]{1,0:T(4,128)(2,1)S(1)} %get-tuple-element.22), channel_id=1, source_target_pairs={{0,4},{2,6},{4,0},{6,2},{8,12},{10,14},{12,8},{14,10},{1,5},{3,7},... | collective-permute-start | bytes 98312 | tf_op jit(solution)/shard_map/ppermute | solution.py:120
  42.3 2.0 %collective-permute-done.7.refs_1_ = bf16[4,4096]{1,0:T(4,128)(2,1)S(1)} collective-permute-done((bf16[4,4096]{1,0:T(4,128)(2,1)S(1)}, bf16[4,4096]{1,0:T(4,128)(2,1)S(1)}, u32[]{:S(2)}, u32[]{:S(2)}) %collective-permute-start.7) | collective-permute-done | bytes 32800 | tf_op jit(solution)/shard_map/ppermute | solution.py:120
  44.3 3.0 %collective-permute-start.8 = (bf16[2,4096]{1,0:T(2,128)(2,1)S(1)}, bf16[2,4096]{1,0:T(2,128)(2,1)S(1)}, u32[]{:S(2)}, u32[]{:S(2)}) collective-permute-start(bf16[2,4096]{1,0:T(2,128)(2,1)S(1)} %get-tuple-element.24), channel_id=1, source_target_pairs={{0,8},{2,10},{4,12},{6,14},{8,0},{10,2},{12,4},{14,6},{1,9},{3,11}... | collective-permute-start | bytes 49160 | tf_op jit(solution)/shard_map/ppermute | solution.py:120
  47.3 1.7 %collective-permute-done.8.refs_1_ = bf16[2,4096]{1,0:T(2,128)(2,1)S(1)} collective-permute-done((bf16[2,4096]{1,0:T(2,128)(2,1)S(1)}, bf16[2,4096]{1,0:T(2,128)(2,1)S(1)}, u32[]{:S(2)}, u32[]{:S(2)}) %collective-permute-start.8) | collective-permute-done | bytes 16416 | tf_op jit(solution)/shard_map/ppermute | solution.py:120
  49.0 0.6 %shard_map.66 = bf16[2,4096]{1,0:T(2,128)(2,1)} custom-call(f32[2,4096]{1,0:T(2,128)S(1)} %get-tuple-element.23.refs_0_, bf16[2,4096]{1,0:T(2,128)(2,1)S(1)} %collective-permute-done.8.refs_1_), custom_call_target="tpu_custom_call" | custom-call | tf_op jit(solution)/shard_map/pallas_call | solution.py:25
  (32 shorter events, 0.1 us)
Async XLA Ops:
  0.0 16.5 %slice-start = ((s8[27262976]{0:T(1024)(128)(4,1)}), s8[4194304]{0:T(1024)(128)(4,1)S(1)}, s32[]{:S(2)}) async-start(s8[27262976]{0:T(1024)(128)(4,1)} %bitcast.3), calls=%async_computation | async-start | bytes 8388608
  0.0 0.9 %copy-start = (bf16[2,1,4096]{2,0,1:T(2,128)(2,1)S(1)}, bf16[2,1,4096]{2,0,1:T(2,128)(2,1)}, u32[]{:S(2)}) copy-start(bf16[2,1,4096]{2,0,1:T(2,128)(2,1)} %param.5) | copy-start | bytes 49156
  0.9 1.5 %copy-start.1 = (f32[4096]{0:T(1024)S(1)}, f32[4096]{0:T(1024)}, u32[]{:S(2)}) copy-start(f32[4096]{0:T(1024)} %param.6) | copy-start | bytes 49156
  0.9 15.7 %slice-start.1 = ((s8[27262976]{0:T(1024)(128)(4,1)}), s8[4194304]{0:T(1024)(128)(4,1)S(1)}, s32[]{:S(2)}) async-start(s8[27262976]{0:T(1024)(128)(4,1)} %bitcast.3), calls=%async_computation.1 | async-start | bytes 8388608
  0.9 15.7 %slice-start.2 = ((s8[27262976]{0:T(1024)(128)(4,1)}), s8[4194304]{0:T(1024)(128)(4,1)S(1)}, s32[]{:S(2)}) async-start(s8[27262976]{0:T(1024)(128)(4,1)} %bitcast.3), calls=%async_computation.2 | async-start | bytes 8388608
  0.9 15.7 %slice-start.3 = ((s8[27262976]{0:T(1024)(128)(4,1)}), s8[4194304]{0:T(1024)(128)(4,1)S(1)}, s32[]{:S(2)}) async-start(s8[27262976]{0:T(1024)(128)(4,1)} %bitcast.3), calls=%async_computation.3 | async-start | bytes 8388608
  0.9 15.7 %slice-start.4 = ((s8[27262976]{0:T(1024)(128)(4,1)}), s8[4194304]{0:T(1024)(128)(4,1)S(1)}, s32[]{:S(2)}) async-start(s8[27262976]{0:T(1024)(128)(4,1)} %bitcast.3), calls=%async_computation.4 | async-start | bytes 8388608
  0.9 15.7 %slice-start.5 = ((s8[27262976]{0:T(1024)(128)(4,1)}), s8[4194304]{0:T(1024)(128)(4,1)S(1)}, s32[]{:S(2)}) async-start(s8[27262976]{0:T(1024)(128)(4,1)} %bitcast.3), calls=%async_computation.5 | async-start | bytes 8388608
  0.9 15.7 %slice-start.6 = ((s8[27262976]{0:T(1024)(128)(4,1)}), s8[2097152]{0:T(1024)(128)(4,1)S(1)}, s32[]{:S(2)}) async-start(s8[27262976]{0:T(1024)(128)(4,1)} %bitcast.3), calls=%async_computation.6 | async-start | bytes 4194304
  0.9 19.5 %slice-start.7 = ((s8[27262976]{0:T(1024)(128)(4,1)}), s8[2097152]{0:T(1024)(128)(4,1)S(1)}, s32[]{:S(2)}) async-start(s8[27262976]{0:T(1024)(128)(4,1)} %bitcast.5), calls=%async_computation.7 | async-start | bytes 4194304
  0.9 19.5 %slice-start.8 = ((s8[27262976]{0:T(1024)(128)(4,1)}), s8[4194304]{0:T(1024)(128)(4,1)S(1)}, s32[]{:S(2)}) async-start(s8[27262976]{0:T(1024)(128)(4,1)} %bitcast.5), calls=%async_computation.8 | async-start | bytes 8388608
  0.9 19.5 %slice-start.9 = ((s8[27262976]{0:T(1024)(128)(4,1)}), s8[4194304]{0:T(1024)(128)(4,1)S(1)}, s32[]{:S(2)}) async-start(s8[27262976]{0:T(1024)(128)(4,1)} %bitcast.5), calls=%async_computation.9 | async-start | bytes 8388608
  0.9 19.5 %slice-start.10 = ((s8[27262976]{0:T(1024)(128)(4,1)}), s8[4194304]{0:T(1024)(128)(4,1)S(1)}, s32[]{:S(2)}) async-start(s8[27262976]{0:T(1024)(128)(4,1)} %bitcast.5), calls=%async_computation.10 | async-start | bytes 8388608
  1.0 19.5 %slice-start.11 = ((s8[27262976]{0:T(1024)(128)(4,1)}), s8[4194304]{0:T(1024)(128)(4,1)S(1)}, s32[]{:S(2)}) async-start(s8[27262976]{0:T(1024)(128)(4,1)} %bitcast.5), calls=%async_computation.11 | async-start | bytes 8388608
  1.1 1.3 %collective-permute-start = (f32[2,128]{1,0:T(2,128)S(1)}, f32[2,128]{1,0:T(2,128)S(1)}, u32[]{:S(2)}, u32[]{:S(2)}) collective-permute-start(f32[2,128]{1,0:T(2,128)S(1)} %shard_map.56.refs_1_), channel_id=1, source_target_pairs={{0,1},{1,0},{2,3},{3,2},{4,5},{5,4},{6,7},{7,6},{8,9},{9,8},{10,11... | collective-permute-start | bytes 3080 | tf_op jit(solution)/shard_map/ppermute | solution.py:120
  2.5 5.7 %collective-permute-start.1 = (bf16[2,4096]{1,0:T(2,128)(2,1)S(1)}, bf16[2,4096]{1,0:T(2,128)(2,1)S(1)}, u32[]{:S(2)}, u32[]{:S(2)}) collective-permute-start(bf16[2,4096]{1,0:T(2,128)(2,1)S(1)} %shard_map.57.refs_0_), channel_id=1, source_target_pairs={{0,8},{2,10},{4,12},{6,14},{8,0},{10,2},{12,4},{14,6},{1,9},{3,11}... | collective-permute-start | bytes 49160 | tf_op jit(solution)/shard_map/ppermute | solution.py:120
  8.2 4.0 %collective-permute-start.2 = (bf16[4,4096]{1,0:T(4,128)(2,1)S(1)}, bf16[4,4096]{1,0:T(4,128)(2,1)S(1)}, u32[]{:S(2)}, u32[]{:S(2)}) collective-permute-start(bf16[4,4096]{1,0:T(4,128)(2,1)S(1)} %shard_map.58.refs_0_), channel_id=1, source_target_pairs={{0,4},{2,6},{4,0},{6,2},{8,12},{10,14},{12,8},{14,10},{1,5},{3,7},... | collective-permute-start | bytes 98312 | tf_op jit(solution)/shard_map/ppermute | solution.py:120
  12.2 4.3 %collective-permute-start.3 = (bf16[8,4096]{1,0:T(8,128)(2,1)S(1)}, bf16[8,4096]{1,0:T(8,128)(2,1)S(1)}, u32[]{:S(2)}, u32[]{:S(2)}) collective-permute-start(bf16[8,4096]{1,0:T(8,128)(2,1)S(1)} %shard_map.59.refs_0_), channel_id=1, source_target_pairs={{0,2},{2,0},{4,6},{6,4},{8,10},{10,8},{12,14},{14,12},{1,3},{3,1},... | collective-permute-start | bytes 196616 | tf_op jit(solution)/shard_map/ppermute | solution.py:120
  16.6 3.8 %slice-start.12 = ((s8[27262976]{0:T(1024)(128)(4,1)}), s8[4194304]{0:T(1024)(128)(4,1)S(1)}, s32[]{:S(2)}) async-start(s8[27262976]{0:T(1024)(128)(4,1)} %bitcast.5), calls=%async_computation.12 | async-start | bytes 8388608
  16.6 4.7 %slice-start.13 = ((s8[27262976]{0:T(1024)(128)(4,1)}), s8[4194304]{0:T(1024)(128)(4,1)S(1)}, s32[]{:S(2)}) async-start(s8[27262976]{0:T(1024)(128)(4,1)} %bitcast.5), calls=%async_computation.13 | async-start | bytes 8388608
  20.3 8.1 %collective-permute-start.5 = (f32[16,3328]{1,0:T(8,128)S(1)}, f32[16,3328]{1,0:T(8,128)S(1)}, u32[]{:S(2)}, u32[]{:S(2)}) collective-permute-start(f32[16,3328]{1,0:T(8,128)S(1)} %get-tuple-element.16.refs_2_), channel_id=1, source_target_pairs={{0,1},{1,0},{2,3},{3,2},{4,5},{5,4},{6,7},{7,6},{8,9},{9,8},{10,11... | collective-permute-start | bytes 638984 | tf_op jit(solution)/shard_map/ppermute | solution.py:120
  28.4 1.5 %collective-permute-start.4 = (f32[16,3328]{1,0:T(8,128)S(1)}, f32[16,3328]{1,0:T(8,128)S(1)}, u32[]{:S(2)}, u32[]{:S(2)}) collective-permute-start(f32[16,3328]{1,0:T(8,128)S(1)} %get-tuple-element.15.refs_0_), channel_id=1, source_target_pairs={{0,1},{1,0},{2,3},{3,2},{4,5},{5,4},{6,7},{7,6},{8,9},{9,8},{10,11... | collective-permute-start | bytes 638984 | tf_op jit(solution)/shard_map/ppermute | solution.py:120
  36.0 4.3 %collective-permute-start.6 = (bf16[8,4096]{1,0:T(8,128)(2,1)S(1)}, bf16[8,4096]{1,0:T(8,128)(2,1)S(1)}, u32[]{:S(2)}, u32[]{:S(2)}) collective-permute-start(bf16[8,4096]{1,0:T(8,128)(2,1)S(1)} %get-tuple-element.20), channel_id=1, source_target_pairs={{0,2},{2,0},{4,6},{6,4},{8,10},{10,8},{12,14},{14,12},{1,3},{3,1},... | collective-permute-start | bytes 196616 | tf_op jit(solution)/shard_map/ppermute | solution.py:120
  40.3 4.0 %collective-permute-start.7 = (bf16[4,4096]{1,0:T(4,128)(2,1)S(1)}, bf16[4,4096]{1,0:T(4,128)(2,1)S(1)}, u32[]{:S(2)}, u32[]{:S(2)}) collective-permute-start(bf16[4,4096]{1,0:T(4,128)(2,1)S(1)} %get-tuple-element.22), channel_id=1, source_target_pairs={{0,4},{2,6},{4,0},{6,2},{8,12},{10,14},{12,8},{14,10},{1,5},{3,7},... | collective-permute-start | bytes 98312 | tf_op jit(solution)/shard_map/ppermute | solution.py:120
  44.3 4.7 %collective-permute-start.8 = (bf16[2,4096]{1,0:T(2,128)(2,1)S(1)}, bf16[2,4096]{1,0:T(2,128)(2,1)S(1)}, u32[]{:S(2)}, u32[]{:S(2)}) collective-permute-start(bf16[2,4096]{1,0:T(2,128)(2,1)S(1)} %get-tuple-element.24), channel_id=1, source_target_pairs={{0,8},{2,10},{4,12},{6,14},{8,0},{10,2},{12,4},{14,6},{1,9},{3,11}... | collective-permute-start | bytes 49160 | tf_op jit(solution)/shard_map/ppermute | solution.py:120

commit v3 on v2

v3 whole, which is shorter than its diff:
```python
import functools

import jax
import jax.numpy as jnp
from jax import lax
from jax.experimental import pallas as pl
from jax.experimental.pallas import tpu as pltpu
from jax.sharding import PartitionSpec as P

epsilon = 1e-05
f32, bf16 = jnp.float32, jnp.bfloat16
MiB = 2**20
VMEM = pl.BlockSpec(memory_space=pltpu.VMEM)
HBM = pl.BlockSpec(memory_space=pl.ANY)
Shape = jax.ShapeDtypeStruct

PAD = (512, 1024)
PADS = 48
UP_SHARE, GATE_SHARE = 2, 5
DOWN_LIMIT = 15
LANES = 128


def call(kernel, outs, *args, pads=(), specs=None, scratch=(), limit=0, flops=0):
    skip = len(pads)
    specs = specs or [VMEM] * len(args)
    limit = max(limit, 2, *(a.shape[0] // 8 for a in args if a.shape[0] <= 256))
    return pl.pallas_call(
        lambda *refs: kernel(*refs[skip:]),
        out_shape=outs,
        in_specs=[VMEM] * skip + specs,
        out_specs=jax.tree.map(lambda _: VMEM, outs),
        scratch_shapes=scratch,
        cost_estimate=pl.CostEstimate(flops=flops, bytes_accessed=flops // 16, transcendentals=0),
        compiler_params=pltpu.CompilerParams(vmem_limit_bytes=limit * MiB),
    )(*pads, *args)


def empty_kernel(out_ref):
    pass


def mark_kernel(out_ref):
    out_ref[...] = jnp.zeros_like(out_ref)


def join_kernel(first_ref, second_ref, *rest):
    out_ref = rest[-1]
    rows = first_ref.shape[0]
    out_ref[:rows, :] = first_ref[...]
    out_ref[rows:, :] = second_ref[...]


def prepare_kernel(first_ref, second_ref, gain_ref, high_ref, low_ref, sums_ref):
    rows = first_ref.shape[0]
    for ref, at in ((first_ref, slice(0, rows)), (second_ref, slice(rows, None))):
        x = ref[...].astype(f32)
        sums_ref[at, :] = jnp.broadcast_to(jnp.sum(x * x, axis=1, keepdims=True), (rows, LANES))
        scaled = x * gain_ref[...]
        high = scaled.astype(bf16)
        high_ref[at, :] = high
        low_ref[at, :] = (scaled - high.astype(f32)).astype(bf16)


def project_kernel(ahead, chunk, first, high_ref, low_ref, w_ref, down_ref, sums_ref, *rest):
    out_ref, *rest = rest
    copies = []
    if ahead:
        taken_ref, sem = rest
        copies.append(pltpu.make_async_copy(down_ref.at[pl.ds(first * chunk, ahead * chunk), :], taken_ref, sem))
        copies[-1].start()
    x = jnp.concatenate([high_ref[...], low_ref[...]], axis=0)
    rows = high_ref.shape[0]
    out_ref[:, :LANES] = sums_ref[...]
    columns = w_ref.shape[1]
    for c in range(0, columns, 256):
        e = min(c + 256, columns)
        both = jnp.dot(x, w_ref[:, c:e], preferred_element_type=f32)
        out_ref[:, LANES + c : LANES + e] = both[:rows] + both[rows:]
    for copy in copies:
        copy.wait()


def down_kernel(chunk, counts, features, g_ref, g2_ref, u_ref, u2_ref, w_ref, *rest):
    taken, (keep_ref, send_ref, acc_ref, h_ref, buf_ref, sem) = rest[:-6], rest[-6:]
    width = w_ref.shape[1]
    tail = pltpu.make_async_copy(
        w_ref.at[pl.ds(sum(counts[:-1]) * chunk, counts[-1] * chunk), :], buf_ref, sem
    )
    tail.start()
    scale = lax.rsqrt((u_ref[:, :1] + u2_ref[:, :1]) / features + epsilon)
    v = (g_ref[:, LANES:] + g2_ref[:, LANES:]) * scale
    h_ref[...] = (v / (1.0 + jnp.exp(-v)) * ((u_ref[:, LANES:] + u2_ref[:, LANES:]) * scale)).astype(bf16)
    rows = keep_ref.shape[0]
    place = 0
    for c in range(0, width, 512) if taken else ():
        place = 0
        total = None
        for ref in taken:
            part = jnp.dot(
                h_ref[:, place : place + ref.shape[0]], ref[:, c : c + 512], preferred_element_type=f32
            )
            total = part if total is None else total + part
            place += ref.shape[0]
        acc_ref[:, c : c + 512] = total
    tail.wait()
    for c in range(0, width, 512):
        total = jnp.dot(h_ref[:, place:], buf_ref[:, c : c + 512], preferred_element_type=f32)
        if taken:
            total = acc_ref[:, c : c + 512] + total
        keep_ref[:, c : c + 512] = total[:rows]
        send_ref[:, c : c + 512] = total[rows:].astype(send_ref.dtype)


def add_kernel(a_ref, b_ref, keep_ref, send_ref):
    rows = keep_ref.shape[0]
    total = a_ref[...] + b_ref[...].astype(f32)
    keep_ref[...] = total[:rows]
    send_ref[...] = total[rows:].astype(send_ref.dtype)


def last_kernel(a_ref, b_ref, out_ref):
    out_ref[...] = (a_ref[...] + b_ref[...].astype(f32)).astype(bf16)


def swap(x, axis, size, mask):
    return lax.ppermute(x, axis, [(i, i ^ mask) for i in range(size)])


def body(tokens, norm_gain, gate_weight, up_weight, down_weight):
    steps, own, half = tokens.shape
    groups, halves = lax.axis_size("gx"), lax.axis_size("gy")
    units = gate_weight.shape[1]
    own_rows = steps * own
    rows = own_rows * groups
    masks = [1 << k for k in range(groups.bit_length() - 1)]
    x = tokens.reshape(own_rows, half)

    pads = (call(empty_kernel, Shape(PAD, f32)),) * PADS
    mark = call(mark_kernel, Shape((8, LANES), f32), pads=pads)
    held, mark = lax.optimization_barrier((x, mark))
    for mask in reversed(masks[1:]):
        held = call(
            join_kernel, Shape((2 * held.shape[0], half), bf16), held, swap(held, "gx", groups, mask), mark
        )
    part = Shape((rows, half), bf16)
    high, low, sums = call(
        prepare_kernel,
        (part, part, Shape((rows, LANES), f32)),
        held, swap(held, "gx", groups, masks[0]), norm_gain.reshape(1, half),
    )
    chunk = max(c for c in range(16, 257, 16) if units % c == 0)
    count = units // chunk
    counts = (count * UP_SHARE // 13, count * GATE_SHARE // 13)
    counts = (*counts, count - sum(counts))

    def project(weight, first, ahead):
        outs = [Shape((rows, LANES + units), f32)]
        scratch = []
        if ahead:
            outs.append(Shape((ahead * chunk, half), bf16))
            scratch.append(pltpu.SemaphoreType.DMA)
        return call(
            functools.partial(project_kernel, ahead, chunk, first),
            outs, high, low, weight, down_weight, sums,
            specs=[VMEM] * 3 + [HBM, VMEM], scratch=scratch, flops=2 * rows * weight.size,
        )

    up, *taken_up = project(up_weight, 0, counts[0])
    up_other = swap(up, "gy", halves, 1)
    gate, *taken_gate = project(gate_weight, counts[0], counts[1])
    gate_other = swap(gate, "gy", halves, 1)
    taken = (*taken_up, *taken_gate)
    keep, send = call(
        functools.partial(down_kernel, chunk, counts, half * halves),
        (Shape((rows // 2, half), f32), Shape((rows // 2, half), bf16)),
        gate, gate_other, up, up_other, down_weight, *taken,
        specs=[VMEM] * 4 + [HBM] + [VMEM] * len(taken),
        scratch=[
            pltpu.VMEM((rows, half), f32),
            pltpu.VMEM((rows, units), bf16),
            pltpu.VMEM((counts[-1] * chunk, half), bf16),
            pltpu.SemaphoreType.DMA,
        ],
        limit=DOWN_LIMIT, flops=2 * rows * down_weight.size,
    )
    for mask in masks[:-1]:
        parts = (Shape((keep.shape[0] // 2, half), f32), Shape((keep.shape[0] // 2, half), bf16))
        keep, send = call(add_kernel, parts, keep, swap(send, "gx", groups, mask))
    out = call(last_kernel, Shape((own_rows, half), bf16), keep, swap(send, "gx", groups, masks[-1]))
    return out.reshape(steps, own, half)


def solution(mesh):
    placed = (P(None, ("grp", "gx"), "gy"), P("gy"), P("gy", "gx"), P("gy", "gx"), P("gx", "gy"))
    return jax.shard_map(
        body, mesh=mesh, in_specs=placed, out_specs=P(None, ("grp", "gx"), "gy"), check_vma=False
    )
```

time: 49.9 us -> 46.4 us (0.930)
  Pallas kernels: 17.7 us -> 16.1 us
  local copies, waits for them, and re-layouts: 1.85 us -> 0.88 us
  waiting for transfers between devices: 14.6 us -> 13.8 us
    pallas_call x12 -> x11, Pallas kernels: 17.7 us -> 16.1 us  [call(): pl.pallas_call(lambda *refs: kernel(*refs[skip:]), out_shape=outs, in_spe...]
    unnamed x32, local copies, waits for them, and re-layouts: 1.85 us -> 0.88 us
    ppermute x9 -> x8, waiting for transfers between devices: 14.6 us -> 13.8 us  [swap(): return lax.ppermute(x, axis, [(i, i ^ mask) for i in range(size)])]
    ppermute x9 -> x8, starting transfers between devices: 15.3 us -> 15.1 us  [swap(): return lax.ppermute(x, axis, [(i, i ^ mask) for i in range(size)])]
  transfers between devices with their start and end apart: 9 -> 8, of which waited for: 8 -> 7; matrix products, arithmetic and copies ran while one was open for 0% -> 0% of each run, Pallas kernels for 14% -> 10%
where the time goes in v3:
time: 46.4 us; the launch traced here: 46.2 us
  Pallas kernels  16.1 us (35%)
  starting transfers between devices  15.1 us (33%)
  waiting for transfers between devices  13.8 us (30%)
  local copies, waits for them, and re-layouts  0.88 us (2%)
    pallas_call x11, Pallas kernels, call(): pl.pallas_call(lambda *refs: kernel(*refs[skip:]), out_shape=outs, in_spe...  16.1 us
    ppermute x8, starting transfers between devices, swap(): return lax.ppermute(x, axis, [(i, i ^ mask) for i in range(size)])  15.1 us
    ppermute x8, waiting for transfers between devices, swap(): return lax.ppermute(x, axis, [(i, i ^ mask) for i in range(size)])  13.8 us
  transfers between devices with their start and end apart: 8, of which 7 were waited for; matrix products, arithmetic and copies ran while one was open for 0% of the time, Pallas kernels for 10%

profile of v3, /device:TPU:0, one launch (start us, length us, event | category | flops | bytes accessed | tf_op | source)
XLA Modules:
  0.0 46.2 jit_solution(15936899507536720481)
XLA Ops:
  0.0 0.0 slice-start.3
  0.1 0.0 slice-start.6
  0.1 0.0 slice-start.7
  0.1 0.0 slice-start.8
  0.1 0.0 slice-start.9
  0.1 0.0 slice-start.10
  0.1 0.0 slice-start.11
  0.2 0.7 %copy-done = bf16[2,1,4096]{2,0,1:T(2,128)(2,1)S(1)} copy-done((bf16[2,1,4096]{2,0,1:T(2,128)(2,1)S(1)}, bf16[2,1,4096]{2,0,1:T(2,128)(2,1)}, u32[]{:S(2)}) %copy-start) | copy-done | bytes 16408
  0.9 4.0 %collective-permute-start = (bf16[2,4096]{1,0:T(2,128)(2,1)S(1)}, bf16[2,4096]{1,0:T(2,128)(2,1)S(1)}, u32[]{:S(2)}, u32[]{:S(2)}) collective-permute-start(bf16[2,4096]{1,0:T(2,128)(2,1)S(1)} %bitcast.7), channel_id=1, source_target_pairs={{0,8},{2,10},{4,12},{6,14},{8,0},{10,2},{12,4},{14,6},{1,9},{3,11}... | collective-permute-start | bytes 49160 | tf_op jit(solution)/shard_map/ppermute | solution.py:127
  4.9 1.7 %collective-permute-done.refs_1_ = bf16[2,4096]{1,0:T(2,128)(2,1)S(1)} collective-permute-done((bf16[2,4096]{1,0:T(2,128)(2,1)S(1)}, bf16[2,4096]{1,0:T(2,128)(2,1)S(1)}, u32[]{:S(2)}, u32[]{:S(2)}) %collective-permute-start) | collective-permute-done | bytes 16416 | tf_op jit(solution)/shard_map/ppermute | solution.py:127
  6.6 2.0 %collective-permute-start.1 = (bf16[4,4096]{1,0:T(4,128)(2,1)S(1)}, bf16[4,4096]{1,0:T(4,128)(2,1)S(1)}, u32[]{:S(2)}, u32[]{:S(2)}) collective-permute-start(bf16[4,4096]{1,0:T(4,128)(2,1)S(1)} %shard_map.57.refs_0_), channel_id=1, source_target_pairs={{0,4},{2,6},{4,0},{6,2},{8,12},{10,14},{12,8},{14,10},{1,5},{3,7},... | collective-permute-start | bytes 98312 | tf_op jit(solution)/shard_map/ppermute | solution.py:127
  8.6 2.0 %collective-permute-done.1.refs_1_ = bf16[4,4096]{1,0:T(4,128)(2,1)S(1)} collective-permute-done((bf16[4,4096]{1,0:T(4,128)(2,1)S(1)}, bf16[4,4096]{1,0:T(4,128)(2,1)S(1)}, u32[]{:S(2)}, u32[]{:S(2)}) %collective-permute-start.1) | collective-permute-done | bytes 32800 | tf_op jit(solution)/shard_map/ppermute | solution.py:127
  10.6 1.9 %collective-permute-start.2 = (bf16[8,4096]{1,0:T(8,128)(2,1)S(1)}, bf16[8,4096]{1,0:T(8,128)(2,1)S(1)}, u32[]{:S(2)}, u32[]{:S(2)}) collective-permute-start(bf16[8,4096]{1,0:T(8,128)(2,1)S(1)} %shard_map.58.refs_0_), channel_id=1, source_target_pairs={{0,2},{2,0},{4,6},{6,4},{8,10},{10,8},{12,14},{14,12},{1,3},{3,1},... | collective-permute-start | bytes 196616 | tf_op jit(solution)/shard_map/ppermute | solution.py:127
  12.6 2.4 %collective-permute-done.2.refs_1_ = bf16[8,4096]{1,0:T(8,128)(2,1)S(1)} collective-permute-done((bf16[8,4096]{1,0:T(8,128)(2,1)S(1)}, bf16[8,4096]{1,0:T(8,128)(2,1)S(1)}, u32[]{:S(2)}, u32[]{:S(2)}) %collective-permute-start.2) | collective-permute-done | bytes 65568 | tf_op jit(solution)/shard_map/ppermute | solution.py:127
  15.0 0.1 shard_map.59
  15.2 0.0 slice-start.12
  15.2 0.0 slice-start.13
  15.2 4.5 %shard_map.61 = (f32[16,3456]{1,0:T(8,128)S(1)}, bf16[512,4096]{1,0:T(8,128)(2,1)S(1)}) custom-call(bf16[16,4096]{1,0:T(8,128)(2,1)S(1)} %get-tuple-element.22.refs_0_, bf16[16,4096]{1,0:T(8,128)(2,1)S(1)} %get-tuple-element.23.refs_1_, bf16[4096,3328]{1,0:T(8,128)(2,1)S(1)} %bitcast.4, bf16[3328,4096]{1,0:T(8,128)(2,1)} %refs_4_.1, ...), custom_call_target="tpu_custom_call" | custom-call | flops 436207616 | bytes 27262976 | tf_op jit(solution)/shard_map/pallas_call | solution.py:28
  19.7 0.1 collective-permute-start.4
  19.8 0.1 slice-done.13
  19.9 4.5 %shard_map.60 = (f32[16,3456]{1,0:T(8,128)S(1)}, bf16[1280,4096]{1,0:T(8,128)(2,1)S(1)}) custom-call(bf16[16,4096]{1,0:T(8,128)(2,1)S(1)} %get-tuple-element.22.refs_0_, bf16[16,4096]{1,0:T(8,128)(2,1)S(1)} %get-tuple-element.23.refs_1_, bf16[4096,3328]{1,0:T(8,128)(2,1)S(1)} %bitcast.6, bf16[3328,4096]{1,0:T(8,128)(2,1)} %refs_4_.1, ...), custom_call_target="tpu_custom_call" | custom-call | flops 436207616 | bytes 27262976 | tf_op jit(solution)/shard_map/pallas_call | solution.py:28
  24.4 0.5 %collective-permute-start.3 = (f32[16,3456]{1,0:T(8,128)S(1)}, f32[16,3456]{1,0:T(8,128)S(1)}, u32[]{:S(2)}, u32[]{:S(2)}) collective-permute-start(f32[16,3456]{1,0:T(8,128)S(1)} %get-tuple-element.25.refs_0_), channel_id=1, source_target_pairs={{0,1},{1,0},{2,3},{3,2},{4,5},{5,4},{6,7},{7,6},{8,9},{9,8},{10,11... | collective-permute-start | bytes 663560 | tf_op jit(solution)/shard_map/ppermute | solution.py:127
  24.8 0.0 collective-permute-done.4.refs_3_
  24.8 1.1 %collective-permute-done.3.refs_1_ = f32[16,3456]{1,0:T(8,128)S(1)} collective-permute-done((f32[16,3456]{1,0:T(8,128)S(1)}, f32[16,3456]{1,0:T(8,128)S(1)}, u32[]{:S(2)}, u32[]{:S(2)}) %collective-permute-start.3) | collective-permute-done | bytes 221216 | tf_op jit(solution)/shard_map/ppermute | solution.py:127
  25.9 6.3 %shard_map.62 = (f32[8,4096]{1,0:T(8,128)S(1)}, bf16[8,4096]{1,0:T(8,128)(2,1)S(1)}) custom-call(f32[16,3456]{1,0:T(8,128)S(1)} %get-tuple-element.25.refs_0_, f32[16,3456]{1,0:T(8,128)S(1)} %collective-permute-done.3.refs_1_, f32[16,3456]{1,0:T(8,128)S(1)} %get-tuple-element.26.refs_2_, f32[16,3456]{1,0:T(8,128)S(1)} %collective-permute-done.4.refs_3_, ...), custom_call_target="tpu_custom_call" | custom-call | flops 436207616 | bytes 27262976 | tf_op jit(solution)/shard_map/pallas_call | solution.py:28
  32.3 2.0 %collective-permute-start.5 = (bf16[8,4096]{1,0:T(8,128)(2,1)S(1)}, bf16[8,4096]{1,0:T(8,128)(2,1)S(1)}, u32[]{:S(2)}, u32[]{:S(2)}) collective-permute-start(bf16[8,4096]{1,0:T(8,128)(2,1)S(1)} %get-tuple-element.30), channel_id=1, source_target_pairs={{0,2},{2,0},{4,6},{6,4},{8,10},{10,8},{12,14},{14,12},{1,3},{3,1},... | collective-permute-start | bytes 196616 | tf_op jit(solution)/shard_map/ppermute | solution.py:127
  34.2 2.6 %collective-permute-done.5.refs_1_ = bf16[8,4096]{1,0:T(8,128)(2,1)S(1)} collective-permute-done((bf16[8,4096]{1,0:T(8,128)(2,1)S(1)}, bf16[8,4096]{1,0:T(8,128)(2,1)S(1)}, u32[]{:S(2)}, u32[]{:S(2)}) %collective-permute-start.5) | collective-permute-done | bytes 65568 | tf_op jit(solution)/shard_map/ppermute | solution.py:127
  36.9 1.8 %collective-permute-start.6 = (bf16[4,4096]{1,0:T(4,128)(2,1)S(1)}, bf16[4,4096]{1,0:T(4,128)(2,1)S(1)}, u32[]{:S(2)}, u32[]{:S(2)}) collective-permute-start(bf16[4,4096]{1,0:T(4,128)(2,1)S(1)} %get-tuple-element.32), channel_id=1, source_target_pairs={{0,4},{2,6},{4,0},{6,2},{8,12},{10,14},{12,8},{14,10},{1,5},{3,7},... | collective-permute-start | bytes 98312 | tf_op jit(solution)/shard_map/ppermute | solution.py:127
  38.7 2.1 %collective-permute-done.6.refs_1_ = bf16[4,4096]{1,0:T(4,128)(2,1)S(1)} collective-permute-done((bf16[4,4096]{1,0:T(4,128)(2,1)S(1)}, bf16[4,4096]{1,0:T(4,128)(2,1)S(1)}, u32[]{:S(2)}, u32[]{:S(2)}) %collective-permute-start.6) | collective-permute-done | bytes 32800 | tf_op jit(solution)/shard_map/ppermute | solution.py:127
  40.9 2.9 %collective-permute-start.7 = (bf16[2,4096]{1,0:T(2,128)(2,1)S(1)}, bf16[2,4096]{1,0:T(2,128)(2,1)S(1)}, u32[]{:S(2)}, u32[]{:S(2)}) collective-permute-start(bf16[2,4096]{1,0:T(2,128)(2,1)S(1)} %get-tuple-element.34), channel_id=1, source_target_pairs={{0,8},{2,10},{4,12},{6,14},{8,0},{10,2},{12,4},{14,6},{1,9},{3,11}... | collective-permute-start | bytes 49160 | tf_op jit(solution)/shard_map/ppermute | solution.py:127
  43.7 1.8 %collective-permute-done.7.refs_1_ = bf16[2,4096]{1,0:T(2,128)(2,1)S(1)} collective-permute-done((bf16[2,4096]{1,0:T(2,128)(2,1)S(1)}, bf16[2,4096]{1,0:T(2,128)(2,1)S(1)}, u32[]{:S(2)}, u32[]{:S(2)}) %collective-permute-start.7) | collective-permute-done | bytes 16416 | tf_op jit(solution)/shard_map/ppermute | solution.py:127
  45.6 0.6 %shard_map.65 = bf16[2,4096]{1,0:T(2,128)(2,1)} custom-call(f32[2,4096]{1,0:T(2,128)S(1)} %get-tuple-element.33.refs_0_, bf16[2,4096]{1,0:T(2,128)(2,1)S(1)} %collective-permute-done.7.refs_1_), custom_call_target="tpu_custom_call" | custom-call | tf_op jit(solution)/shard_map/pallas_call | solution.py:28
  (29 shorter events, 0.1 us)
Async XLA Ops:
  0.0 15.1 %slice-start = ((s8[27262976]{0:T(1024)(128)(4,1)}), s8[4194304]{0:T(1024)(128)(4,1)S(1)}, s32[]{:S(2)}) async-start(s8[27262976]{0:T(1024)(128)(4,1)} %bitcast.3), calls=%async_computation | async-start | bytes 8388608
  0.0 0.9 %copy-start = (bf16[2,1,4096]{2,0,1:T(2,128)(2,1)S(1)}, bf16[2,1,4096]{2,0,1:T(2,128)(2,1)}, u32[]{:S(2)}) copy-start(bf16[2,1,4096]{2,0,1:T(2,128)(2,1)} %param.5) | copy-start | bytes 49156
  0.0 15.0 %copy-start.1 = (f32[4096]{0:T(1024)S(1)}, f32[4096]{0:T(1024)}, u32[]{:S(2)}) copy-start(f32[4096]{0:T(1024)} %param.6) | copy-start | bytes 49156
  0.0 15.1 %slice-start.1 = ((s8[27262976]{0:T(1024)(128)(4,1)}), s8[4194304]{0:T(1024)(128)(4,1)S(1)}, s32[]{:S(2)}) async-start(s8[27262976]{0:T(1024)(128)(4,1)} %bitcast.3), calls=%async_computation.1 | async-start | bytes 8388608
  0.0 15.1 %slice-start.2 = ((s8[27262976]{0:T(1024)(128)(4,1)}), s8[4194304]{0:T(1024)(128)(4,1)S(1)}, s32[]{:S(2)}) async-start(s8[27262976]{0:T(1024)(128)(4,1)} %bitcast.3), calls=%async_computation.2 | async-start | bytes 8388608
  0.0 15.1 %slice-start.3 = ((s8[27262976]{0:T(1024)(128)(4,1)}), s8[4194304]{0:T(1024)(128)(4,1)S(1)}, s32[]{:S(2)}) async-start(s8[27262976]{0:T(1024)(128)(4,1)} %bitcast.3), calls=%async_computation.3 | async-start | bytes 8388608
  0.0 15.1 %slice-start.4 = ((s8[27262976]{0:T(1024)(128)(4,1)}), s8[4194304]{0:T(1024)(128)(4,1)S(1)}, s32[]{:S(2)}) async-start(s8[27262976]{0:T(1024)(128)(4,1)} %bitcast.3), calls=%async_computation.4 | async-start | bytes 8388608
  0.0 15.1 %slice-start.5 = ((s8[27262976]{0:T(1024)(128)(4,1)}), s8[4194304]{0:T(1024)(128)(4,1)S(1)}, s32[]{:S(2)}) async-start(s8[27262976]{0:T(1024)(128)(4,1)} %bitcast.3), calls=%async_computation.5 | async-start | bytes 8388608
  0.1 15.1 %slice-start.6 = ((s8[27262976]{0:T(1024)(128)(4,1)}), s8[2097152]{0:T(1024)(128)(4,1)S(1)}, s32[]{:S(2)}) async-start(s8[27262976]{0:T(1024)(128)(4,1)} %bitcast.3), calls=%async_computation.6 | async-start | bytes 4194304
  0.1 19.7 %slice-start.7 = ((s8[27262976]{0:T(1024)(128)(4,1)}), s8[2097152]{0:T(1024)(128)(4,1)S(1)}, s32[]{:S(2)}) async-start(s8[27262976]{0:T(1024)(128)(4,1)} %bitcast.5), calls=%async_computation.7 | async-start | bytes 4194304
  0.1 19.7 %slice-start.8 = ((s8[27262976]{0:T(1024)(128)(4,1)}), s8[4194304]{0:T(1024)(128)(4,1)S(1)}, s32[]{:S(2)}) async-start(s8[27262976]{0:T(1024)(128)(4,1)} %bitcast.5), calls=%async_computation.8 | async-start | bytes 8388608
  0.1 19.7 %slice-start.9 = ((s8[27262976]{0:T(1024)(128)(4,1)}), s8[4194304]{0:T(1024)(128)(4,1)S(1)}, s32[]{:S(2)}) async-start(s8[27262976]{0:T(1024)(128)(4,1)} %bitcast.5), calls=%async_computation.9 | async-start | bytes 8388608
  0.1 19.7 %slice-start.10 = ((s8[27262976]{0:T(1024)(128)(4,1)}), s8[4194304]{0:T(1024)(128)(4,1)S(1)}, s32[]{:S(2)}) async-start(s8[27262976]{0:T(1024)(128)(4,1)} %bitcast.5), calls=%async_computation.10 | async-start | bytes 8388608
  0.1 19.7 %slice-start.11 = ((s8[27262976]{0:T(1024)(128)(4,1)}), s8[4194304]{0:T(1024)(128)(4,1)S(1)}, s32[]{:S(2)}) async-start(s8[27262976]{0:T(1024)(128)(4,1)} %bitcast.5), calls=%async_computation.11 | async-start | bytes 8388608
  0.9 5.8 %collective-permute-start = (bf16[2,4096]{1,0:T(2,128)(2,1)S(1)}, bf16[2,4096]{1,0:T(2,128)(2,1)S(1)}, u32[]{:S(2)}, u32[]{:S(2)}) collective-permute-start(bf16[2,4096]{1,0:T(2,128)(2,1)S(1)} %bitcast.7), channel_id=1, source_target_pairs={{0,8},{2,10},{4,12},{6,14},{8,0},{10,2},{12,4},{14,6},{1,9},{3,11}... | collective-permute-start | bytes 49160 | tf_op jit(solution)/shard_map/ppermute | solution.py:127
  6.6 4.0 %collective-permute-start.1 = (bf16[4,4096]{1,0:T(4,128)(2,1)S(1)}, bf16[4,4096]{1,0:T(4,128)(2,1)S(1)}, u32[]{:S(2)}, u32[]{:S(2)}) collective-permute-start(bf16[4,4096]{1,0:T(4,128)(2,1)S(1)} %shard_map.57.refs_0_), channel_id=1, source_target_pairs={{0,4},{2,6},{4,0},{6,2},{8,12},{10,14},{12,8},{14,10},{1,5},{3,7},... | collective-permute-start | bytes 98312 | tf_op jit(solution)/shard_map/ppermute | solution.py:127
  10.6 4.3 %collective-permute-start.2 = (bf16[8,4096]{1,0:T(8,128)(2,1)S(1)}, bf16[8,4096]{1,0:T(8,128)(2,1)S(1)}, u32[]{:S(2)}, u32[]{:S(2)}) collective-permute-start(bf16[8,4096]{1,0:T(8,128)(2,1)S(1)} %shard_map.58.refs_0_), channel_id=1, source_target_pairs={{0,2},{2,0},{4,6},{6,4},{8,10},{10,8},{12,14},{14,12},{1,3},{3,1},... | collective-permute-start | bytes 196616 | tf_op jit(solution)/shard_map/ppermute | solution.py:127
  15.2 4.6 %slice-start.12 = ((s8[27262976]{0:T(1024)(128)(4,1)}), s8[4194304]{0:T(1024)(128)(4,1)S(1)}, s32[]{:S(2)}) async-start(s8[27262976]{0:T(1024)(128)(4,1)} %bitcast.5), calls=%async_computation.12 | async-start | bytes 8388608
  15.2 4.7 %slice-start.13 = ((s8[27262976]{0:T(1024)(128)(4,1)}), s8[4194304]{0:T(1024)(128)(4,1)S(1)}, s32[]{:S(2)}) async-start(s8[27262976]{0:T(1024)(128)(4,1)} %bitcast.5), calls=%async_computation.13 | async-start | bytes 8388608
  19.7 5.2 %collective-permute-start.4 = (f32[16,3456]{1,0:T(8,128)S(1)}, f32[16,3456]{1,0:T(8,128)S(1)}, u32[]{:S(2)}, u32[]{:S(2)}) collective-permute-start(f32[16,3456]{1,0:T(8,128)S(1)} %get-tuple-element.26.refs_2_), channel_id=1, source_target_pairs={{0,1},{1,0},{2,3},{3,2},{4,5},{5,4},{6,7},{7,6},{8,9},{9,8},{10,11... | collective-permute-start | bytes 663560 | tf_op jit(solution)/shard_map/ppermute | solution.py:127
  24.4 1.6 %collective-permute-start.3 = (f32[16,3456]{1,0:T(8,128)S(1)}, f32[16,3456]{1,0:T(8,128)S(1)}, u32[]{:S(2)}, u32[]{:S(2)}) collective-permute-start(f32[16,3456]{1,0:T(8,128)S(1)} %get-tuple-element.25.refs_0_), channel_id=1, source_target_pairs={{0,1},{1,0},{2,3},{3,2},{4,5},{5,4},{6,7},{7,6},{8,9},{9,8},{10,11... | collective-permute-start | bytes 663560 | tf_op jit(solution)/shard_map/ppermute | solution.py:127
  32.3 4.6 %collective-permute-start.5 = (bf16[8,4096]{1,0:T(8,128)(2,1)S(1)}, bf16[8,4096]{1,0:T(8,128)(2,1)S(1)}, u32[]{:S(2)}, u32[]{:S(2)}) collective-permute-start(bf16[8,4096]{1,0:T(8,128)(2,1)S(1)} %get-tuple-element.30), channel_id=1, source_target_pairs={{0,2},{2,0},{4,6},{6,4},{8,10},{10,8},{12,14},{14,12},{1,3},{3,1},... | collective-permute-start | bytes 196616 | tf_op jit(solution)/shard_map/ppermute | solution.py:127
  36.9 4.0 %collective-permute-start.6 = (bf16[4,4096]{1,0:T(4,128)(2,1)S(1)}, bf16[4,4096]{1,0:T(4,128)(2,1)S(1)}, u32[]{:S(2)}, u32[]{:S(2)}) collective-permute-start(bf16[4,4096]{1,0:T(4,128)(2,1)S(1)} %get-tuple-element.32), channel_id=1, source_target_pairs={{0,4},{2,6},{4,0},{6,2},{8,12},{10,14},{12,8},{14,10},{1,5},{3,7},... | collective-permute-start | bytes 98312 | tf_op jit(solution)/shard_map/ppermute | solution.py:127
  40.9 4.7 %collective-permute-start.7 = (bf16[2,4096]{1,0:T(2,128)(2,1)S(1)}, bf16[2,4096]{1,0:T(2,128)(2,1)S(1)}, u32[]{:S(2)}, u32[]{:S(2)}) collective-permute-start(bf16[2,4096]{1,0:T(2,128)(2,1)S(1)} %get-tuple-element.34), channel_id=1, source_target_pairs={{0,8},{2,10},{4,12},{6,14},{8,0},{10,2},{12,4},{14,6},{1,9},{3,11}... | collective-permute-start | bytes 49160 | tf_op jit(solution)/shard_map/ppermute | solution.py:127

commit v4 on v2

v4 whole, which is shorter than its diff:
```python
import functools

import jax
import jax.numpy as jnp
from jax import lax
from jax.experimental import pallas as pl
from jax.experimental.pallas import tpu as pltpu
from jax.sharding import PartitionSpec as P

epsilon = 1e-05
f32, bf16 = jnp.float32, jnp.bfloat16
MiB = 2**20
VMEM = pl.BlockSpec(memory_space=pltpu.VMEM)
HBM = pl.BlockSpec(memory_space=pl.ANY)
Shape = jax.ShapeDtypeStruct

PAD = (512, 1024)
PADS = 48
UP_SHARE, GATE_SHARE = 2, 5
DOWN_LIMIT = 15


def call(kernel, outs, *args, pads=(), specs=None, scratch=(), limit=0, flops=0):
    skip = len(pads)
    specs = specs or [VMEM] * len(args)
    limit = max(limit, 2, *(a.shape[0] // 8 for a in args if a.shape[0] <= 256))
    return pl.pallas_call(
        lambda *refs: kernel(*refs[skip:]),
        out_shape=outs,
        in_specs=[VMEM] * skip + specs,
        out_specs=jax.tree.map(lambda _: VMEM, outs),
        scratch_shapes=scratch,
        cost_estimate=pl.CostEstimate(flops=flops, bytes_accessed=flops // 16, transcendentals=0),
        compiler_params=pltpu.CompilerParams(vmem_limit_bytes=limit * MiB),
    )(*pads, *args)


def empty_kernel(out_ref):
    pass


def mark_kernel(out_ref):
    out_ref[...] = jnp.zeros_like(out_ref)


def pack_kernel(mark_ref, x_ref, gain_ref, out_ref):
    rows = x_ref.shape[0]
    out_ref[:rows, :] = x_ref[...].astype(f32)
    out_ref[rows:, :] = gain_ref[...]


def norm_kernel(own_ref, other_ref, own_out_ref, other_out_ref):
    rows = own_out_ref.shape[0]
    halves = [ref[:rows, :] for ref in (own_ref, other_ref)]
    features = 2 * own_ref.shape[1]
    mean_square = sum(jnp.sum(x * x, axis=1, keepdims=True) for x in halves) / features
    scale = lax.rsqrt(mean_square + epsilon)
    for x, ref, out_ref in zip(halves, (own_ref, other_ref), (own_out_ref, other_out_ref)):
        out_ref[...] = (x * scale * ref[rows:, :]).astype(bf16)


def join_kernel(first_ref, second_ref, out_ref):
    rows = first_ref.shape[0]
    out_ref[:rows, :] = first_ref[...]
    out_ref[rows:, :] = second_ref[...]


def project_kernel(ahead, chunk, first, x_ref, w_ref, down_ref, out_ref, *rest):
    copies = []
    if ahead:
        taken_ref, sem = rest
        copies.append(pltpu.make_async_copy(down_ref.at[pl.ds(first * chunk, ahead * chunk), :], taken_ref, sem))
        copies[-1].start()
    columns = w_ref.shape[1]
    for c in range(0, columns, 256):
        e = min(c + 256, columns)
        out_ref[:, c:e] = jnp.dot(x_ref[...], w_ref[:, c:e], preferred_element_type=f32)
    for copy in copies:
        copy.wait()


def down_kernel(bounds, g_ref, g2_ref, u_ref, u2_ref, w_ref, *rest):
    taken, (keep_ref, send_ref, acc_ref, h_ref, buf_ref, sems) = rest[:-6], rest[-6:]
    width = w_ref.shape[1]
    start = bounds[0]
    copies = [
        pltpu.make_async_copy(w_ref.at[pl.ds(a, b - a), :], buf_ref.at[pl.ds(a - start, b - a), :], sems.at[k])
        for k, (a, b) in enumerate(zip(bounds, bounds[1:]))
    ]
    for copy in copies:
        copy.start()
    v = g_ref[...] + g2_ref[...]
    h_ref[...] = (v / (1.0 + jnp.exp(-v)) * (u_ref[...] + u2_ref[...])).astype(bf16)
    rows = keep_ref.shape[0]
    passes = [(copy, [(buf_ref, a - start, a, b)]) for copy, a, b in zip(copies, bounds, bounds[1:])]
    if taken:
        place, parts = 0, []
        for ref in taken:
            parts.append((ref, 0, place, place + ref.shape[0]))
            place += ref.shape[0]
        passes.insert(0, (None, parts))
    for k, (copy, parts) in enumerate(passes):
        if copy is not None:
            copy.wait()
        for c in range(0, width, 512):
            total = acc_ref[:, c : c + 512] if k else None
            for ref, at, a, b in parts:
                part = jnp.dot(h_ref[:, a:b], ref[at : at + b - a, c : c + 512], preferred_element_type=f32)
                total = part if total is None else total + part
            if k < len(passes) - 1:
                acc_ref[:, c : c + 512] = total
            else:
                keep_ref[:, c : c + 512] = total[:rows]
                send_ref[:, c : c + 512] = total[rows:].astype(send_ref.dtype)


def add_kernel(a_ref, b_ref, keep_ref, send_ref):
    rows = keep_ref.shape[0]
    total = a_ref[...] + b_ref[...].astype(f32)
    keep_ref[...] = total[:rows]
    send_ref[...] = total[rows:].astype(send_ref.dtype)


def last_kernel(a_ref, b_ref, out_ref):
    out_ref[...] = (a_ref[...] + b_ref[...].astype(f32)).astype(bf16)


def cross(x, groups, mask):
    return lax.ppermute(
        x, ("gx", "gy"), [(2 * i + c, 2 * (i ^ mask) + 1 - c) for i in range(groups) for c in range(2)]
    )


def swap(x, axis, size, mask):
    return lax.ppermute(x, axis, [(i, i ^ mask) for i in range(size)])


def body(tokens, norm_gain, gate_weight, up_weight, down_weight):
    steps, local, half = tokens.shape
    groups, halves = lax.axis_size("gx"), lax.axis_size("gy")
    units = gate_weight.shape[1]
    own_rows = steps * local
    rows = own_rows * groups
    masks = [1 << k for k in range(groups.bit_length() - 1)]
    x = tokens.reshape(own_rows, half)

    pads = (call(empty_kernel, Shape(PAD, f32)),) * PADS
    mark = call(mark_kernel, Shape((8, 128), f32), pads=pads)
    packed = call(pack_kernel, Shape((own_rows + 1, half), f32), mark, x, norm_gain.reshape(1, half))
    own, other = call(
        norm_kernel, (Shape((own_rows, half), bf16),) * 2, packed, swap(packed, "gy", halves, 1)
    )
    held = call(join_kernel, Shape((2 * own_rows, half), bf16), own, cross(other, groups, masks[-1]))
    for mask in reversed(masks[:-1]):
        held = call(join_kernel, Shape((2 * held.shape[0], half), bf16), held, swap(held, "gx", groups, mask))
    chunk = max(c for c in range(16, 257, 16) if units % c == 0)
    count = units // chunk
    counts = (count * UP_SHARE // 13, count * GATE_SHARE // 13)
    counts = (*counts, count - sum(counts))

    def project(weight, first, ahead):
        outs = [Shape((rows, units), f32)]
        scratch = []
        if ahead:
            outs.append(Shape((ahead * chunk, half), bf16))
            scratch.append(pltpu.SemaphoreType.DMA)
        return call(
            functools.partial(project_kernel, ahead, chunk, first),
            outs, held, weight, down_weight,
            specs=[VMEM, VMEM, HBM], scratch=scratch, flops=2 * rows * weight.size,
        )

    up, *taken_up = project(up_weight, 0, counts[0])
    up_other = swap(up, "gy", halves, 1)
    gate, *taken_gate = project(gate_weight, counts[0], counts[1])
    gate_other = swap(gate, "gy", halves, 1)
    taken = (*taken_up, *taken_gate)
    start = sum(counts[:-1]) * chunk
    bounds = (*range(start, units, 2 * chunk), units)
    keep, send = call(
        functools.partial(down_kernel, bounds),
        (Shape((rows // 2, half), f32), Shape((rows // 2, half), bf16)),
        gate, gate_other, up, up_other, down_weight, *taken,
        specs=[VMEM] * 4 + [HBM] + [VMEM] * len(taken),
        scratch=[
            pltpu.VMEM((rows, half), f32),
            pltpu.VMEM((rows, units), bf16),
            pltpu.VMEM((units - start, half), bf16),
            pltpu.SemaphoreType.DMA((len(bounds) - 1,)),
        ],
        limit=DOWN_LIMIT, flops=2 * rows * down_weight.size,
    )
    for mask in masks[:-1]:
        parts = (Shape((keep.shape[0] // 2, half), f32), Shape((keep.shape[0] // 2, half), bf16))
        keep, send = call(add_kernel, parts, keep, swap(send, "gx", groups, mask))
    out = call(last_kernel, Shape((own_rows, half), bf16), keep, swap(send, "gx", groups, masks[-1]))
    return out.reshape(steps, local, half)


def solution(mesh):
    placed = (P(None, ("grp", "gx"), "gy"), P("gy"), P("gy", "gx"), P("gy", "gx"), P("gx", "gy"))
    return jax.shard_map(
        body, mesh=mesh, in_specs=placed, out_specs=P(None, ("grp", "gx"), "gy"), check_vma=False
    )
```

time: 49.9 us -> 46.3 us (0.928)
  Pallas kernels: 17.7 us -> 14.6 us
  starting transfers between devices: 15.3 us -> 14.8 us
    ppermute x9 -> x8, starting transfers between devices: 15.3 us -> 11.1 us  [swap(): return lax.ppermute(x, axis, [(i, i ^ mask) for i in range(size)])]
    ppermute x0 -> x1, starting transfers between devices: none -> 3.76 us  [cross(): lax.ppermute(x, ('gx', 'gy'), [(2 * i + c, 2 * (i ^ mask) + 1 - c) for i...]
    pallas_call x12 -> x13, Pallas kernels: 17.7 us -> 14.6 us  [call(): pl.pallas_call(lambda *refs: kernel(*refs[skip:]), out_shape=outs, in_spe...]
    ppermute x0 -> x1, waiting for transfers between devices: none -> 1.44 us  [cross(): lax.ppermute(x, ('gx', 'gy'), [(2 * i + c, 2 * (i ^ mask) + 1 - c) for i...]
    ppermute x9 -> x8, waiting for transfers between devices: 14.6 us -> 13.3 us  [swap(): return lax.ppermute(x, axis, [(i, i ^ mask) for i in range(size)])]
  transfers between devices with their start and end apart: 9 -> 9, of which waited for: 8 -> 8; matrix products, arithmetic and copies ran while one was open for 0% -> 0% of each run, Pallas kernels for 14% -> 9%
where the time goes in v4:
time: 46.3 us; the launch traced here: 46.2 us
  starting transfers between devices  14.8 us (32%)
  waiting for transfers between devices  14.7 us (32%)
  Pallas kernels  14.6 us (32%)
  local copies, waits for them, and re-layouts  1.72 us (4%)
    pallas_call x13, Pallas kernels, call(): pl.pallas_call(lambda *refs: kernel(*refs[skip:]), out_shape=outs, in_spe...  14.6 us
    ppermute x8, waiting for transfers between devices, swap(): return lax.ppermute(x, axis, [(i, i ^ mask) for i in range(size)])  13.3 us
    ppermute x8, starting transfers between devices, swap(): return lax.ppermute(x, axis, [(i, i ^ mask) for i in range(size)])  11.1 us
    ppermute x1, starting transfers between devices, cross(): lax.ppermute(x, ('gx', 'gy'), [(2 * i + c, 2 * (i ^ mask) + 1 - c) for i...  3.76 us
    unnamed x32, local copies, waits for them, and re-layouts  1.72 us
    ppermute x1, waiting for transfers between devices, cross(): lax.ppermute(x, ('gx', 'gy'), [(2 * i + c, 2 * (i ^ mask) + 1 - c) for i...  1.44 us
  transfers between devices with their start and end apart: 9, of which 8 were waited for; matrix products, arithmetic and copies ran while one was open for 0% of the time, Pallas kernels for 9%

profile of v4, /device:TPU:0, one launch (start us, length us, event | category | flops | bytes accessed | tf_op | source)
XLA Modules:
  0.0 46.2 jit_solution(10803634556805684501)
XLA Ops:
  0.0 0.0 slice-start.2
  0.1 0.0 slice-start.7
  0.1 0.0 slice-start.8
  0.1 0.0 slice-start.9
  0.1 0.0 slice-start.10
  0.1 0.0 slice-start.11
  0.2 0.7 %copy-done = bf16[2,1,4096]{2,0,1:T(2,128)(2,1)S(1)} copy-done((bf16[2,1,4096]{2,0,1:T(2,128)(2,1)S(1)}, bf16[2,1,4096]{2,0,1:T(2,128)(2,1)}, u32[]{:S(2)}) %copy-start) | copy-done | bytes 16408
  0.9 0.0 copy-done.1
  0.9 0.5 %collective-permute-start = (f32[3,4096]{1,0:T(4,128)S(1)}, f32[3,4096]{1,0:T(4,128)S(1)}, u32[]{:S(2)}, u32[]{:S(2)}) collective-permute-start(f32[3,4096]{1,0:T(4,128)S(1)} %shard_map.57.refs_0_), channel_id=1, source_target_pairs={{0,1},{1,0},{2,3},{3,2},{4,5},{5,4},{6,7},{7,6},{8,9},{9,8},{10,11... | collective-permute-start | bytes 147464 | tf_op jit(solution)/shard_map/ppermute | solution.py:135
  1.4 0.9 %collective-permute-done.refs_1_ = f32[3,4096]{1,0:T(4,128)S(1)} collective-permute-done((f32[3,4096]{1,0:T(4,128)S(1)}, f32[3,4096]{1,0:T(4,128)S(1)}, u32[]{:S(2)}, u32[]{:S(2)}) %collective-permute-start) | collective-permute-done | bytes 49184 | tf_op jit(solution)/shard_map/ppermute | solution.py:135
  2.3 0.2 shard_map.58
  2.5 3.8 %collective-permute-start.1 = (bf16[2,4096]{1,0:T(2,128)(2,1)S(1)}, bf16[2,4096]{1,0:T(2,128)(2,1)S(1)}, u32[]{:S(2)}, u32[]{:S(2)}) collective-permute-start(bf16[2,4096]{1,0:T(2,128)(2,1)S(1)} %get-tuple-element.18), channel_id=1, source_target_pairs={{0,9},{1,8},{2,11},{3,10},{4,13},{5,12},{6,15},{7,14},{8,1},{9,0},... | collective-permute-start | bytes 49160 | tf_op jit(solution)/shard_map/ppermute | solution.py:129
  6.2 1.4 %collective-permute-done.1.refs_1_ = bf16[2,4096]{1,0:T(2,128)(2,1)S(1)} collective-permute-done((bf16[2,4096]{1,0:T(2,128)(2,1)S(1)}, bf16[2,4096]{1,0:T(2,128)(2,1)S(1)}, u32[]{:S(2)}, u32[]{:S(2)}) %collective-permute-start.1) | collective-permute-done | bytes 16416 | tf_op jit(solution)/shard_map/ppermute | solution.py:129
  7.7 1.9 %collective-permute-start.2 = (bf16[4,4096]{1,0:T(4,128)(2,1)S(1)}, bf16[4,4096]{1,0:T(4,128)(2,1)S(1)}, u32[]{:S(2)}, u32[]{:S(2)}) collective-permute-start(bf16[4,4096]{1,0:T(4,128)(2,1)S(1)} %shard_map.59.refs_0_), channel_id=1, source_target_pairs={{0,4},{2,6},{4,0},{6,2},{8,12},{10,14},{12,8},{14,10},{1,5},{3,7},... | collective-permute-start | bytes 98312 | tf_op jit(solution)/shard_map/ppermute | solution.py:135
  9.6 2.1 %collective-permute-done.2.refs_1_ = bf16[4,4096]{1,0:T(4,128)(2,1)S(1)} collective-permute-done((bf16[4,4096]{1,0:T(4,128)(2,1)S(1)}, bf16[4,4096]{1,0:T(4,128)(2,1)S(1)}, u32[]{:S(2)}, u32[]{:S(2)}) %collective-permute-start.2) | collective-permute-done | bytes 32800 | tf_op jit(solution)/shard_map/ppermute | solution.py:135
  11.7 1.8 %collective-permute-start.3 = (bf16[8,4096]{1,0:T(8,128)(2,1)S(1)}, bf16[8,4096]{1,0:T(8,128)(2,1)S(1)}, u32[]{:S(2)}, u32[]{:S(2)}) collective-permute-start(bf16[8,4096]{1,0:T(8,128)(2,1)S(1)} %shard_map.60.refs_0_), channel_id=1, source_target_pairs={{0,2},{2,0},{4,6},{6,4},{8,10},{10,8},{12,14},{14,12},{1,3},{3,1},... | collective-permute-start | bytes 196616 | tf_op jit(solution)/shard_map/ppermute | solution.py:135
  13.5 2.5 %collective-permute-done.3.refs_1_ = bf16[8,4096]{1,0:T(8,128)(2,1)S(1)} collective-permute-done((bf16[8,4096]{1,0:T(8,128)(2,1)S(1)}, bf16[8,4096]{1,0:T(8,128)(2,1)S(1)}, u32[]{:S(2)}, u32[]{:S(2)}) %collective-permute-start.3) | collective-permute-done | bytes 65568 | tf_op jit(solution)/shard_map/ppermute | solution.py:135
  16.1 0.0 slice-start.12
  16.2 3.6 %shard_map.63 = (f32[16,3328]{1,0:T(8,128)S(1)}, bf16[512,4096]{1,0:T(8,128)(2,1)S(1)}) custom-call(bf16[16,4096]{1,0:T(8,128)(2,1)S(1)} %shard_map.61.refs_0_, bf16[4096,3328]{1,0:T(8,128)(2,1)S(1)} %bitcast.4, bf16[3328,4096]{1,0:T(8,128)(2,1)} %refs_4_.1), custom_call_target="tpu_custom_call" | custom-call | flops 436207616 | bytes 27262976 | tf_op jit(solution)/shard_map/pallas_call | solution.py:27
  19.8 0.1 collective-permute-start.5
  19.9 0.9 %slice-done.13 = s8[4194304]{0:T(1024)(128)(4,1)S(1)} async-done(((s8[27262976]{0:T(1024)(128)(4,1)}), s8[4194304]{0:T(1024)(128)(4,1)S(1)}, s32[]{:S(2)}) %slice-start.13) | async-done | bytes 4194328
  20.9 4.0 %shard_map.62 = (f32[16,3328]{1,0:T(8,128)S(1)}, bf16[1280,4096]{1,0:T(8,128)(2,1)S(1)}) custom-call(bf16[16,4096]{1,0:T(8,128)(2,1)S(1)} %shard_map.61.refs_0_, bf16[4096,3328]{1,0:T(8,128)(2,1)S(1)} %bitcast.6, bf16[3328,4096]{1,0:T(8,128)(2,1)} %refs_4_.1), custom_call_target="tpu_custom_call" | custom-call | flops 436207616 | bytes 27262976 | tf_op jit(solution)/shard_map/pallas_call | solution.py:27
  24.9 0.1 collective-permute-start.4
  25.0 1.4 %collective-permute-done.4.refs_1_ = f32[16,3328]{1,0:T(8,128)S(1)} collective-permute-done((f32[16,3328]{1,0:T(8,128)S(1)}, f32[16,3328]{1,0:T(8,128)S(1)}, u32[]{:S(2)}, u32[]{:S(2)}) %collective-permute-start.4) | collective-permute-done | bytes 213024 | tf_op jit(solution)/shard_map/ppermute | solution.py:135
  26.4 6.1 %shard_map.64 = (f32[8,4096]{1,0:T(8,128)S(1)}, bf16[8,4096]{1,0:T(8,128)(2,1)S(1)}) custom-call(f32[16,3328]{1,0:T(8,128)S(1)} %get-tuple-element.19.refs_0_, f32[16,3328]{1,0:T(8,128)S(1)} %collective-permute-done.4.refs_1_, f32[16,3328]{1,0:T(8,128)S(1)} %get-tuple-element.20.refs_2_, f32[16,3328]{1,0:T(8,128)S(1)} %collective-permute-done.5.refs_3_, ...), custom_call_target="tpu_custom_call" | custom-call | flops 436207616 | bytes 27262976 | tf_op jit(solution)/shard_map/pallas_call | solution.py:27
  32.5 1.8 %collective-permute-start.6 = (bf16[8,4096]{1,0:T(8,128)(2,1)S(1)}, bf16[8,4096]{1,0:T(8,128)(2,1)S(1)}, u32[]{:S(2)}, u32[]{:S(2)}) collective-permute-start(bf16[8,4096]{1,0:T(8,128)(2,1)S(1)} %get-tuple-element.24), channel_id=1, source_target_pairs={{0,2},{2,0},{4,6},{6,4},{8,10},{10,8},{12,14},{14,12},{1,3},{3,1},... | collective-permute-start | bytes 196616 | tf_op jit(solution)/shard_map/ppermute | solution.py:135
  34.3 2.5 %collective-permute-done.6.refs_1_ = bf16[8,4096]{1,0:T(8,128)(2,1)S(1)} collective-permute-done((bf16[8,4096]{1,0:T(8,128)(2,1)S(1)}, bf16[8,4096]{1,0:T(8,128)(2,1)S(1)}, u32[]{:S(2)}, u32[]{:S(2)}) %collective-permute-start.6) | collective-permute-done | bytes 65568 | tf_op jit(solution)/shard_map/ppermute | solution.py:135
  36.8 1.9 %collective-permute-start.7 = (bf16[4,4096]{1,0:T(4,128)(2,1)S(1)}, bf16[4,4096]{1,0:T(4,128)(2,1)S(1)}, u32[]{:S(2)}, u32[]{:S(2)}) collective-permute-start(bf16[4,4096]{1,0:T(4,128)(2,1)S(1)} %get-tuple-element.26), channel_id=1, source_target_pairs={{0,4},{2,6},{4,0},{6,2},{8,12},{10,14},{12,8},{14,10},{1,5},{3,7},... | collective-permute-start | bytes 98312 | tf_op jit(solution)/shard_map/ppermute | solution.py:135
  38.7 2.1 %collective-permute-done.7.refs_1_ = bf16[4,4096]{1,0:T(4,128)(2,1)S(1)} collective-permute-done((bf16[4,4096]{1,0:T(4,128)(2,1)S(1)}, bf16[4,4096]{1,0:T(4,128)(2,1)S(1)}, u32[]{:S(2)}, u32[]{:S(2)}) %collective-permute-start.7) | collective-permute-done | bytes 32800 | tf_op jit(solution)/shard_map/ppermute | solution.py:135
  40.8 2.9 %collective-permute-start.8 = (bf16[2,4096]{1,0:T(2,128)(2,1)S(1)}, bf16[2,4096]{1,0:T(2,128)(2,1)S(1)}, u32[]{:S(2)}, u32[]{:S(2)}) collective-permute-start(bf16[2,4096]{1,0:T(2,128)(2,1)S(1)} %get-tuple-element.28), channel_id=1, source_target_pairs={{0,8},{2,10},{4,12},{6,14},{8,0},{10,2},{12,4},{14,6},{1,9},{3,11}... | collective-permute-start | bytes 49160 | tf_op jit(solution)/shard_map/ppermute | solution.py:135
  43.8 1.8 %collective-permute-done.8.refs_1_ = bf16[2,4096]{1,0:T(2,128)(2,1)S(1)} collective-permute-done((bf16[2,4096]{1,0:T(2,128)(2,1)S(1)}, bf16[2,4096]{1,0:T(2,128)(2,1)S(1)}, u32[]{:S(2)}, u32[]{:S(2)}) %collective-permute-start.8) | collective-permute-done | bytes 16416 | tf_op jit(solution)/shard_map/ppermute | solution.py:135
  45.5 0.6 %shard_map.67 = bf16[2,4096]{1,0:T(2,128)(2,1)} custom-call(f32[2,4096]{1,0:T(2,128)S(1)} %get-tuple-element.27.refs_0_, bf16[2,4096]{1,0:T(2,128)(2,1)S(1)} %collective-permute-done.8.refs_1_), custom_call_target="tpu_custom_call" | custom-call | tf_op jit(solution)/shard_map/pallas_call | solution.py:27
  (33 shorter events, 0.2 us)
Async XLA Ops:
  0.0 16.1 %slice-start = ((s8[27262976]{0:T(1024)(128)(4,1)}), s8[4194304]{0:T(1024)(128)(4,1)S(1)}, s32[]{:S(2)}) async-start(s8[27262976]{0:T(1024)(128)(4,1)} %bitcast.3), calls=%async_computation | async-start | bytes 8388608
  0.0 0.9 %copy-start = (bf16[2,1,4096]{2,0,1:T(2,128)(2,1)S(1)}, bf16[2,1,4096]{2,0,1:T(2,128)(2,1)}, u32[]{:S(2)}) copy-start(bf16[2,1,4096]{2,0,1:T(2,128)(2,1)} %param.5) | copy-start | bytes 49156
  0.0 0.9 %copy-start.1 = (f32[4096]{0:T(1024)S(1)}, f32[4096]{0:T(1024)}, u32[]{:S(2)}) copy-start(f32[4096]{0:T(1024)} %param.6) | copy-start | bytes 49156
  0.0 16.1 %slice-start.1 = ((s8[27262976]{0:T(1024)(128)(4,1)}), s8[4194304]{0:T(1024)(128)(4,1)S(1)}, s32[]{:S(2)}) async-start(s8[27262976]{0:T(1024)(128)(4,1)} %bitcast.3), calls=%async_computation.1 | async-start | bytes 8388608
  0.0 16.1 %slice-start.2 = ((s8[27262976]{0:T(1024)(128)(4,1)}), s8[4194304]{0:T(1024)(128)(4,1)S(1)}, s32[]{:S(2)}) async-start(s8[27262976]{0:T(1024)(128)(4,1)} %bitcast.3), calls=%async_computation.2 | async-start | bytes 8388608
  0.0 16.1 %slice-start.3 = ((s8[27262976]{0:T(1024)(128)(4,1)}), s8[4194304]{0:T(1024)(128)(4,1)S(1)}, s32[]{:S(2)}) async-start(s8[27262976]{0:T(1024)(128)(4,1)} %bitcast.3), calls=%async_computation.3 | async-start | bytes 8388608
  0.0 16.1 %slice-start.4 = ((s8[27262976]{0:T(1024)(128)(4,1)}), s8[4194304]{0:T(1024)(128)(4,1)S(1)}, s32[]{:S(2)}) async-start(s8[27262976]{0:T(1024)(128)(4,1)} %bitcast.3), calls=%async_computation.4 | async-start | bytes 8388608
  0.0 16.1 %slice-start.5 = ((s8[27262976]{0:T(1024)(128)(4,1)}), s8[4194304]{0:T(1024)(128)(4,1)S(1)}, s32[]{:S(2)}) async-start(s8[27262976]{0:T(1024)(128)(4,1)} %bitcast.3), calls=%async_computation.5 | async-start | bytes 8388608
  0.1 16.1 %slice-start.6 = ((s8[27262976]{0:T(1024)(128)(4,1)}), s8[2097152]{0:T(1024)(128)(4,1)S(1)}, s32[]{:S(2)}) async-start(s8[27262976]{0:T(1024)(128)(4,1)} %bitcast.3), calls=%async_computation.6 | async-start | bytes 4194304
  0.1 19.8 %slice-start.7 = ((s8[27262976]{0:T(1024)(128)(4,1)}), s8[2097152]{0:T(1024)(128)(4,1)S(1)}, s32[]{:S(2)}) async-start(s8[27262976]{0:T(1024)(128)(4,1)} %bitcast.5), calls=%async_computation.7 | async-start | bytes 4194304
  0.1 19.8 %slice-start.8 = ((s8[27262976]{0:T(1024)(128)(4,1)}), s8[4194304]{0:T(1024)(128)(4,1)S(1)}, s32[]{:S(2)}) async-start(s8[27262976]{0:T(1024)(128)(4,1)} %bitcast.5), calls=%async_computation.8 | async-start | bytes 8388608
  0.1 19.8 %slice-start.9 = ((s8[27262976]{0:T(1024)(128)(4,1)}), s8[4194304]{0:T(1024)(128)(4,1)S(1)}, s32[]{:S(2)}) async-start(s8[27262976]{0:T(1024)(128)(4,1)} %bitcast.5), calls=%async_computation.9 | async-start | bytes 8388608
  0.1 19.8 %slice-start.10 = ((s8[27262976]{0:T(1024)(128)(4,1)}), s8[4194304]{0:T(1024)(128)(4,1)S(1)}, s32[]{:S(2)}) async-start(s8[27262976]{0:T(1024)(128)(4,1)} %bitcast.5), calls=%async_computation.10 | async-start | bytes 8388608
  0.1 19.8 %slice-start.11 = ((s8[27262976]{0:T(1024)(128)(4,1)}), s8[4194304]{0:T(1024)(128)(4,1)S(1)}, s32[]{:S(2)}) async-start(s8[27262976]{0:T(1024)(128)(4,1)} %bitcast.5), calls=%async_computation.11 | async-start | bytes 8388608
  0.9 1.4 %collective-permute-start = (f32[3,4096]{1,0:T(4,128)S(1)}, f32[3,4096]{1,0:T(4,128)S(1)}, u32[]{:S(2)}, u32[]{:S(2)}) collective-permute-start(f32[3,4096]{1,0:T(4,128)S(1)} %shard_map.57.refs_0_), channel_id=1, source_target_pairs={{0,1},{1,0},{2,3},{3,2},{4,5},{5,4},{6,7},{7,6},{8,9},{9,8},{10,11... | collective-permute-start | bytes 147464 | tf_op jit(solution)/shard_map/ppermute | solution.py:135
  2.5 5.2 %collective-permute-start.1 = (bf16[2,4096]{1,0:T(2,128)(2,1)S(1)}, bf16[2,4096]{1,0:T(2,128)(2,1)S(1)}, u32[]{:S(2)}, u32[]{:S(2)}) collective-permute-start(bf16[2,4096]{1,0:T(2,128)(2,1)S(1)} %get-tuple-element.18), channel_id=1, source_target_pairs={{0,9},{1,8},{2,11},{3,10},{4,13},{5,12},{6,15},{7,14},{8,1},{9,0},... | collective-permute-start | bytes 49160 | tf_op jit(solution)/shard_map/ppermute | solution.py:129
  7.7 4.0 %collective-permute-start.2 = (bf16[4,4096]{1,0:T(4,128)(2,1)S(1)}, bf16[4,4096]{1,0:T(4,128)(2,1)S(1)}, u32[]{:S(2)}, u32[]{:S(2)}) collective-permute-start(bf16[4,4096]{1,0:T(4,128)(2,1)S(1)} %shard_map.59.refs_0_), channel_id=1, source_target_pairs={{0,4},{2,6},{4,0},{6,2},{8,12},{10,14},{12,8},{14,10},{1,5},{3,7},... | collective-permute-start | bytes 98312 | tf_op jit(solution)/shard_map/ppermute | solution.py:135
  11.7 4.3 %collective-permute-start.3 = (bf16[8,4096]{1,0:T(8,128)(2,1)S(1)}, bf16[8,4096]{1,0:T(8,128)(2,1)S(1)}, u32[]{:S(2)}, u32[]{:S(2)}) collective-permute-start(bf16[8,4096]{1,0:T(8,128)(2,1)S(1)} %shard_map.60.refs_0_), channel_id=1, source_target_pairs={{0,2},{2,0},{4,6},{6,4},{8,10},{10,8},{12,14},{14,12},{1,3},{3,1},... | collective-permute-start | bytes 196616 | tf_op jit(solution)/shard_map/ppermute | solution.py:135
  16.1 3.8 %slice-start.12 = ((s8[27262976]{0:T(1024)(128)(4,1)}), s8[4194304]{0:T(1024)(128)(4,1)S(1)}, s32[]{:S(2)}) async-start(s8[27262976]{0:T(1024)(128)(4,1)} %bitcast.5), calls=%async_computation.12 | async-start | bytes 8388608
  16.1 4.7 %slice-start.13 = ((s8[27262976]{0:T(1024)(128)(4,1)}), s8[4194304]{0:T(1024)(128)(4,1)S(1)}, s32[]{:S(2)}) async-start(s8[27262976]{0:T(1024)(128)(4,1)} %bitcast.5), calls=%async_computation.13 | async-start | bytes 8388608
  19.8 5.2 %collective-permute-start.5 = (f32[16,3328]{1,0:T(8,128)S(1)}, f32[16,3328]{1,0:T(8,128)S(1)}, u32[]{:S(2)}, u32[]{:S(2)}) collective-permute-start(f32[16,3328]{1,0:T(8,128)S(1)} %get-tuple-element.20.refs_2_), channel_id=1, source_target_pairs={{0,1},{1,0},{2,3},{3,2},{4,5},{5,4},{6,7},{7,6},{8,9},{9,8},{10,11... | collective-permute-start | bytes 638984 | tf_op jit(solution)/shard_map/ppermute | solution.py:135
  24.9 1.5 %collective-permute-start.4 = (f32[16,3328]{1,0:T(8,128)S(1)}, f32[16,3328]{1,0:T(8,128)S(1)}, u32[]{:S(2)}, u32[]{:S(2)}) collective-permute-start(f32[16,3328]{1,0:T(8,128)S(1)} %get-tuple-element.19.refs_0_), channel_id=1, source_target_pairs={{0,1},{1,0},{2,3},{3,2},{4,5},{5,4},{6,7},{7,6},{8,9},{9,8},{10,11... | collective-permute-start | bytes 638984 | tf_op jit(solution)/shard_map/ppermute | solution.py:135
  32.5 4.3 %collective-permute-start.6 = (bf16[8,4096]{1,0:T(8,128)(2,1)S(1)}, bf16[8,4096]{1,0:T(8,128)(2,1)S(1)}, u32[]{:S(2)}, u32[]{:S(2)}) collective-permute-start(bf16[8,4096]{1,0:T(8,128)(2,1)S(1)} %get-tuple-element.24), channel_id=1, source_target_pairs={{0,2},{2,0},{4,6},{6,4},{8,10},{10,8},{12,14},{14,12},{1,3},{3,1},... | collective-permute-start | bytes 196616 | tf_op jit(solution)/shard_map/ppermute | solution.py:135
  36.8 4.0 %collective-permute-start.7 = (bf16[4,4096]{1,0:T(4,128)(2,1)S(1)}, bf16[4,4096]{1,0:T(4,128)(2,1)S(1)}, u32[]{:S(2)}, u32[]{:S(2)}) collective-permute-start(bf16[4,4096]{1,0:T(4,128)(2,1)S(1)} %get-tuple-element.26), channel_id=1, source_target_pairs={{0,4},{2,6},{4,0},{6,2},{8,12},{10,14},{12,8},{14,10},{1,5},{3,7},... | collective-permute-start | bytes 98312 | tf_op jit(solution)/shard_map/ppermute | solution.py:135
  40.8 4.7 %collective-permute-start.8 = (bf16[2,4096]{1,0:T(2,128)(2,1)S(1)}, bf16[2,4096]{1,0:T(2,128)(2,1)S(1)}, u32[]{:S(2)}, u32[]{:S(2)}) collective-permute-start(bf16[2,4096]{1,0:T(2,128)(2,1)S(1)} %get-tuple-element.28), channel_id=1, source_target_pairs={{0,8},{2,10},{4,12},{6,14},{8,0},{10,2},{12,4},{14,6},{1,9},{3,11}... | collective-permute-start | bytes 49160 | tf_op jit(solution)/shard_map/ppermute | solution.py:135

commit v5 on v4

--- a/solution.py
+++ b/solution.py
@@ -15,7 +15,7 @@
 Shape = jax.ShapeDtypeStruct
 
 PAD = (512, 1024)
-PADS = 48
+PADS = 96
 UP_SHARE, GATE_SHARE = 2, 5
 DOWN_LIMIT = 15
 
@@ -153,6 +153,7 @@
     held = call(join_kernel, Shape((2 * own_rows, half), bf16), own, cross(other, groups, masks[-1]))
     for mask in reversed(masks[:-1]):
         held = call(join_kernel, Shape((2 * held.shape[0], half), bf16), held, swap(held, "gx", groups, mask))
+    down_weight = pltpu.with_memory_space_constraint(down_weight, pltpu.HBM)
     chunk = max(c for c in range(16, 257, 16) if units % c == 0)
     count = units // chunk
     counts = (count * UP_SHARE // 13, count * GATE_SHARE // 13)

time: 46.3 us -> 45.7 us (0.987)
  local copies, waits for them, and re-layouts: 1.72 us -> 0.77 us
  starting transfers between devices: 14.8 us -> 15.3 us
    unnamed x32, local copies, waits for them, and re-layouts: 1.72 us -> 0.77 us
where the time goes in v5:
time: 45.7 us; the launch traced here: 45.5 us
  starting transfers between devices  15.3 us (33%)
  Pallas kernels  14.6 us (32%)
  waiting for transfers between devices  14.5 us (32%)
  local copies, waits for them, and re-layouts  0.77 us (2%)
    pallas_call x13, Pallas kernels, call(): pl.pallas_call(lambda *refs: kernel(*refs[skip:]), out_shape=outs, in_spe...  14.6 us
    ppermute x8, waiting for transfers between devices, swap(): return lax.ppermute(x, axis, [(i, i ^ mask) for i in range(size)])  13.1 us
    ppermute x8, starting transfers between devices, swap(): return lax.ppermute(x, axis, [(i, i ^ mask) for i in range(size)])  11.5 us
    ppermute x1, starting transfers between devices, cross(): lax.ppermute(x, ('gx', 'gy'), [(2 * i + c, 2 * (i ^ mask) + 1 - c) for i...  3.76 us
    ppermute x1, waiting for transfers between devices, cross(): lax.ppermute(x, ('gx', 'gy'), [(2 * i + c, 2 * (i ^ mask) + 1 - c) for i...  1.44 us
  transfers between devices with their start and end apart: 9, of which 8 were waited for; matrix products, arithmetic and copies ran while one was open for 0% of the time, Pallas kernels for 9%

profile of v5, /device:TPU:0, one launch (start us, length us, event | category | flops | bytes accessed | tf_op | source)
XLA Modules:
  0.0 45.5 jit_solution(3776027214038535845)
XLA Ops:
  0.1 0.0 slice-start.7
  0.1 0.0 slice-start.8
  0.1 0.0 slice-start.9
  0.1 0.0 slice-start.10
  0.1 0.0 slice-start.11
  0.1 0.0 slice-start.12
  0.1 0.1 shard_map.56.refs_0_
  0.2 0.7 %copy-done = bf16[2,1,4096]{2,0,1:T(2,128)(2,1)S(1)} copy-done((bf16[2,1,4096]{2,0,1:T(2,128)(2,1)S(1)}, bf16[2,1,4096]{2,0,1:T(2,128)(2,1)}, u32[]{:S(2)}) %copy-start) | copy-done | bytes 16408
  0.9 0.0 copy-done.1
  0.9 0.5 %collective-permute-start = (f32[3,4096]{1,0:T(4,128)S(1)}, f32[3,4096]{1,0:T(4,128)S(1)}, u32[]{:S(2)}, u32[]{:S(2)}) collective-permute-start(f32[3,4096]{1,0:T(4,128)S(1)} %shard_map.57.refs_0_), channel_id=1, source_target_pairs={{0,1},{1,0},{2,3},{3,2},{4,5},{5,4},{6,7},{7,6},{8,9},{9,8},{10,11... | collective-permute-start | bytes 147464 | tf_op jit(solution)/shard_map/ppermute | solution.py:135
  1.4 0.9 %collective-permute-done.refs_1_ = f32[3,4096]{1,0:T(4,128)S(1)} collective-permute-done((f32[3,4096]{1,0:T(4,128)S(1)}, f32[3,4096]{1,0:T(4,128)S(1)}, u32[]{:S(2)}, u32[]{:S(2)}) %collective-permute-start) | collective-permute-done | bytes 49184 | tf_op jit(solution)/shard_map/ppermute | solution.py:135
  2.3 0.2 shard_map.58
  2.5 3.8 %collective-permute-start.1 = (bf16[2,4096]{1,0:T(2,128)(2,1)S(1)}, bf16[2,4096]{1,0:T(2,128)(2,1)S(1)}, u32[]{:S(2)}, u32[]{:S(2)}) collective-permute-start(bf16[2,4096]{1,0:T(2,128)(2,1)S(1)} %get-tuple-element.18), channel_id=1, source_target_pairs={{0,9},{1,8},{2,11},{3,10},{4,13},{5,12},{6,15},{7,14},{8,1},{9,0},... | collective-permute-start | bytes 49160 | tf_op jit(solution)/shard_map/ppermute | solution.py:129
  6.2 1.4 %collective-permute-done.1.refs_1_ = bf16[2,4096]{1,0:T(2,128)(2,1)S(1)} collective-permute-done((bf16[2,4096]{1,0:T(2,128)(2,1)S(1)}, bf16[2,4096]{1,0:T(2,128)(2,1)S(1)}, u32[]{:S(2)}, u32[]{:S(2)}) %collective-permute-start.1) | collective-permute-done | bytes 16416 | tf_op jit(solution)/shard_map/ppermute | solution.py:129
  7.7 1.9 %collective-permute-start.2 = (bf16[4,4096]{1,0:T(4,128)(2,1)S(1)}, bf16[4,4096]{1,0:T(4,128)(2,1)S(1)}, u32[]{:S(2)}, u32[]{:S(2)}) collective-permute-start(bf16[4,4096]{1,0:T(4,128)(2,1)S(1)} %shard_map.59.refs_0_), channel_id=1, source_target_pairs={{0,4},{2,6},{4,0},{6,2},{8,12},{10,14},{12,8},{14,10},{1,5},{3,7},... | collective-permute-start | bytes 98312 | tf_op jit(solution)/shard_map/ppermute | solution.py:135
  9.6 2.1 %collective-permute-done.2.refs_1_ = bf16[4,4096]{1,0:T(4,128)(2,1)S(1)} collective-permute-done((bf16[4,4096]{1,0:T(4,128)(2,1)S(1)}, bf16[4,4096]{1,0:T(4,128)(2,1)S(1)}, u32[]{:S(2)}, u32[]{:S(2)}) %collective-permute-start.2) | collective-permute-done | bytes 32800 | tf_op jit(solution)/shard_map/ppermute | solution.py:135
  11.7 1.8 %collective-permute-start.3 = (bf16[8,4096]{1,0:T(8,128)(2,1)S(1)}, bf16[8,4096]{1,0:T(8,128)(2,1)S(1)}, u32[]{:S(2)}, u32[]{:S(2)}) collective-permute-start(bf16[8,4096]{1,0:T(8,128)(2,1)S(1)} %shard_map.60.refs_0_), channel_id=1, source_target_pairs={{0,2},{2,0},{4,6},{6,4},{8,10},{10,8},{12,14},{14,12},{1,3},{3,1},... | collective-permute-start | bytes 196616 | tf_op jit(solution)/shard_map/ppermute | solution.py:135
  13.5 2.5 %collective-permute-done.3.refs_1_ = bf16[8,4096]{1,0:T(8,128)(2,1)S(1)} collective-permute-done((bf16[8,4096]{1,0:T(8,128)(2,1)S(1)}, bf16[8,4096]{1,0:T(8,128)(2,1)S(1)}, u32[]{:S(2)}, u32[]{:S(2)}) %collective-permute-start.3) | collective-permute-done | bytes 65568 | tf_op jit(solution)/shard_map/ppermute | solution.py:135
  16.1 0.0 slice-start.13
  16.1 3.6 %shard_map.63 = (f32[16,3328]{1,0:T(8,128)S(1)}, bf16[512,4096]{1,0:T(8,128)(2,1)S(1)}) custom-call(bf16[16,4096]{1,0:T(8,128)(2,1)S(1)} %shard_map.61.refs_0_, bf16[4096,3328]{1,0:T(8,128)(2,1)S(1)} %bitcast.4, bf16[3328,4096]{1,0:T(8,128)(2,1)} %refs_4_.1), custom_call_target="tpu_custom_call" | custom-call | flops 436207616 | bytes 27262976 | tf_op jit(solution)/shard_map/pallas_call | solution.py:27
  19.8 0.1 collective-permute-start.5
  20.0 4.0 %shard_map.62 = (f32[16,3328]{1,0:T(8,128)S(1)}, bf16[1280,4096]{1,0:T(8,128)(2,1)S(1)}) custom-call(bf16[16,4096]{1,0:T(8,128)(2,1)S(1)} %shard_map.61.refs_0_, bf16[4096,3328]{1,0:T(8,128)(2,1)S(1)} %bitcast.6, bf16[3328,4096]{1,0:T(8,128)(2,1)} %refs_4_.1), custom_call_target="tpu_custom_call" | custom-call | flops 436207616 | bytes 27262976 | tf_op jit(solution)/shard_map/pallas_call | solution.py:27
  24.0 0.5 %collective-permute-start.4 = (f32[16,3328]{1,0:T(8,128)S(1)}, f32[16,3328]{1,0:T(8,128)S(1)}, u32[]{:S(2)}, u32[]{:S(2)}) collective-permute-start(f32[16,3328]{1,0:T(8,128)S(1)} %get-tuple-element.19.refs_0_), channel_id=1, source_target_pairs={{0,1},{1,0},{2,3},{3,2},{4,5},{5,4},{6,7},{7,6},{8,9},{9,8},{10,11... | collective-permute-start | bytes 638984 | tf_op jit(solution)/shard_map/ppermute | solution.py:135
  24.5 1.1 %collective-permute-done.4.refs_1_ = f32[16,3328]{1,0:T(8,128)S(1)} collective-permute-done((f32[16,3328]{1,0:T(8,128)S(1)}, f32[16,3328]{1,0:T(8,128)S(1)}, u32[]{:S(2)}, u32[]{:S(2)}) %collective-permute-start.4) | collective-permute-done | bytes 213024 | tf_op jit(solution)/shard_map/ppermute | solution.py:135
  25.6 6.1 %shard_map.64 = (f32[8,4096]{1,0:T(8,128)S(1)}, bf16[8,4096]{1,0:T(8,128)(2,1)S(1)}) custom-call(f32[16,3328]{1,0:T(8,128)S(1)} %get-tuple-element.19.refs_0_, f32[16,3328]{1,0:T(8,128)S(1)} %collective-permute-done.4.refs_1_, f32[16,3328]{1,0:T(8,128)S(1)} %get-tuple-element.20.refs_2_, f32[16,3328]{1,0:T(8,128)S(1)} %collective-permute-done.5.refs_3_, ...), custom_call_target="tpu_custom_call" | custom-call | flops 436207616 | bytes 27262976 | tf_op jit(solution)/shard_map/pallas_call | solution.py:27
  31.7 1.8 %collective-permute-start.6 = (bf16[8,4096]{1,0:T(8,128)(2,1)S(1)}, bf16[8,4096]{1,0:T(8,128)(2,1)S(1)}, u32[]{:S(2)}, u32[]{:S(2)}) collective-permute-start(bf16[8,4096]{1,0:T(8,128)(2,1)S(1)} %get-tuple-element.24), channel_id=1, source_target_pairs={{0,2},{2,0},{4,6},{6,4},{8,10},{10,8},{12,14},{14,12},{1,3},{3,1},... | collective-permute-start | bytes 196616 | tf_op jit(solution)/shard_map/ppermute | solution.py:135
  33.5 2.6 %collective-permute-done.6.refs_1_ = bf16[8,4096]{1,0:T(8,128)(2,1)S(1)} collective-permute-done((bf16[8,4096]{1,0:T(8,128)(2,1)S(1)}, bf16[8,4096]{1,0:T(8,128)(2,1)S(1)}, u32[]{:S(2)}, u32[]{:S(2)}) %collective-permute-start.6) | collective-permute-done | bytes 65568 | tf_op jit(solution)/shard_map/ppermute | solution.py:135
  36.1 1.9 %collective-permute-start.7 = (bf16[4,4096]{1,0:T(4,128)(2,1)S(1)}, bf16[4,4096]{1,0:T(4,128)(2,1)S(1)}, u32[]{:S(2)}, u32[]{:S(2)}) collective-permute-start(bf16[4,4096]{1,0:T(4,128)(2,1)S(1)} %get-tuple-element.26), channel_id=1, source_target_pairs={{0,4},{2,6},{4,0},{6,2},{8,12},{10,14},{12,8},{14,10},{1,5},{3,7},... | collective-permute-start | bytes 98312 | tf_op jit(solution)/shard_map/ppermute | solution.py:135
  38.0 2.1 %collective-permute-done.7.refs_1_ = bf16[4,4096]{1,0:T(4,128)(2,1)S(1)} collective-permute-done((bf16[4,4096]{1,0:T(4,128)(2,1)S(1)}, bf16[4,4096]{1,0:T(4,128)(2,1)S(1)}, u32[]{:S(2)}, u32[]{:S(2)}) %collective-permute-start.7) | collective-permute-done | bytes 32800 | tf_op jit(solution)/shard_map/ppermute | solution.py:135
  40.1 2.9 %collective-permute-start.8 = (bf16[2,4096]{1,0:T(2,128)(2,1)S(1)}, bf16[2,4096]{1,0:T(2,128)(2,1)S(1)}, u32[]{:S(2)}, u32[]{:S(2)}) collective-permute-start(bf16[2,4096]{1,0:T(2,128)(2,1)S(1)} %get-tuple-element.28), channel_id=1, source_target_pairs={{0,8},{2,10},{4,12},{6,14},{8,0},{10,2},{12,4},{14,6},{1,9},{3,11}... | collective-permute-start | bytes 49160 | tf_op jit(solution)/shard_map/ppermute | solution.py:135
  43.1 1.8 %collective-permute-done.8.refs_1_ = bf16[2,4096]{1,0:T(2,128)(2,1)S(1)} collective-permute-done((bf16[2,4096]{1,0:T(2,128)(2,1)S(1)}, bf16[2,4096]{1,0:T(2,128)(2,1)S(1)}, u32[]{:S(2)}, u32[]{:S(2)}) %collective-permute-start.8) | collective-permute-done | bytes 16416 | tf_op jit(solution)/shard_map/ppermute | solution.py:135
  44.8 0.6 %shard_map.67 = bf16[2,4096]{1,0:T(2,128)(2,1)} custom-call(f32[2,4096]{1,0:T(2,128)S(1)} %get-tuple-element.27.refs_0_, bf16[2,4096]{1,0:T(2,128)(2,1)S(1)} %collective-permute-done.8.refs_1_), custom_call_target="tpu_custom_call" | custom-call | tf_op jit(solution)/shard_map/pallas_call | solution.py:27
  (33 shorter events, 0.1 us)
Async XLA Ops:
  0.0 16.1 %slice-start = ((s8[27262976]{0:T(1024)(128)(4,1)}), s8[4194304]{0:T(1024)(128)(4,1)S(1)}, s32[]{:S(2)}) async-start(s8[27262976]{0:T(1024)(128)(4,1)} %bitcast.3), calls=%async_computation | async-start | bytes 8388608
  0.0 0.9 %copy-start = (bf16[2,1,4096]{2,0,1:T(2,128)(2,1)S(1)}, bf16[2,1,4096]{2,0,1:T(2,128)(2,1)}, u32[]{:S(2)}) copy-start(bf16[2,1,4096]{2,0,1:T(2,128)(2,1)} %param.5) | copy-start | bytes 49156
  0.0 0.9 %copy-start.1 = (f32[4096]{0:T(1024)S(1)}, f32[4096]{0:T(1024)}, u32[]{:S(2)}) copy-start(f32[4096]{0:T(1024)} %param.6) | copy-start | bytes 49156
  0.0 16.1 %slice-start.1 = ((s8[27262976]{0:T(1024)(128)(4,1)}), s8[4194304]{0:T(1024)(128)(4,1)S(1)}, s32[]{:S(2)}) async-start(s8[27262976]{0:T(1024)(128)(4,1)} %bitcast.3), calls=%async_computation.1 | async-start | bytes 8388608
  0.0 16.1 %slice-start.2 = ((s8[27262976]{0:T(1024)(128)(4,1)}), s8[4194304]{0:T(1024)(128)(4,1)S(1)}, s32[]{:S(2)}) async-start(s8[27262976]{0:T(1024)(128)(4,1)} %bitcast.3), calls=%async_computation.2 | async-start | bytes 8388608
  0.0 16.1 %slice-start.3 = ((s8[27262976]{0:T(1024)(128)(4,1)}), s8[4194304]{0:T(1024)(128)(4,1)S(1)}, s32[]{:S(2)}) async-start(s8[27262976]{0:T(1024)(128)(4,1)} %bitcast.3), calls=%async_computation.3 | async-start | bytes 8388608
  0.0 16.1 %slice-start.4 = ((s8[27262976]{0:T(1024)(128)(4,1)}), s8[4194304]{0:T(1024)(128)(4,1)S(1)}, s32[]{:S(2)}) async-start(s8[27262976]{0:T(1024)(128)(4,1)} %bitcast.3), calls=%async_computation.4 | async-start | bytes 8388608
  0.0 16.1 %slice-start.5 = ((s8[27262976]{0:T(1024)(128)(4,1)}), s8[4194304]{0:T(1024)(128)(4,1)S(1)}, s32[]{:S(2)}) async-start(s8[27262976]{0:T(1024)(128)(4,1)} %bitcast.3), calls=%async_computation.5 | async-start | bytes 8388608
  0.1 16.1 %slice-start.6 = ((s8[27262976]{0:T(1024)(128)(4,1)}), s8[2097152]{0:T(1024)(128)(4,1)S(1)}, s32[]{:S(2)}) async-start(s8[27262976]{0:T(1024)(128)(4,1)} %bitcast.3), calls=%async_computation.6 | async-start | bytes 4194304
  0.1 19.8 %slice-start.7 = ((s8[27262976]{0:T(1024)(128)(4,1)}), s8[2097152]{0:T(1024)(128)(4,1)S(1)}, s32[]{:S(2)}) async-start(s8[27262976]{0:T(1024)(128)(4,1)} %bitcast.5), calls=%async_computation.7 | async-start | bytes 4194304
  0.1 19.8 %slice-start.8 = ((s8[27262976]{0:T(1024)(128)(4,1)}), s8[4194304]{0:T(1024)(128)(4,1)S(1)}, s32[]{:S(2)}) async-start(s8[27262976]{0:T(1024)(128)(4,1)} %bitcast.5), calls=%async_computation.8 | async-start | bytes 8388608
  0.1 19.8 %slice-start.9 = ((s8[27262976]{0:T(1024)(128)(4,1)}), s8[4194304]{0:T(1024)(128)(4,1)S(1)}, s32[]{:S(2)}) async-start(s8[27262976]{0:T(1024)(128)(4,1)} %bitcast.5), calls=%async_computation.9 | async-start | bytes 8388608
  0.1 19.8 %slice-start.10 = ((s8[27262976]{0:T(1024)(128)(4,1)}), s8[4194304]{0:T(1024)(128)(4,1)S(1)}, s32[]{:S(2)}) async-start(s8[27262976]{0:T(1024)(128)(4,1)} %bitcast.5), calls=%async_computation.10 | async-start | bytes 8388608
  0.1 19.8 %slice-start.11 = ((s8[27262976]{0:T(1024)(128)(4,1)}), s8[4194304]{0:T(1024)(128)(4,1)S(1)}, s32[]{:S(2)}) async-start(s8[27262976]{0:T(1024)(128)(4,1)} %bitcast.5), calls=%async_computation.11 | async-start | bytes 8388608
  0.1 19.8 %slice-start.12 = ((s8[27262976]{0:T(1024)(128)(4,1)}), s8[4194304]{0:T(1024)(128)(4,1)S(1)}, s32[]{:S(2)}) async-start(s8[27262976]{0:T(1024)(128)(4,1)} %bitcast.5), calls=%async_computation.12 | async-start | bytes 8388608
  0.9 1.4 %collective-permute-start = (f32[3,4096]{1,0:T(4,128)S(1)}, f32[3,4096]{1,0:T(4,128)S(1)}, u32[]{:S(2)}, u32[]{:S(2)}) collective-permute-start(f32[3,4096]{1,0:T(4,128)S(1)} %shard_map.57.refs_0_), channel_id=1, source_target_pairs={{0,1},{1,0},{2,3},{3,2},{4,5},{5,4},{6,7},{7,6},{8,9},{9,8},{10,11... | collective-permute-start | bytes 147464 | tf_op jit(solution)/shard_map/ppermute | solution.py:135
  2.5 5.2 %collective-permute-start.1 = (bf16[2,4096]{1,0:T(2,128)(2,1)S(1)}, bf16[2,4096]{1,0:T(2,128)(2,1)S(1)}, u32[]{:S(2)}, u32[]{:S(2)}) collective-permute-start(bf16[2,4096]{1,0:T(2,128)(2,1)S(1)} %get-tuple-element.18), channel_id=1, source_target_pairs={{0,9},{1,8},{2,11},{3,10},{4,13},{5,12},{6,15},{7,14},{8,1},{9,0},... | collective-permute-start | bytes 49160 | tf_op jit(solution)/shard_map/ppermute | solution.py:129
  7.7 4.0 %collective-permute-start.2 = (bf16[4,4096]{1,0:T(4,128)(2,1)S(1)}, bf16[4,4096]{1,0:T(4,128)(2,1)S(1)}, u32[]{:S(2)}, u32[]{:S(2)}) collective-permute-start(bf16[4,4096]{1,0:T(4,128)(2,1)S(1)} %shard_map.59.refs_0_), channel_id=1, source_target_pairs={{0,4},{2,6},{4,0},{6,2},{8,12},{10,14},{12,8},{14,10},{1,5},{3,7},... | collective-permute-start | bytes 98312 | tf_op jit(solution)/shard_map/ppermute | solution.py:135
  11.7 4.3 %collective-permute-start.3 = (bf16[8,4096]{1,0:T(8,128)(2,1)S(1)}, bf16[8,4096]{1,0:T(8,128)(2,1)S(1)}, u32[]{:S(2)}, u32[]{:S(2)}) collective-permute-start(bf16[8,4096]{1,0:T(8,128)(2,1)S(1)} %shard_map.60.refs_0_), channel_id=1, source_target_pairs={{0,2},{2,0},{4,6},{6,4},{8,10},{10,8},{12,14},{14,12},{1,3},{3,1},... | collective-permute-start | bytes 196616 | tf_op jit(solution)/shard_map/ppermute | solution.py:135
  16.1 3.8 %slice-start.13 = ((s8[27262976]{0:T(1024)(128)(4,1)}), s8[4194304]{0:T(1024)(128)(4,1)S(1)}, s32[]{:S(2)}) async-start(s8[27262976]{0:T(1024)(128)(4,1)} %bitcast.5), calls=%async_computation.13 | async-start | bytes 8388608
  19.8 4.7 %collective-permute-start.5 = (f32[16,3328]{1,0:T(8,128)S(1)}, f32[16,3328]{1,0:T(8,128)S(1)}, u32[]{:S(2)}, u32[]{:S(2)}) collective-permute-start(f32[16,3328]{1,0:T(8,128)S(1)} %get-tuple-element.20.refs_2_), channel_id=1, source_target_pairs={{0,1},{1,0},{2,3},{3,2},{4,5},{5,4},{6,7},{7,6},{8,9},{9,8},{10,11... | collective-permute-start | bytes 638984 | tf_op jit(solution)/shard_map/ppermute | solution.py:135
  24.0 1.6 %collective-permute-start.4 = (f32[16,3328]{1,0:T(8,128)S(1)}, f32[16,3328]{1,0:T(8,128)S(1)}, u32[]{:S(2)}, u32[]{:S(2)}) collective-permute-start(f32[16,3328]{1,0:T(8,128)S(1)} %get-tuple-element.19.refs_0_), channel_id=1, source_target_pairs={{0,1},{1,0},{2,3},{3,2},{4,5},{5,4},{6,7},{7,6},{8,9},{9,8},{10,11... | collective-permute-start | bytes 638984 | tf_op jit(solution)/shard_map/ppermute | solution.py:135
  31.7 4.5 %collective-permute-start.6 = (bf16[8,4096]{1,0:T(8,128)(2,1)S(1)}, bf16[8,4096]{1,0:T(8,128)(2,1)S(1)}, u32[]{:S(2)}, u32[]{:S(2)}) collective-permute-start(bf16[8,4096]{1,0:T(8,128)(2,1)S(1)} %get-tuple-element.24), channel_id=1, source_target_pairs={{0,2},{2,0},{4,6},{6,4},{8,10},{10,8},{12,14},{14,12},{1,3},{3,1},... | collective-permute-start | bytes 196616 | tf_op jit(solution)/shard_map/ppermute | solution.py:135
  36.1 4.0 %collective-permute-start.7 = (bf16[4,4096]{1,0:T(4,128)(2,1)S(1)}, bf16[4,4096]{1,0:T(4,128)(2,1)S(1)}, u32[]{:S(2)}, u32[]{:S(2)}) collective-permute-start(bf16[4,4096]{1,0:T(4,128)(2,1)S(1)} %get-tuple-element.26), channel_id=1, source_target_pairs={{0,4},{2,6},{4,0},{6,2},{8,12},{10,14},{12,8},{14,10},{1,5},{3,7},... | collective-permute-start | bytes 98312 | tf_op jit(solution)/shard_map/ppermute | solution.py:135
  40.1 4.7 %collective-permute-start.8 = (bf16[2,4096]{1,0:T(2,128)(2,1)S(1)}, bf16[2,4096]{1,0:T(2,128)(2,1)S(1)}, u32[]{:S(2)}, u32[]{:S(2)}) collective-permute-start(bf16[2,4096]{1,0:T(2,128)(2,1)S(1)} %get-tuple-element.28), channel_id=1, source_target_pairs={{0,8},{2,10},{4,12},{6,14},{8,0},{10,2},{12,4},{14,6},{1,9},{3,11}... | collective-permute-start | bytes 49160 | tf_op jit(solution)/shard_map/ppermute | solution.py:135

commit v6 on v5

--- a/solution.py
+++ b/solution.py
@@ -65,7 +65,7 @@
     out_ref[rows:, :] = second_ref[...]
 
 
-def project_kernel(ahead, chunk, first, x_ref, w_ref, down_ref, out_ref, *rest):
+def project_kernel(ahead, chunk, first, x_ref, w_ref, down_ref, out_ref, send_ref, *rest):
     copies = []
     if ahead:
         taken_ref, sem = rest
@@ -74,7 +74,9 @@
     columns = w_ref.shape[1]
     for c in range(0, columns, 256):
         e = min(c + 256, columns)
-        out_ref[:, c:e] = jnp.dot(x_ref[...], w_ref[:, c:e], preferred_element_type=f32)
+        part = jnp.dot(x_ref[...], w_ref[:, c:e], preferred_element_type=f32)
+        out_ref[:, c:e] = part
+        send_ref[:, c:e] = part.astype(send_ref.dtype)
     for copy in copies:
         copy.wait()
 
@@ -89,8 +91,8 @@
     ]
     for copy in copies:
         copy.start()
-    v = g_ref[...] + g2_ref[...]
-    h_ref[...] = (v / (1.0 + jnp.exp(-v)) * (u_ref[...] + u2_ref[...])).astype(bf16)
+    v = g_ref[...] + g2_ref[...].astype(f32)
+    h_ref[...] = (v / (1.0 + jnp.exp(-v)) * (u_ref[...] + u2_ref[...].astype(f32))).astype(bf16)
     rows = keep_ref.shape[0]
     passes = [(copy, [(buf_ref, a - start, a, b)]) for copy, a, b in zip(copies, bounds, bounds[1:])]
     if taken:
@@ -160,7 +162,7 @@
     counts = (*counts, count - sum(counts))
 
     def project(weight, first, ahead):
-        outs = [Shape((rows, units), f32)]
+        outs = [Shape((rows, units), f32), Shape((rows, units), bf16)]
         scratch = []
         if ahead:
             outs.append(Shape((ahead * chunk, half), bf16))
@@ -171,13 +173,15 @@
             specs=[VMEM, VMEM, HBM], scratch=scratch, flops=2 * rows * weight.size,
         )
 
-    up, *taken_up = project(up_weight, 0, counts[0])
-    up_other = swap(up, "gy", halves, 1)
-    gate, *taken_gate = project(gate_weight, counts[0], counts[1])
-    gate_other = swap(gate, "gy", halves, 1)
+    up, up_send, *taken_up = project(up_weight, 0, counts[0])
+    up_other = swap(up_send, "gy", halves, 1)
+    gate, gate_send, *taken_gate = project(gate_weight, counts[0], counts[1])
+    gate_other = swap(gate_send, "gy", halves, 1)
     taken = (*taken_up, *taken_gate)
     start = sum(counts[:-1]) * chunk
-    bounds = (*range(start, units, 2 * chunk), units)
+    bounds = [start]
+    while bounds[-1] < units:
+        bounds.append(bounds[-1] + (2 * chunk if units - bounds[-1] > 3 * chunk else chunk))
     keep, send = call(
         functools.partial(down_kernel, bounds),
         (Shape((rows // 2, half), f32), Shape((rows // 2, half), bf16)),

time: 45.7 us -> 44.7 us (0.978)
  Pallas kernels: 14.6 us -> 13.9 us
    pallas_call x13, Pallas kernels: 14.6 us -> 13.9 us  [call(): pl.pallas_call(lambda *refs: kernel(*refs[skip:]), out_shape=outs, in_spe...]
where the time goes in v6:
time: 44.7 us; the launch traced here: 44.6 us
  starting transfers between devices  15.3 us (34%)
  waiting for transfers between devices  14.4 us (32%)
  Pallas kernels  13.9 us (31%)
  local copies, waits for them, and re-layouts  0.77 us (2%)
    pallas_call x13, Pallas kernels, call(): pl.pallas_call(lambda *refs: kernel(*refs[skip:]), out_shape=outs, in_spe...  13.9 us
    ppermute x8, waiting for transfers between devices, swap(): return lax.ppermute(x, axis, [(i, i ^ mask) for i in range(size)])  12.9 us
    ppermute x8, starting transfers between devices, swap(): return lax.ppermute(x, axis, [(i, i ^ mask) for i in range(size)])  11.5 us
    ppermute x1, starting transfers between devices, cross(): lax.ppermute(x, ('gx', 'gy'), [(2 * i + c, 2 * (i ^ mask) + 1 - c) for i...  3.76 us
    ppermute x1, waiting for transfers between devices, cross(): lax.ppermute(x, ('gx', 'gy'), [(2 * i + c, 2 * (i ^ mask) + 1 - c) for i...  1.44 us
  transfers between devices with their start and end apart: 9, of which 8 were waited for; matrix products, arithmetic and copies ran while one was open for 0% of the time, Pallas kernels for 9%

profile of v6, /device:TPU:0, one launch (start us, length us, event | category | flops | bytes accessed | tf_op | source)
XLA Modules:
  0.0 44.6 jit_solution(7238739135306663114)
XLA Ops:
  0.1 0.0 slice-start.7
  0.1 0.0 slice-start.8
  0.1 0.0 slice-start.9
  0.1 0.0 slice-start.10
  0.1 0.0 slice-start.11
  0.1 0.0 slice-start.12
  0.1 0.1 shard_map.56.refs_0_
  0.2 0.7 %copy-done = bf16[2,1,4096]{2,0,1:T(2,128)(2,1)S(1)} copy-done((bf16[2,1,4096]{2,0,1:T(2,128)(2,1)S(1)}, bf16[2,1,4096]{2,0,1:T(2,128)(2,1)}, u32[]{:S(2)}) %copy-start) | copy-done | bytes 16408
  0.9 0.0 copy-done.1
  0.9 0.5 %collective-permute-start = (f32[3,4096]{1,0:T(4,128)S(1)}, f32[3,4096]{1,0:T(4,128)S(1)}, u32[]{:S(2)}, u32[]{:S(2)}) collective-permute-start(f32[3,4096]{1,0:T(4,128)S(1)} %shard_map.57.refs_0_), channel_id=1, source_target_pairs={{0,1},{1,0},{2,3},{3,2},{4,5},{5,4},{6,7},{7,6},{8,9},{9,8},{10,11... | collective-permute-start | bytes 147464 | tf_op jit(solution)/shard_map/ppermute | solution.py:137
  1.4 0.9 %collective-permute-done.refs_1_ = f32[3,4096]{1,0:T(4,128)S(1)} collective-permute-done((f32[3,4096]{1,0:T(4,128)S(1)}, f32[3,4096]{1,0:T(4,128)S(1)}, u32[]{:S(2)}, u32[]{:S(2)}) %collective-permute-start) | collective-permute-done | bytes 49184 | tf_op jit(solution)/shard_map/ppermute | solution.py:137
  2.3 0.2 shard_map.58
  2.5 3.8 %collective-permute-start.1 = (bf16[2,4096]{1,0:T(2,128)(2,1)S(1)}, bf16[2,4096]{1,0:T(2,128)(2,1)S(1)}, u32[]{:S(2)}, u32[]{:S(2)}) collective-permute-start(bf16[2,4096]{1,0:T(2,128)(2,1)S(1)} %get-tuple-element.20), channel_id=1, source_target_pairs={{0,9},{1,8},{2,11},{3,10},{4,13},{5,12},{6,15},{7,14},{8,1},{9,0},... | collective-permute-start | bytes 49160 | tf_op jit(solution)/shard_map/ppermute | solution.py:131
  6.2 1.4 %collective-permute-done.1.refs_1_ = bf16[2,4096]{1,0:T(2,128)(2,1)S(1)} collective-permute-done((bf16[2,4096]{1,0:T(2,128)(2,1)S(1)}, bf16[2,4096]{1,0:T(2,128)(2,1)S(1)}, u32[]{:S(2)}, u32[]{:S(2)}) %collective-permute-start.1) | collective-permute-done | bytes 16416 | tf_op jit(solution)/shard_map/ppermute | solution.py:131
  7.7 1.9 %collective-permute-start.2 = (bf16[4,4096]{1,0:T(4,128)(2,1)S(1)}, bf16[4,4096]{1,0:T(4,128)(2,1)S(1)}, u32[]{:S(2)}, u32[]{:S(2)}) collective-permute-start(bf16[4,4096]{1,0:T(4,128)(2,1)S(1)} %shard_map.59.refs_0_), channel_id=1, source_target_pairs={{0,4},{2,6},{4,0},{6,2},{8,12},{10,14},{12,8},{14,10},{1,5},{3,7},... | collective-permute-start | bytes 98312 | tf_op jit(solution)/shard_map/ppermute | solution.py:137
  9.6 2.1 %collective-permute-done.2.refs_1_ = bf16[4,4096]{1,0:T(4,128)(2,1)S(1)} collective-permute-done((bf16[4,4096]{1,0:T(4,128)(2,1)S(1)}, bf16[4,4096]{1,0:T(4,128)(2,1)S(1)}, u32[]{:S(2)}, u32[]{:S(2)}) %collective-permute-start.2) | collective-permute-done | bytes 32800 | tf_op jit(solution)/shard_map/ppermute | solution.py:137
  11.7 1.8 %collective-permute-start.3 = (bf16[8,4096]{1,0:T(8,128)(2,1)S(1)}, bf16[8,4096]{1,0:T(8,128)(2,1)S(1)}, u32[]{:S(2)}, u32[]{:S(2)}) collective-permute-start(bf16[8,4096]{1,0:T(8,128)(2,1)S(1)} %shard_map.60.refs_0_), channel_id=1, source_target_pairs={{0,2},{2,0},{4,6},{6,4},{8,10},{10,8},{12,14},{14,12},{1,3},{3,1},... | collective-permute-start | bytes 196616 | tf_op jit(solution)/shard_map/ppermute | solution.py:137
  13.5 2.5 %collective-permute-done.3.refs_1_ = bf16[8,4096]{1,0:T(8,128)(2,1)S(1)} collective-permute-done((bf16[8,4096]{1,0:T(8,128)(2,1)S(1)}, bf16[8,4096]{1,0:T(8,128)(2,1)S(1)}, u32[]{:S(2)}, u32[]{:S(2)}) %collective-permute-start.3) | collective-permute-done | bytes 65568 | tf_op jit(solution)/shard_map/ppermute | solution.py:137
  16.1 0.0 slice-start.13
  16.1 3.6 %shard_map.63 = (f32[16,3328]{1,0:T(8,128)S(1)}, bf16[16,3328]{1,0:T(8,128)(2,1)S(1)}, bf16[512,4096]{1,0:T(8,128)(2,1)S(1)}) custom-call(bf16[16,4096]{1,0:T(8,128)(2,1)S(1)} %shard_map.61.refs_0_, bf16[4096,3328]{1,0:T(8,128)(2,1)S(1)} %bitcast.4, bf16[3328,4096]{1,0:T(8,128)(2,1)} %refs_4_.1), custom_call_target="tpu_custom_call" | custom-call | flops 436207616 | bytes 27262976 | tf_op jit(solution)/shard_map/pallas_call | solution.py:27
  19.8 0.1 collective-permute-start.5
  20.0 4.0 %shard_map.62 = (f32[16,3328]{1,0:T(8,128)S(1)}, bf16[16,3328]{1,0:T(8,128)(2,1)S(1)}, bf16[1280,4096]{1,0:T(8,128)(2,1)S(1)}) custom-call(bf16[16,4096]{1,0:T(8,128)(2,1)S(1)} %shard_map.61.refs_0_, bf16[4096,3328]{1,0:T(8,128)(2,1)S(1)} %bitcast.6, bf16[3328,4096]{1,0:T(8,128)(2,1)} %refs_4_.1), custom_call_target="tpu_custom_call" | custom-call | flops 436207616 | bytes 27262976 | tf_op jit(solution)/shard_map/pallas_call | solution.py:27
  24.0 0.5 %collective-permute-start.4 = (bf16[16,3328]{1,0:T(8,128)(2,1)S(1)}, bf16[16,3328]{1,0:T(8,128)(2,1)S(1)}, u32[]{:S(2)}, u32[]{:S(2)}) collective-permute-start(bf16[16,3328]{1,0:T(8,128)(2,1)S(1)} %get-tuple-element.22), channel_id=1, source_target_pairs={{0,1},{1,0},{2,3},{3,2},{4,5},{5,4},{6,7},{7,6},{8,9},{9,8},{10,11... | collective-permute-start | bytes 319496 | tf_op jit(solution)/shard_map/ppermute | solution.py:137
  24.5 1.0 %collective-permute-done.4.refs_1_ = bf16[16,3328]{1,0:T(8,128)(2,1)S(1)} collective-permute-done((bf16[16,3328]{1,0:T(8,128)(2,1)S(1)}, bf16[16,3328]{1,0:T(8,128)(2,1)S(1)}, u32[]{:S(2)}, u32[]{:S(2)}) %collective-permute-start.4) | collective-permute-done | bytes 106528 | tf_op jit(solution)/shard_map/ppermute | solution.py:137
  25.5 5.3 %shard_map.64 = (f32[8,4096]{1,0:T(8,128)S(1)}, bf16[8,4096]{1,0:T(8,128)(2,1)S(1)}) custom-call(f32[16,3328]{1,0:T(8,128)S(1)} %get-tuple-element.21.refs_0_, bf16[16,3328]{1,0:T(8,128)(2,1)S(1)} %collective-permute-done.4.refs_1_, f32[16,3328]{1,0:T(8,128)S(1)} %get-tuple-element.23.refs_2_, bf16[16,3328]{1,0:T(8,128)(2,1)S(1)} %collective-permute-done.5.refs_3_, ...), custom_call_target="tpu_custom_call" | custom-call | flops 436207616 | bytes 27262976 | tf_op jit(solution)/shard_map/pallas_call | solution.py:27
  30.8 1.8 %collective-permute-start.6 = (bf16[8,4096]{1,0:T(8,128)(2,1)S(1)}, bf16[8,4096]{1,0:T(8,128)(2,1)S(1)}, u32[]{:S(2)}, u32[]{:S(2)}) collective-permute-start(bf16[8,4096]{1,0:T(8,128)(2,1)S(1)} %get-tuple-element.28), channel_id=1, source_target_pairs={{0,2},{2,0},{4,6},{6,4},{8,10},{10,8},{12,14},{14,12},{1,3},{3,1},... | collective-permute-start | bytes 196616 | tf_op jit(solution)/shard_map/ppermute | solution.py:137
  32.6 2.6 %collective-permute-done.6.refs_1_ = bf16[8,4096]{1,0:T(8,128)(2,1)S(1)} collective-permute-done((bf16[8,4096]{1,0:T(8,128)(2,1)S(1)}, bf16[8,4096]{1,0:T(8,128)(2,1)S(1)}, u32[]{:S(2)}, u32[]{:S(2)}) %collective-permute-start.6) | collective-permute-done | bytes 65568 | tf_op jit(solution)/shard_map/ppermute | solution.py:137
  35.3 1.9 %collective-permute-start.7 = (bf16[4,4096]{1,0:T(4,128)(2,1)S(1)}, bf16[4,4096]{1,0:T(4,128)(2,1)S(1)}, u32[]{:S(2)}, u32[]{:S(2)}) collective-permute-start(bf16[4,4096]{1,0:T(4,128)(2,1)S(1)} %get-tuple-element.30), channel_id=1, source_target_pairs={{0,4},{2,6},{4,0},{6,2},{8,12},{10,14},{12,8},{14,10},{1,5},{3,7},... | collective-permute-start | bytes 98312 | tf_op jit(solution)/shard_map/ppermute | solution.py:137
  37.1 2.1 %collective-permute-done.7.refs_1_ = bf16[4,4096]{1,0:T(4,128)(2,1)S(1)} collective-permute-done((bf16[4,4096]{1,0:T(4,128)(2,1)S(1)}, bf16[4,4096]{1,0:T(4,128)(2,1)S(1)}, u32[]{:S(2)}, u32[]{:S(2)}) %collective-permute-start.7) | collective-permute-done | bytes 32800 | tf_op jit(solution)/shard_map/ppermute | solution.py:137
  39.3 2.9 %collective-permute-start.8 = (bf16[2,4096]{1,0:T(2,128)(2,1)S(1)}, bf16[2,4096]{1,0:T(2,128)(2,1)S(1)}, u32[]{:S(2)}, u32[]{:S(2)}) collective-permute-start(bf16[2,4096]{1,0:T(2,128)(2,1)S(1)} %get-tuple-element.32), channel_id=1, source_target_pairs={{0,8},{2,10},{4,12},{6,14},{8,0},{10,2},{12,4},{14,6},{1,9},{3,11}... | collective-permute-start | bytes 49160 | tf_op jit(solution)/shard_map/ppermute | solution.py:137
  42.2 1.8 %collective-permute-done.8.refs_1_ = bf16[2,4096]{1,0:T(2,128)(2,1)S(1)} collective-permute-done((bf16[2,4096]{1,0:T(2,128)(2,1)S(1)}, bf16[2,4096]{1,0:T(2,128)(2,1)S(1)}, u32[]{:S(2)}, u32[]{:S(2)}) %collective-permute-start.8) | collective-permute-done | bytes 16416 | tf_op jit(solution)/shard_map/ppermute | solution.py:137
  44.0 0.6 %shard_map.67 = bf16[2,4096]{1,0:T(2,128)(2,1)} custom-call(f32[2,4096]{1,0:T(2,128)S(1)} %get-tuple-element.31.refs_0_, bf16[2,4096]{1,0:T(2,128)(2,1)S(1)} %collective-permute-done.8.refs_1_), custom_call_target="tpu_custom_call" | custom-call | tf_op jit(solution)/shard_map/pallas_call | solution.py:27
  (33 shorter events, 0.1 us)
Async XLA Ops:
  0.0 16.1 %slice-start = ((s8[27262976]{0:T(1024)(128)(4,1)}), s8[4194304]{0:T(1024)(128)(4,1)S(1)}, s32[]{:S(2)}) async-start(s8[27262976]{0:T(1024)(128)(4,1)} %bitcast.3), calls=%async_computation | async-start | bytes 8388608
  0.0 0.9 %copy-start = (bf16[2,1,4096]{2,0,1:T(2,128)(2,1)S(1)}, bf16[2,1,4096]{2,0,1:T(2,128)(2,1)}, u32[]{:S(2)}) copy-start(bf16[2,1,4096]{2,0,1:T(2,128)(2,1)} %param.5) | copy-start | bytes 49156
  0.0 0.9 %copy-start.1 = (f32[4096]{0:T(1024)S(1)}, f32[4096]{0:T(1024)}, u32[]{:S(2)}) copy-start(f32[4096]{0:T(1024)} %param.6) | copy-start | bytes 49156
  0.0 16.1 %slice-start.1 = ((s8[27262976]{0:T(1024)(128)(4,1)}), s8[4194304]{0:T(1024)(128)(4,1)S(1)}, s32[]{:S(2)}) async-start(s8[27262976]{0:T(1024)(128)(4,1)} %bitcast.3), calls=%async_computation.1 | async-start | bytes 8388608
  0.0 16.1 %slice-start.2 = ((s8[27262976]{0:T(1024)(128)(4,1)}), s8[4194304]{0:T(1024)(128)(4,1)S(1)}, s32[]{:S(2)}) async-start(s8[27262976]{0:T(1024)(128)(4,1)} %bitcast.3), calls=%async_computation.2 | async-start | bytes 8388608
  0.0 16.1 %slice-start.3 = ((s8[27262976]{0:T(1024)(128)(4,1)}), s8[4194304]{0:T(1024)(128)(4,1)S(1)}, s32[]{:S(2)}) async-start(s8[27262976]{0:T(1024)(128)(4,1)} %bitcast.3), calls=%async_computation.3 | async-start | bytes 8388608
  0.0 16.1 %slice-start.4 = ((s8[27262976]{0:T(1024)(128)(4,1)}), s8[4194304]{0:T(1024)(128)(4,1)S(1)}, s32[]{:S(2)}) async-start(s8[27262976]{0:T(1024)(128)(4,1)} %bitcast.3), calls=%async_computation.4 | async-start | bytes 8388608
  0.0 16.1 %slice-start.5 = ((s8[27262976]{0:T(1024)(128)(4,1)}), s8[4194304]{0:T(1024)(128)(4,1)S(1)}, s32[]{:S(2)}) async-start(s8[27262976]{0:T(1024)(128)(4,1)} %bitcast.3), calls=%async_computation.5 | async-start | bytes 8388608
  0.1 16.1 %slice-start.6 = ((s8[27262976]{0:T(1024)(128)(4,1)}), s8[2097152]{0:T(1024)(128)(4,1)S(1)}, s32[]{:S(2)}) async-start(s8[27262976]{0:T(1024)(128)(4,1)} %bitcast.3), calls=%async_computation.6 | async-start | bytes 4194304
  0.1 19.8 %slice-start.7 = ((s8[27262976]{0:T(1024)(128)(4,1)}), s8[2097152]{0:T(1024)(128)(4,1)S(1)}, s32[]{:S(2)}) async-start(s8[27262976]{0:T(1024)(128)(4,1)} %bitcast.5), calls=%async_computation.7 | async-start | bytes 4194304
  0.1 19.8 %slice-start.8 = ((s8[27262976]{0:T(1024)(128)(4,1)}), s8[4194304]{0:T(1024)(128)(4,1)S(1)}, s32[]{:S(2)}) async-start(s8[27262976]{0:T(1024)(128)(4,1)} %bitcast.5), calls=%async_computation.8 | async-start | bytes 8388608
  0.1 19.8 %slice-start.9 = ((s8[27262976]{0:T(1024)(128)(4,1)}), s8[4194304]{0:T(1024)(128)(4,1)S(1)}, s32[]{:S(2)}) async-start(s8[27262976]{0:T(1024)(128)(4,1)} %bitcast.5), calls=%async_computation.9 | async-start | bytes 8388608
  0.1 19.8 %slice-start.10 = ((s8[27262976]{0:T(1024)(128)(4,1)}), s8[4194304]{0:T(1024)(128)(4,1)S(1)}, s32[]{:S(2)}) async-start(s8[27262976]{0:T(1024)(128)(4,1)} %bitcast.5), calls=%async_computation.10 | async-start | bytes 8388608
  0.1 19.8 %slice-start.11 = ((s8[27262976]{0:T(1024)(128)(4,1)}), s8[4194304]{0:T(1024)(128)(4,1)S(1)}, s32[]{:S(2)}) async-start(s8[27262976]{0:T(1024)(128)(4,1)} %bitcast.5), calls=%async_computation.11 | async-start | bytes 8388608
  0.1 19.8 %slice-start.12 = ((s8[27262976]{0:T(1024)(128)(4,1)}), s8[4194304]{0:T(1024)(128)(4,1)S(1)}, s32[]{:S(2)}) async-start(s8[27262976]{0:T(1024)(128)(4,1)} %bitcast.5), calls=%async_computation.12 | async-start | bytes 8388608
  0.9 1.4 %collective-permute-start = (f32[3,4096]{1,0:T(4,128)S(1)}, f32[3,4096]{1,0:T(4,128)S(1)}, u32[]{:S(2)}, u32[]{:S(2)}) collective-permute-start(f32[3,4096]{1,0:T(4,128)S(1)} %shard_map.57.refs_0_), channel_id=1, source_target_pairs={{0,1},{1,0},{2,3},{3,2},{4,5},{5,4},{6,7},{7,6},{8,9},{9,8},{10,11... | collective-permute-start | bytes 147464 | tf_op jit(solution)/shard_map/ppermute | solution.py:137
  2.5 5.2 %collective-permute-start.1 = (bf16[2,4096]{1,0:T(2,128)(2,1)S(1)}, bf16[2,4096]{1,0:T(2,128)(2,1)S(1)}, u32[]{:S(2)}, u32[]{:S(2)}) collective-permute-start(bf16[2,4096]{1,0:T(2,128)(2,1)S(1)} %get-tuple-element.20), channel_id=1, source_target_pairs={{0,9},{1,8},{2,11},{3,10},{4,13},{5,12},{6,15},{7,14},{8,1},{9,0},... | collective-permute-start | bytes 49160 | tf_op jit(solution)/shard_map/ppermute | solution.py:131
  7.7 4.0 %collective-permute-start.2 = (bf16[4,4096]{1,0:T(4,128)(2,1)S(1)}, bf16[4,4096]{1,0:T(4,128)(2,1)S(1)}, u32[]{:S(2)}, u32[]{:S(2)}) collective-permute-start(bf16[4,4096]{1,0:T(4,128)(2,1)S(1)} %shard_map.59.refs_0_), channel_id=1, source_target_pairs={{0,4},{2,6},{4,0},{6,2},{8,12},{10,14},{12,8},{14,10},{1,5},{3,7},... | collective-permute-start | bytes 98312 | tf_op jit(solution)/shard_map/ppermute | solution.py:137
  11.7 4.3 %collective-permute-start.3 = (bf16[8,4096]{1,0:T(8,128)(2,1)S(1)}, bf16[8,4096]{1,0:T(8,128)(2,1)S(1)}, u32[]{:S(2)}, u32[]{:S(2)}) collective-permute-start(bf16[8,4096]{1,0:T(8,128)(2,1)S(1)} %shard_map.60.refs_0_), channel_id=1, source_target_pairs={{0,2},{2,0},{4,6},{6,4},{8,10},{10,8},{12,14},{14,12},{1,3},{3,1},... | collective-permute-start | bytes 196616 | tf_op jit(solution)/shard_map/ppermute | solution.py:137
  16.1 3.8 %slice-start.13 = ((s8[27262976]{0:T(1024)(128)(4,1)}), s8[4194304]{0:T(1024)(128)(4,1)S(1)}, s32[]{:S(2)}) async-start(s8[27262976]{0:T(1024)(128)(4,1)} %bitcast.5), calls=%async_computation.13 | async-start | bytes 8388608
  19.8 4.7 %collective-permute-start.5 = (bf16[16,3328]{1,0:T(8,128)(2,1)S(1)}, bf16[16,3328]{1,0:T(8,128)(2,1)S(1)}, u32[]{:S(2)}, u32[]{:S(2)}) collective-permute-start(bf16[16,3328]{1,0:T(8,128)(2,1)S(1)} %get-tuple-element.24), channel_id=1, source_target_pairs={{0,1},{1,0},{2,3},{3,2},{4,5},{5,4},{6,7},{7,6},{8,9},{9,8},{10,11... | collective-permute-start | bytes 319496 | tf_op jit(solution)/shard_map/ppermute | solution.py:137
  24.0 1.5 %collective-permute-start.4 = (bf16[16,3328]{1,0:T(8,128)(2,1)S(1)}, bf16[16,3328]{1,0:T(8,128)(2,1)S(1)}, u32[]{:S(2)}, u32[]{:S(2)}) collective-permute-start(bf16[16,3328]{1,0:T(8,128)(2,1)S(1)} %get-tuple-element.22), channel_id=1, source_target_pairs={{0,1},{1,0},{2,3},{3,2},{4,5},{5,4},{6,7},{7,6},{8,9},{9,8},{10,11... | collective-permute-start | bytes 319496 | tf_op jit(solution)/shard_map/ppermute | solution.py:137
  30.8 4.4 %collective-permute-start.6 = (bf16[8,4096]{1,0:T(8,128)(2,1)S(1)}, bf16[8,4096]{1,0:T(8,128)(2,1)S(1)}, u32[]{:S(2)}, u32[]{:S(2)}) collective-permute-start(bf16[8,4096]{1,0:T(8,128)(2,1)S(1)} %get-tuple-element.28), channel_id=1, source_target_pairs={{0,2},{2,0},{4,6},{6,4},{8,10},{10,8},{12,14},{14,12},{1,3},{3,1},... | collective-permute-start | bytes 196616 | tf_op jit(solution)/shard_map/ppermute | solution.py:137
  35.3 4.0 %collective-permute-start.7 = (bf16[4,4096]{1,0:T(4,128)(2,1)S(1)}, bf16[4,4096]{1,0:T(4,128)(2,1)S(1)}, u32[]{:S(2)}, u32[]{:S(2)}) collective-permute-start(bf16[4,4096]{1,0:T(4,128)(2,1)S(1)} %get-tuple-element.30), channel_id=1, source_target_pairs={{0,4},{2,6},{4,0},{6,2},{8,12},{10,14},{12,8},{14,10},{1,5},{3,7},... | collective-permute-start | bytes 98312 | tf_op jit(solution)/shard_map/ppermute | solution.py:137
  39.3 4.7 %collective-permute-start.8 = (bf16[2,4096]{1,0:T(2,128)(2,1)S(1)}, bf16[2,4096]{1,0:T(2,128)(2,1)S(1)}, u32[]{:S(2)}, u32[]{:S(2)}) collective-permute-start(bf16[2,4096]{1,0:T(2,128)(2,1)S(1)} %get-tuple-element.32), channel_id=1, source_target_pairs={{0,8},{2,10},{4,12},{6,14},{8,0},{10,2},{12,4},{14,6},{1,9},{3,11}... | collective-permute-start | bytes 49160 | tf_op jit(solution)/shard_map/ppermute | solution.py:137

commit v7 on v6

--- a/solution.py
+++ b/solution.py
@@ -65,10 +65,11 @@
     out_ref[rows:, :] = second_ref[...]
 
 
-def project_kernel(ahead, chunk, first, x_ref, w_ref, down_ref, out_ref, send_ref, *rest):
+def project_kernel(narrow, ahead, chunk, first, x_ref, w_ref, down_ref, out_ref, *rest):
     copies = []
+    send_ref = None if narrow is None else rest[0]
     if ahead:
-        taken_ref, sem = rest
+        taken_ref, sem = rest[-2:]
         copies.append(pltpu.make_async_copy(down_ref.at[pl.ds(first * chunk, ahead * chunk), :], taken_ref, sem))
         copies[-1].start()
     columns = w_ref.shape[1]
@@ -76,7 +77,8 @@
         e = min(c + 256, columns)
         part = jnp.dot(x_ref[...], w_ref[:, c:e], preferred_element_type=f32)
         out_ref[:, c:e] = part
-        send_ref[:, c:e] = part.astype(send_ref.dtype)
+        if send_ref is not None:
+            send_ref[:, c:e] = part.astype(narrow)
     for copy in copies:
         copy.wait()
 
@@ -161,27 +163,33 @@
     counts = (count * UP_SHARE // 13, count * GATE_SHARE // 13)
     counts = (*counts, count - sum(counts))
 
-    def project(weight, first, ahead):
-        outs = [Shape((rows, units), f32), Shape((rows, units), bf16)]
+    def project(weight, first, ahead, narrow=None):
+        outs = [Shape((rows, units), f32)]
+        if narrow is not None:
+            outs.append(Shape((rows, units), narrow))
         scratch = []
         if ahead:
             outs.append(Shape((ahead * chunk, half), bf16))
             scratch.append(pltpu.SemaphoreType.DMA)
         return call(
-            functools.partial(project_kernel, ahead, chunk, first),
+            functools.partial(project_kernel, narrow, ahead, chunk, first),
             outs, held, weight, down_weight,
             specs=[VMEM, VMEM, HBM], scratch=scratch, flops=2 * rows * weight.size,
         )
 
-    up, up_send, *taken_up = project(up_weight, 0, counts[0])
-    up_other = swap(up_send, "gy", halves, 1)
-    gate, gate_send, *taken_gate = project(gate_weight, counts[0], counts[1])
+    up, *taken_up = project(up_weight, 0, counts[0])
+    up_other = swap(up, "gy", halves, 1)
+    gate, gate_send, *taken_gate = project(gate_weight, counts[0], counts[1], bf16)
     gate_other = swap(gate_send, "gy", halves, 1)
     taken = (*taken_up, *taken_gate)
     start = sum(counts[:-1]) * chunk
     bounds = [start]
     while bounds[-1] < units:
-        bounds.append(bounds[-1] + (2 * chunk if units - bounds[-1] > 3 * chunk else chunk))
+        left = units - bounds[-1]
+        step = 2 * chunk if left > 3 * chunk else chunk
+        if left <= chunk and chunk % 256 == 0:
+            step = chunk // 2
+        bounds.append(bounds[-1] + min(step, left))
     keep, send = call(
         functools.partial(down_kernel, bounds),
         (Shape((rows // 2, half), f32), Shape((rows // 2, half), bf16)),

time: 44.7 us -> 44.4 us (level)
  no operation moved by 1% of the time
where the time goes in v7:
time: 44.4 us; the launch traced here: 44.2 us
  starting transfers between devices  15.3 us (34%)
  waiting for transfers between devices  14.4 us (32%)
  Pallas kernels  13.5 us (30%)
  local copies, waits for them, and re-layouts  0.77 us (2%)
    pallas_call x13, Pallas kernels, call(): pl.pallas_call(lambda *refs: kernel(*refs[skip:]), out_shape=outs, in_spe...  13.5 us
    ppermute x8, waiting for transfers between devices, swap(): return lax.ppermute(x, axis, [(i, i ^ mask) for i in range(size)])  12.9 us
    ppermute x8, starting transfers between devices, swap(): return lax.ppermute(x, axis, [(i, i ^ mask) for i in range(size)])  11.5 us
    ppermute x1, starting transfers between devices, cross(): lax.ppermute(x, ('gx', 'gy'), [(2 * i + c, 2 * (i ^ mask) + 1 - c) for i...  3.76 us
    ppermute x1, waiting for transfers between devices, cross(): lax.ppermute(x, ('gx', 'gy'), [(2 * i + c, 2 * (i ^ mask) + 1 - c) for i...  1.44 us
  transfers between devices with their start and end apart: 9, of which 8 were waited for; matrix products, arithmetic and copies ran while one was open for 0% of the time, Pallas kernels for 9%

profile of v7, /device:TPU:0, one launch (start us, length us, event | category | flops | bytes accessed | tf_op | source)
XLA Modules:
  0.0 44.2 jit_solution(17959659856014783313)
XLA Ops:
  0.1 0.0 slice-start.7
  0.1 0.0 slice-start.8
  0.1 0.0 slice-start.9
  0.1 0.0 slice-start.10
  0.1 0.0 slice-start.11
  0.1 0.0 slice-start.12
  0.1 0.1 shard_map.56.refs_0_
  0.2 0.7 %copy-done = bf16[2,1,4096]{2,0,1:T(2,128)(2,1)S(1)} copy-done((bf16[2,1,4096]{2,0,1:T(2,128)(2,1)S(1)}, bf16[2,1,4096]{2,0,1:T(2,128)(2,1)}, u32[]{:S(2)}) %copy-start) | copy-done | bytes 16408
  0.9 0.0 copy-done.1
  0.9 0.5 %collective-permute-start = (f32[3,4096]{1,0:T(4,128)S(1)}, f32[3,4096]{1,0:T(4,128)S(1)}, u32[]{:S(2)}, u32[]{:S(2)}) collective-permute-start(f32[3,4096]{1,0:T(4,128)S(1)} %shard_map.57.refs_0_), channel_id=1, source_target_pairs={{0,1},{1,0},{2,3},{3,2},{4,5},{5,4},{6,7},{7,6},{8,9},{9,8},{10,11... | collective-permute-start | bytes 147464 | tf_op jit(solution)/shard_map/ppermute | solution.py:139
  1.4 0.9 %collective-permute-done.refs_1_ = f32[3,4096]{1,0:T(4,128)S(1)} collective-permute-done((f32[3,4096]{1,0:T(4,128)S(1)}, f32[3,4096]{1,0:T(4,128)S(1)}, u32[]{:S(2)}, u32[]{:S(2)}) %collective-permute-start) | collective-permute-done | bytes 49184 | tf_op jit(solution)/shard_map/ppermute | solution.py:139
  2.3 0.2 shard_map.58
  2.5 3.8 %collective-permute-start.1 = (bf16[2,4096]{1,0:T(2,128)(2,1)S(1)}, bf16[2,4096]{1,0:T(2,128)(2,1)S(1)}, u32[]{:S(2)}, u32[]{:S(2)}) collective-permute-start(bf16[2,4096]{1,0:T(2,128)(2,1)S(1)} %get-tuple-element.19), channel_id=1, source_target_pairs={{0,9},{1,8},{2,11},{3,10},{4,13},{5,12},{6,15},{7,14},{8,1},{9,0},... | collective-permute-start | bytes 49160 | tf_op jit(solution)/shard_map/ppermute | solution.py:133
  6.2 1.4 %collective-permute-done.1.refs_1_ = bf16[2,4096]{1,0:T(2,128)(2,1)S(1)} collective-permute-done((bf16[2,4096]{1,0:T(2,128)(2,1)S(1)}, bf16[2,4096]{1,0:T(2,128)(2,1)S(1)}, u32[]{:S(2)}, u32[]{:S(2)}) %collective-permute-start.1) | collective-permute-done | bytes 16416 | tf_op jit(solution)/shard_map/ppermute | solution.py:133
  7.7 1.9 %collective-permute-start.2 = (bf16[4,4096]{1,0:T(4,128)(2,1)S(1)}, bf16[4,4096]{1,0:T(4,128)(2,1)S(1)}, u32[]{:S(2)}, u32[]{:S(2)}) collective-permute-start(bf16[4,4096]{1,0:T(4,128)(2,1)S(1)} %shard_map.59.refs_0_), channel_id=1, source_target_pairs={{0,4},{2,6},{4,0},{6,2},{8,12},{10,14},{12,8},{14,10},{1,5},{3,7},... | collective-permute-start | bytes 98312 | tf_op jit(solution)/shard_map/ppermute | solution.py:139
  9.6 2.1 %collective-permute-done.2.refs_1_ = bf16[4,4096]{1,0:T(4,128)(2,1)S(1)} collective-permute-done((bf16[4,4096]{1,0:T(4,128)(2,1)S(1)}, bf16[4,4096]{1,0:T(4,128)(2,1)S(1)}, u32[]{:S(2)}, u32[]{:S(2)}) %collective-permute-start.2) | collective-permute-done | bytes 32800 | tf_op jit(solution)/shard_map/ppermute | solution.py:139
  11.7 1.8 %collective-permute-start.3 = (bf16[8,4096]{1,0:T(8,128)(2,1)S(1)}, bf16[8,4096]{1,0:T(8,128)(2,1)S(1)}, u32[]{:S(2)}, u32[]{:S(2)}) collective-permute-start(bf16[8,4096]{1,0:T(8,128)(2,1)S(1)} %shard_map.60.refs_0_), channel_id=1, source_target_pairs={{0,2},{2,0},{4,6},{6,4},{8,10},{10,8},{12,14},{14,12},{1,3},{3,1},... | collective-permute-start | bytes 196616 | tf_op jit(solution)/shard_map/ppermute | solution.py:139
  13.5 2.5 %collective-permute-done.3.refs_1_ = bf16[8,4096]{1,0:T(8,128)(2,1)S(1)} collective-permute-done((bf16[8,4096]{1,0:T(8,128)(2,1)S(1)}, bf16[8,4096]{1,0:T(8,128)(2,1)S(1)}, u32[]{:S(2)}, u32[]{:S(2)}) %collective-permute-start.3) | collective-permute-done | bytes 65568 | tf_op jit(solution)/shard_map/ppermute | solution.py:139
  16.1 0.0 slice-start.13
  16.1 3.7 %shard_map.63 = (f32[16,3328]{1,0:T(8,128)S(1)}, bf16[512,4096]{1,0:T(8,128)(2,1)S(1)}) custom-call(bf16[16,4096]{1,0:T(8,128)(2,1)S(1)} %shard_map.61.refs_0_, bf16[4096,3328]{1,0:T(8,128)(2,1)S(1)} %bitcast.4, bf16[3328,4096]{1,0:T(8,128)(2,1)} %refs_4_.1), custom_call_target="tpu_custom_call" | custom-call | flops 436207616 | bytes 27262976 | tf_op jit(solution)/shard_map/pallas_call | solution.py:27
  19.8 0.1 collective-permute-start.5
  20.0 4.0 %shard_map.62 = (f32[16,3328]{1,0:T(8,128)S(1)}, bf16[16,3328]{1,0:T(8,128)(2,1)S(1)}, bf16[1280,4096]{1,0:T(8,128)(2,1)S(1)}) custom-call(bf16[16,4096]{1,0:T(8,128)(2,1)S(1)} %shard_map.61.refs_0_, bf16[4096,3328]{1,0:T(8,128)(2,1)S(1)} %bitcast.6, bf16[3328,4096]{1,0:T(8,128)(2,1)} %refs_4_.1), custom_call_target="tpu_custom_call" | custom-call | flops 436207616 | bytes 27262976 | tf_op jit(solution)/shard_map/pallas_call | solution.py:27
  24.0 0.5 %collective-permute-start.4 = (bf16[16,3328]{1,0:T(8,128)(2,1)S(1)}, bf16[16,3328]{1,0:T(8,128)(2,1)S(1)}, u32[]{:S(2)}, u32[]{:S(2)}) collective-permute-start(bf16[16,3328]{1,0:T(8,128)(2,1)S(1)} %get-tuple-element.21), channel_id=1, source_target_pairs={{0,1},{1,0},{2,3},{3,2},{4,5},{5,4},{6,7},{7,6},{8,9},{9,8},{10,11... | collective-permute-start | bytes 319496 | tf_op jit(solution)/shard_map/ppermute | solution.py:139
  24.5 1.0 %collective-permute-done.4.refs_1_ = bf16[16,3328]{1,0:T(8,128)(2,1)S(1)} collective-permute-done((bf16[16,3328]{1,0:T(8,128)(2,1)S(1)}, bf16[16,3328]{1,0:T(8,128)(2,1)S(1)}, u32[]{:S(2)}, u32[]{:S(2)}) %collective-permute-start.4) | collective-permute-done | bytes 106528 | tf_op jit(solution)/shard_map/ppermute | solution.py:139
  25.5 4.9 %shard_map.64 = (f32[8,4096]{1,0:T(8,128)S(1)}, bf16[8,4096]{1,0:T(8,128)(2,1)S(1)}) custom-call(f32[16,3328]{1,0:T(8,128)S(1)} %get-tuple-element.20.refs_0_, bf16[16,3328]{1,0:T(8,128)(2,1)S(1)} %collective-permute-done.4.refs_1_, f32[16,3328]{1,0:T(8,128)S(1)} %get-tuple-element.22.refs_2_, f32[16,3328]{1,0:T(8,128)S(1)} %collective-permute-done.5.refs_3_, ...), custom_call_target="tpu_custom_call" | custom-call | flops 436207616 | bytes 27262976 | tf_op jit(solution)/shard_map/pallas_call | solution.py:27
  30.4 1.8 %collective-permute-start.6 = (bf16[8,4096]{1,0:T(8,128)(2,1)S(1)}, bf16[8,4096]{1,0:T(8,128)(2,1)S(1)}, u32[]{:S(2)}, u32[]{:S(2)}) collective-permute-start(bf16[8,4096]{1,0:T(8,128)(2,1)S(1)} %get-tuple-element.26), channel_id=1, source_target_pairs={{0,2},{2,0},{4,6},{6,4},{8,10},{10,8},{12,14},{14,12},{1,3},{3,1},... | collective-permute-start | bytes 196616 | tf_op jit(solution)/shard_map/ppermute | solution.py:139
  32.3 2.6 %collective-permute-done.6.refs_1_ = bf16[8,4096]{1,0:T(8,128)(2,1)S(1)} collective-permute-done((bf16[8,4096]{1,0:T(8,128)(2,1)S(1)}, bf16[8,4096]{1,0:T(8,128)(2,1)S(1)}, u32[]{:S(2)}, u32[]{:S(2)}) %collective-permute-start.6) | collective-permute-done | bytes 65568 | tf_op jit(solution)/shard_map/ppermute | solution.py:139
  34.9 1.9 %collective-permute-start.7 = (bf16[4,4096]{1,0:T(4,128)(2,1)S(1)}, bf16[4,4096]{1,0:T(4,128)(2,1)S(1)}, u32[]{:S(2)}, u32[]{:S(2)}) collective-permute-start(bf16[4,4096]{1,0:T(4,128)(2,1)S(1)} %get-tuple-element.28), channel_id=1, source_target_pairs={{0,4},{2,6},{4,0},{6,2},{8,12},{10,14},{12,8},{14,10},{1,5},{3,7},... | collective-permute-start | bytes 98312 | tf_op jit(solution)/shard_map/ppermute | solution.py:139
  36.8 2.1 %collective-permute-done.7.refs_1_ = bf16[4,4096]{1,0:T(4,128)(2,1)S(1)} collective-permute-done((bf16[4,4096]{1,0:T(4,128)(2,1)S(1)}, bf16[4,4096]{1,0:T(4,128)(2,1)S(1)}, u32[]{:S(2)}, u32[]{:S(2)}) %collective-permute-start.7) | collective-permute-done | bytes 32800 | tf_op jit(solution)/shard_map/ppermute | solution.py:139
  38.9 2.9 %collective-permute-start.8 = (bf16[2,4096]{1,0:T(2,128)(2,1)S(1)}, bf16[2,4096]{1,0:T(2,128)(2,1)S(1)}, u32[]{:S(2)}, u32[]{:S(2)}) collective-permute-start(bf16[2,4096]{1,0:T(2,128)(2,1)S(1)} %get-tuple-element.30), channel_id=1, source_target_pairs={{0,8},{2,10},{4,12},{6,14},{8,0},{10,2},{12,4},{14,6},{1,9},{3,11}... | collective-permute-start | bytes 49160 | tf_op jit(solution)/shard_map/ppermute | solution.py:139
  41.8 1.8 %collective-permute-done.8.refs_1_ = bf16[2,4096]{1,0:T(2,128)(2,1)S(1)} collective-permute-done((bf16[2,4096]{1,0:T(2,128)(2,1)S(1)}, bf16[2,4096]{1,0:T(2,128)(2,1)S(1)}, u32[]{:S(2)}, u32[]{:S(2)}) %collective-permute-start.8) | collective-permute-done | bytes 16416 | tf_op jit(solution)/shard_map/ppermute | solution.py:139
  43.6 0.6 %shard_map.67 = bf16[2,4096]{1,0:T(2,128)(2,1)} custom-call(f32[2,4096]{1,0:T(2,128)S(1)} %get-tuple-element.29.refs_0_, bf16[2,4096]{1,0:T(2,128)(2,1)S(1)} %collective-permute-done.8.refs_1_), custom_call_target="tpu_custom_call" | custom-call | tf_op jit(solution)/shard_map/pallas_call | solution.py:27
  (33 shorter events, 0.1 us)
Async XLA Ops:
  0.0 16.1 %slice-start = ((s8[27262976]{0:T(1024)(128)(4,1)}), s8[4194304]{0:T(1024)(128)(4,1)S(1)}, s32[]{:S(2)}) async-start(s8[27262976]{0:T(1024)(128)(4,1)} %bitcast.3), calls=%async_computation | async-start | bytes 8388608
  0.0 0.9 %copy-start = (bf16[2,1,4096]{2,0,1:T(2,128)(2,1)S(1)}, bf16[2,1,4096]{2,0,1:T(2,128)(2,1)}, u32[]{:S(2)}) copy-start(bf16[2,1,4096]{2,0,1:T(2,128)(2,1)} %param.5) | copy-start | bytes 49156
  0.0 0.9 %copy-start.1 = (f32[4096]{0:T(1024)S(1)}, f32[4096]{0:T(1024)}, u32[]{:S(2)}) copy-start(f32[4096]{0:T(1024)} %param.6) | copy-start | bytes 49156
  0.0 16.1 %slice-start.1 = ((s8[27262976]{0:T(1024)(128)(4,1)}), s8[4194304]{0:T(1024)(128)(4,1)S(1)}, s32[]{:S(2)}) async-start(s8[27262976]{0:T(1024)(128)(4,1)} %bitcast.3), calls=%async_computation.1 | async-start | bytes 8388608
  0.0 16.1 %slice-start.2 = ((s8[27262976]{0:T(1024)(128)(4,1)}), s8[4194304]{0:T(1024)(128)(4,1)S(1)}, s32[]{:S(2)}) async-start(s8[27262976]{0:T(1024)(128)(4,1)} %bitcast.3), calls=%async_computation.2 | async-start | bytes 8388608
  0.0 16.1 %slice-start.3 = ((s8[27262976]{0:T(1024)(128)(4,1)}), s8[4194304]{0:T(1024)(128)(4,1)S(1)}, s32[]{:S(2)}) async-start(s8[27262976]{0:T(1024)(128)(4,1)} %bitcast.3), calls=%async_computation.3 | async-start | bytes 8388608
  0.0 16.1 %slice-start.4 = ((s8[27262976]{0:T(1024)(128)(4,1)}), s8[4194304]{0:T(1024)(128)(4,1)S(1)}, s32[]{:S(2)}) async-start(s8[27262976]{0:T(1024)(128)(4,1)} %bitcast.3), calls=%async_computation.4 | async-start | bytes 8388608
  0.0 16.1 %slice-start.5 = ((s8[27262976]{0:T(1024)(128)(4,1)}), s8[4194304]{0:T(1024)(128)(4,1)S(1)}, s32[]{:S(2)}) async-start(s8[27262976]{0:T(1024)(128)(4,1)} %bitcast.3), calls=%async_computation.5 | async-start | bytes 8388608
  0.1 16.1 %slice-start.6 = ((s8[27262976]{0:T(1024)(128)(4,1)}), s8[2097152]{0:T(1024)(128)(4,1)S(1)}, s32[]{:S(2)}) async-start(s8[27262976]{0:T(1024)(128)(4,1)} %bitcast.3), calls=%async_computation.6 | async-start | bytes 4194304
  0.1 19.8 %slice-start.7 = ((s8[27262976]{0:T(1024)(128)(4,1)}), s8[2097152]{0:T(1024)(128)(4,1)S(1)}, s32[]{:S(2)}) async-start(s8[27262976]{0:T(1024)(128)(4,1)} %bitcast.5), calls=%async_computation.7 | async-start | bytes 4194304
  0.1 19.8 %slice-start.8 = ((s8[27262976]{0:T(1024)(128)(4,1)}), s8[4194304]{0:T(1024)(128)(4,1)S(1)}, s32[]{:S(2)}) async-start(s8[27262976]{0:T(1024)(128)(4,1)} %bitcast.5), calls=%async_computation.8 | async-start | bytes 8388608
  0.1 19.8 %slice-start.9 = ((s8[27262976]{0:T(1024)(128)(4,1)}), s8[4194304]{0:T(1024)(128)(4,1)S(1)}, s32[]{:S(2)}) async-start(s8[27262976]{0:T(1024)(128)(4,1)} %bitcast.5), calls=%async_computation.9 | async-start | bytes 8388608
  0.1 19.8 %slice-start.10 = ((s8[27262976]{0:T(1024)(128)(4,1)}), s8[4194304]{0:T(1024)(128)(4,1)S(1)}, s32[]{:S(2)}) async-start(s8[27262976]{0:T(1024)(128)(4,1)} %bitcast.5), calls=%async_computation.10 | async-start | bytes 8388608
  0.1 19.8 %slice-start.11 = ((s8[27262976]{0:T(1024)(128)(4,1)}), s8[4194304]{0:T(1024)(128)(4,1)S(1)}, s32[]{:S(2)}) async-start(s8[27262976]{0:T(1024)(128)(4,1)} %bitcast.5), calls=%async_computation.11 | async-start | bytes 8388608
  0.1 19.8 %slice-start.12 = ((s8[27262976]{0:T(1024)(128)(4,1)}), s8[4194304]{0:T(1024)(128)(4,1)S(1)}, s32[]{:S(2)}) async-start(s8[27262976]{0:T(1024)(128)(4,1)} %bitcast.5), calls=%async_computation.12 | async-start | bytes 8388608
  0.9 1.4 %collective-permute-start = (f32[3,4096]{1,0:T(4,128)S(1)}, f32[3,4096]{1,0:T(4,128)S(1)}, u32[]{:S(2)}, u32[]{:S(2)}) collective-permute-start(f32[3,4096]{1,0:T(4,128)S(1)} %shard_map.57.refs_0_), channel_id=1, source_target_pairs={{0,1},{1,0},{2,3},{3,2},{4,5},{5,4},{6,7},{7,6},{8,9},{9,8},{10,11... | collective-permute-start | bytes 147464 | tf_op jit(solution)/shard_map/ppermute | solution.py:139
  2.5 5.2 %collective-permute-start.1 = (bf16[2,4096]{1,0:T(2,128)(2,1)S(1)}, bf16[2,4096]{1,0:T(2,128)(2,1)S(1)}, u32[]{:S(2)}, u32[]{:S(2)}) collective-permute-start(bf16[2,4096]{1,0:T(2,128)(2,1)S(1)} %get-tuple-element.19), channel_id=1, source_target_pairs={{0,9},{1,8},{2,11},{3,10},{4,13},{5,12},{6,15},{7,14},{8,1},{9,0},... | collective-permute-start | bytes 49160 | tf_op jit(solution)/shard_map/ppermute | solution.py:133
  7.7 4.0 %collective-permute-start.2 = (bf16[4,4096]{1,0:T(4,128)(2,1)S(1)}, bf16[4,4096]{1,0:T(4,128)(2,1)S(1)}, u32[]{:S(2)}, u32[]{:S(2)}) collective-permute-start(bf16[4,4096]{1,0:T(4,128)(2,1)S(1)} %shard_map.59.refs_0_), channel_id=1, source_target_pairs={{0,4},{2,6},{4,0},{6,2},{8,12},{10,14},{12,8},{14,10},{1,5},{3,7},... | collective-permute-start | bytes 98312 | tf_op jit(solution)/shard_map/ppermute | solution.py:139
  11.7 4.3 %collective-permute-start.3 = (bf16[8,4096]{1,0:T(8,128)(2,1)S(1)}, bf16[8,4096]{1,0:T(8,128)(2,1)S(1)}, u32[]{:S(2)}, u32[]{:S(2)}) collective-permute-start(bf16[8,4096]{1,0:T(8,128)(2,1)S(1)} %shard_map.60.refs_0_), channel_id=1, source_target_pairs={{0,2},{2,0},{4,6},{6,4},{8,10},{10,8},{12,14},{14,12},{1,3},{3,1},... | collective-permute-start | bytes 196616 | tf_op jit(solution)/shard_map/ppermute | solution.py:139
  16.1 3.8 %slice-start.13 = ((s8[27262976]{0:T(1024)(128)(4,1)}), s8[4194304]{0:T(1024)(128)(4,1)S(1)}, s32[]{:S(2)}) async-start(s8[27262976]{0:T(1024)(128)(4,1)} %bitcast.5), calls=%async_computation.13 | async-start | bytes 8388608
  19.8 5.7 %collective-permute-start.5 = (f32[16,3328]{1,0:T(8,128)S(1)}, f32[16,3328]{1,0:T(8,128)S(1)}, u32[]{:S(2)}, u32[]{:S(2)}) collective-permute-start(f32[16,3328]{1,0:T(8,128)S(1)} %get-tuple-element.22.refs_2_), channel_id=1, source_target_pairs={{0,1},{1,0},{2,3},{3,2},{4,5},{5,4},{6,7},{7,6},{8,9},{9,8},{10,11... | collective-permute-start | bytes 638984 | tf_op jit(solution)/shard_map/ppermute | solution.py:139
  24.0 1.5 %collective-permute-start.4 = (bf16[16,3328]{1,0:T(8,128)(2,1)S(1)}, bf16[16,3328]{1,0:T(8,128)(2,1)S(1)}, u32[]{:S(2)}, u32[]{:S(2)}) collective-permute-start(bf16[16,3328]{1,0:T(8,128)(2,1)S(1)} %get-tuple-element.21), channel_id=1, source_target_pairs={{0,1},{1,0},{2,3},{3,2},{4,5},{5,4},{6,7},{7,6},{8,9},{9,8},{10,11... | collective-permute-start | bytes 319496 | tf_op jit(solution)/shard_map/ppermute | solution.py:139
  30.4 4.4 %collective-permute-start.6 = (bf16[8,4096]{1,0:T(8,128)(2,1)S(1)}, bf16[8,4096]{1,0:T(8,128)(2,1)S(1)}, u32[]{:S(2)}, u32[]{:S(2)}) collective-permute-start(bf16[8,4096]{1,0:T(8,128)(2,1)S(1)} %get-tuple-element.26), channel_id=1, source_target_pairs={{0,2},{2,0},{4,6},{6,4},{8,10},{10,8},{12,14},{14,12},{1,3},{3,1},... | collective-permute-start | bytes 196616 | tf_op jit(solution)/shard_map/ppermute | solution.py:139
  34.9 4.0 %collective-permute-start.7 = (bf16[4,4096]{1,0:T(4,128)(2,1)S(1)}, bf16[4,4096]{1,0:T(4,128)(2,1)S(1)}, u32[]{:S(2)}, u32[]{:S(2)}) collective-permute-start(bf16[4,4096]{1,0:T(4,128)(2,1)S(1)} %get-tuple-element.28), channel_id=1, source_target_pairs={{0,4},{2,6},{4,0},{6,2},{8,12},{10,14},{12,8},{14,10},{1,5},{3,7},... | collective-permute-start | bytes 98312 | tf_op jit(solution)/shard_map/ppermute | solution.py:139
  38.9 4.7 %collective-permute-start.8 = (bf16[2,4096]{1,0:T(2,128)(2,1)S(1)}, bf16[2,4096]{1,0:T(2,128)(2,1)S(1)}, u32[]{:S(2)}, u32[]{:S(2)}) collective-permute-start(bf16[2,4096]{1,0:T(2,128)(2,1)S(1)} %get-tuple-element.30), channel_id=1, source_target_pairs={{0,8},{2,10},{4,12},{6,14},{8,0},{10,2},{12,4},{14,6},{1,9},{3,11}... | collective-permute-start | bytes 49160 | tf_op jit(solution)/shard_map/ppermute | solution.py:139

commit v8 on v7

--- a/solution.py
+++ b/solution.py
@@ -16,8 +16,8 @@
 
 PAD = (512, 1024)
 PADS = 96
-UP_SHARE, GATE_SHARE = 2, 5
-DOWN_LIMIT = 15
+UP_SHARE, GATE_SHARE = 2, 6
+DOWN_LIMIT = 13
 
 
 def call(kernel, outs, *args, pads=(), specs=None, scratch=(), limit=0, flops=0):

time: 44.4 us -> 44.4 us (level)
  transfers between devices with their start and end apart: 9 -> 9, of which waited for: 8 -> 8; matrix products, arithmetic and copies ran while one was open for 0% -> 0% of each run, Pallas kernels for 9% -> 10%
where the time goes in v8:
time: 44.4 us; the launch traced here: 44.2 us
  starting transfers between devices  15.3 us (34%)
  waiting for transfers between devices  14.4 us (32%)
  Pallas kernels  13.5 us (30%)
  local copies, waits for them, and re-layouts  0.77 us (2%)
    pallas_call x13, Pallas kernels, call(): pl.pallas_call(lambda *refs: kernel(*refs[skip:]), out_shape=outs, in_spe...  13.5 us
    ppermute x8, waiting for transfers between devices, swap(): return lax.ppermute(x, axis, [(i, i ^ mask) for i in range(size)])  12.9 us
    ppermute x8, starting transfers between devices, swap(): return lax.ppermute(x, axis, [(i, i ^ mask) for i in range(size)])  11.5 us
    ppermute x1, starting transfers between devices, cross(): lax.ppermute(x, ('gx', 'gy'), [(2 * i + c, 2 * (i ^ mask) + 1 - c) for i...  3.76 us
    ppermute x1, waiting for transfers between devices, cross(): lax.ppermute(x, ('gx', 'gy'), [(2 * i + c, 2 * (i ^ mask) + 1 - c) for i...  1.44 us
  transfers between devices with their start and end apart: 9, of which 8 were waited for; matrix products, arithmetic and copies ran while one was open for 0% of the time, Pallas kernels for 10%

profile of v8, /device:TPU:0, one launch (start us, length us, event | category | flops | bytes accessed | tf_op | source)
XLA Modules:
  0.0 44.2 jit_solution(4411058478862033976)
XLA Ops:
  0.1 0.0 slice-start.7
  0.1 0.0 slice-start.8
  0.1 0.0 slice-start.9
  0.1 0.0 slice-start.10
  0.1 0.0 slice-start.11
  0.1 0.0 slice-start.12
  0.1 0.1 shard_map.56.refs_0_
  0.2 0.7 %copy-done = bf16[2,1,4096]{2,0,1:T(2,128)(2,1)S(1)} copy-done((bf16[2,1,4096]{2,0,1:T(2,128)(2,1)S(1)}, bf16[2,1,4096]{2,0,1:T(2,128)(2,1)}, u32[]{:S(2)}) %copy-start) | copy-done | bytes 16408
  0.9 0.0 copy-done.1
  0.9 0.5 %collective-permute-start = (f32[3,4096]{1,0:T(4,128)S(1)}, f32[3,4096]{1,0:T(4,128)S(1)}, u32[]{:S(2)}, u32[]{:S(2)}) collective-permute-start(f32[3,4096]{1,0:T(4,128)S(1)} %shard_map.57.refs_0_), channel_id=1, source_target_pairs={{0,1},{1,0},{2,3},{3,2},{4,5},{5,4},{6,7},{7,6},{8,9},{9,8},{10,11... | collective-permute-start | bytes 147464 | tf_op jit(solution)/shard_map/ppermute | solution.py:139
  1.4 0.9 %collective-permute-done.refs_1_ = f32[3,4096]{1,0:T(4,128)S(1)} collective-permute-done((f32[3,4096]{1,0:T(4,128)S(1)}, f32[3,4096]{1,0:T(4,128)S(1)}, u32[]{:S(2)}, u32[]{:S(2)}) %collective-permute-start) | collective-permute-done | bytes 49184 | tf_op jit(solution)/shard_map/ppermute | solution.py:139
  2.3 0.2 shard_map.58
  2.5 3.8 %collective-permute-start.1 = (bf16[2,4096]{1,0:T(2,128)(2,1)S(1)}, bf16[2,4096]{1,0:T(2,128)(2,1)S(1)}, u32[]{:S(2)}, u32[]{:S(2)}) collective-permute-start(bf16[2,4096]{1,0:T(2,128)(2,1)S(1)} %get-tuple-element.19), channel_id=1, source_target_pairs={{0,9},{1,8},{2,11},{3,10},{4,13},{5,12},{6,15},{7,14},{8,1},{9,0},... | collective-permute-start | bytes 49160 | tf_op jit(solution)/shard_map/ppermute | solution.py:133
  6.2 1.4 %collective-permute-done.1.refs_1_ = bf16[2,4096]{1,0:T(2,128)(2,1)S(1)} collective-permute-done((bf16[2,4096]{1,0:T(2,128)(2,1)S(1)}, bf16[2,4096]{1,0:T(2,128)(2,1)S(1)}, u32[]{:S(2)}, u32[]{:S(2)}) %collective-permute-start.1) | collective-permute-done | bytes 16416 | tf_op jit(solution)/shard_map/ppermute | solution.py:133
  7.7 1.9 %collective-permute-start.2 = (bf16[4,4096]{1,0:T(4,128)(2,1)S(1)}, bf16[4,4096]{1,0:T(4,128)(2,1)S(1)}, u32[]{:S(2)}, u32[]{:S(2)}) collective-permute-start(bf16[4,4096]{1,0:T(4,128)(2,1)S(1)} %shard_map.59.refs_0_), channel_id=1, source_target_pairs={{0,4},{2,6},{4,0},{6,2},{8,12},{10,14},{12,8},{14,10},{1,5},{3,7},... | collective-permute-start | bytes 98312 | tf_op jit(solution)/shard_map/ppermute | solution.py:139
  9.6 2.1 %collective-permute-done.2.refs_1_ = bf16[4,4096]{1,0:T(4,128)(2,1)S(1)} collective-permute-done((bf16[4,4096]{1,0:T(4,128)(2,1)S(1)}, bf16[4,4096]{1,0:T(4,128)(2,1)S(1)}, u32[]{:S(2)}, u32[]{:S(2)}) %collective-permute-start.2) | collective-permute-done | bytes 32800 | tf_op jit(solution)/shard_map/ppermute | solution.py:139
  11.7 1.8 %collective-permute-start.3 = (bf16[8,4096]{1,0:T(8,128)(2,1)S(1)}, bf16[8,4096]{1,0:T(8,128)(2,1)S(1)}, u32[]{:S(2)}, u32[]{:S(2)}) collective-permute-start(bf16[8,4096]{1,0:T(8,128)(2,1)S(1)} %shard_map.60.refs_0_), channel_id=1, source_target_pairs={{0,2},{2,0},{4,6},{6,4},{8,10},{10,8},{12,14},{14,12},{1,3},{3,1},... | collective-permute-start | bytes 196616 | tf_op jit(solution)/shard_map/ppermute | solution.py:139
  13.5 2.5 %collective-permute-done.3.refs_1_ = bf16[8,4096]{1,0:T(8,128)(2,1)S(1)} collective-permute-done((bf16[8,4096]{1,0:T(8,128)(2,1)S(1)}, bf16[8,4096]{1,0:T(8,128)(2,1)S(1)}, u32[]{:S(2)}, u32[]{:S(2)}) %collective-permute-start.3) | collective-permute-done | bytes 65568 | tf_op jit(solution)/shard_map/ppermute | solution.py:139
  16.1 0.0 slice-start.13
  16.1 3.7 %shard_map.63 = (f32[16,3328]{1,0:T(8,128)S(1)}, bf16[512,4096]{1,0:T(8,128)(2,1)S(1)}) custom-call(bf16[16,4096]{1,0:T(8,128)(2,1)S(1)} %shard_map.61.refs_0_, bf16[4096,3328]{1,0:T(8,128)(2,1)S(1)} %bitcast.4, bf16[3328,4096]{1,0:T(8,128)(2,1)} %refs_4_.1), custom_call_target="tpu_custom_call" | custom-call | flops 436207616 | bytes 27262976 | tf_op jit(solution)/shard_map/pallas_call | solution.py:27
  19.8 0.1 collective-permute-start.5
  20.0 4.6 %shard_map.62 = (f32[16,3328]{1,0:T(8,128)S(1)}, bf16[16,3328]{1,0:T(8,128)(2,1)S(1)}, bf16[1536,4096]{1,0:T(8,128)(2,1)S(1)}) custom-call(bf16[16,4096]{1,0:T(8,128)(2,1)S(1)} %shard_map.61.refs_0_, bf16[4096,3328]{1,0:T(8,128)(2,1)S(1)} %bitcast.6, bf16[3328,4096]{1,0:T(8,128)(2,1)} %refs_4_.1), custom_call_target="tpu_custom_call" | custom-call | flops 436207616 | bytes 27262976 | tf_op jit(solution)/shard_map/pallas_call | solution.py:27
  24.6 0.5 %collective-permute-start.4 = (bf16[16,3328]{1,0:T(8,128)(2,1)S(1)}, bf16[16,3328]{1,0:T(8,128)(2,1)S(1)}, u32[]{:S(2)}, u32[]{:S(2)}) collective-permute-start(bf16[16,3328]{1,0:T(8,128)(2,1)S(1)} %get-tuple-element.21), channel_id=1, source_target_pairs={{0,1},{1,0},{2,3},{3,2},{4,5},{5,4},{6,7},{7,6},{8,9},{9,8},{10,11... | collective-permute-start | bytes 319496 | tf_op jit(solution)/shard_map/ppermute | solution.py:139
  25.1 1.0 %collective-permute-done.4.refs_1_ = bf16[16,3328]{1,0:T(8,128)(2,1)S(1)} collective-permute-done((bf16[16,3328]{1,0:T(8,128)(2,1)S(1)}, bf16[16,3328]{1,0:T(8,128)(2,1)S(1)}, u32[]{:S(2)}, u32[]{:S(2)}) %collective-permute-start.4) | collective-permute-done | bytes 106528 | tf_op jit(solution)/shard_map/ppermute | solution.py:139
  26.1 4.3 %shard_map.64 = (f32[8,4096]{1,0:T(8,128)S(1)}, bf16[8,4096]{1,0:T(8,128)(2,1)S(1)}) custom-call(f32[16,3328]{1,0:T(8,128)S(1)} %get-tuple-element.20.refs_0_, bf16[16,3328]{1,0:T(8,128)(2,1)S(1)} %collective-permute-done.4.refs_1_, f32[16,3328]{1,0:T(8,128)S(1)} %get-tuple-element.22.refs_2_, f32[16,3328]{1,0:T(8,128)S(1)} %collective-permute-done.5.refs_3_, ...), custom_call_target="tpu_custom_call" | custom-call | flops 436207616 | bytes 27262976 | tf_op jit(solution)/shard_map/pallas_call | solution.py:27
  30.4 1.8 %collective-permute-start.6 = (bf16[8,4096]{1,0:T(8,128)(2,1)S(1)}, bf16[8,4096]{1,0:T(8,128)(2,1)S(1)}, u32[]{:S(2)}, u32[]{:S(2)}) collective-permute-start(bf16[8,4096]{1,0:T(8,128)(2,1)S(1)} %get-tuple-element.26), channel_id=1, source_target_pairs={{0,2},{2,0},{4,6},{6,4},{8,10},{10,8},{12,14},{14,12},{1,3},{3,1},... | collective-permute-start | bytes 196616 | tf_op jit(solution)/shard_map/ppermute | solution.py:139
  32.3 2.6 %collective-permute-done.6.refs_1_ = bf16[8,4096]{1,0:T(8,128)(2,1)S(1)} collective-permute-done((bf16[8,4096]{1,0:T(8,128)(2,1)S(1)}, bf16[8,4096]{1,0:T(8,128)(2,1)S(1)}, u32[]{:S(2)}, u32[]{:S(2)}) %collective-permute-start.6) | collective-permute-done | bytes 65568 | tf_op jit(solution)/shard_map/ppermute | solution.py:139
  34.9 1.9 %collective-permute-start.7 = (bf16[4,4096]{1,0:T(4,128)(2,1)S(1)}, bf16[4,4096]{1,0:T(4,128)(2,1)S(1)}, u32[]{:S(2)}, u32[]{:S(2)}) collective-permute-start(bf16[4,4096]{1,0:T(4,128)(2,1)S(1)} %get-tuple-element.28), channel_id=1, source_target_pairs={{0,4},{2,6},{4,0},{6,2},{8,12},{10,14},{12,8},{14,10},{1,5},{3,7},... | collective-permute-start | bytes 98312 | tf_op jit(solution)/shard_map/ppermute | solution.py:139
  36.8 2.1 %collective-permute-done.7.refs_1_ = bf16[4,4096]{1,0:T(4,128)(2,1)S(1)} collective-permute-done((bf16[4,4096]{1,0:T(4,128)(2,1)S(1)}, bf16[4,4096]{1,0:T(4,128)(2,1)S(1)}, u32[]{:S(2)}, u32[]{:S(2)}) %collective-permute-start.7) | collective-permute-done | bytes 32800 | tf_op jit(solution)/shard_map/ppermute | solution.py:139
  38.9 2.9 %collective-permute-start.8 = (bf16[2,4096]{1,0:T(2,128)(2,1)S(1)}, bf16[2,4096]{1,0:T(2,128)(2,1)S(1)}, u32[]{:S(2)}, u32[]{:S(2)}) collective-permute-start(bf16[2,4096]{1,0:T(2,128)(2,1)S(1)} %get-tuple-element.30), channel_id=1, source_target_pairs={{0,8},{2,10},{4,12},{6,14},{8,0},{10,2},{12,4},{14,6},{1,9},{3,11}... | collective-permute-start | bytes 49160 | tf_op jit(solution)/shard_map/ppermute | solution.py:139
  41.8 1.8 %collective-permute-done.8.refs_1_ = bf16[2,4096]{1,0:T(2,128)(2,1)S(1)} collective-permute-done((bf16[2,4096]{1,0:T(2,128)(2,1)S(1)}, bf16[2,4096]{1,0:T(2,128)(2,1)S(1)}, u32[]{:S(2)}, u32[]{:S(2)}) %collective-permute-start.8) | collective-permute-done | bytes 16416 | tf_op jit(solution)/shard_map/ppermute | solution.py:139
  43.6 0.6 %shard_map.67 = bf16[2,4096]{1,0:T(2,128)(2,1)} custom-call(f32[2,4096]{1,0:T(2,128)S(1)} %get-tuple-element.29.refs_0_, bf16[2,4096]{1,0:T(2,128)(2,1)S(1)} %collective-permute-done.8.refs_1_), custom_call_target="tpu_custom_call" | custom-call | tf_op jit(solution)/shard_map/pallas_call | solution.py:27
  (33 shorter events, 0.1 us)
Async XLA Ops:
  0.0 16.1 %slice-start = ((s8[27262976]{0:T(1024)(128)(4,1)}), s8[4194304]{0:T(1024)(128)(4,1)S(1)}, s32[]{:S(2)}) async-start(s8[27262976]{0:T(1024)(128)(4,1)} %bitcast.3), calls=%async_computation | async-start | bytes 8388608
  0.0 0.9 %copy-start = (bf16[2,1,4096]{2,0,1:T(2,128)(2,1)S(1)}, bf16[2,1,4096]{2,0,1:T(2,128)(2,1)}, u32[]{:S(2)}) copy-start(bf16[2,1,4096]{2,0,1:T(2,128)(2,1)} %param.5) | copy-start | bytes 49156
  0.0 0.9 %copy-start.1 = (f32[4096]{0:T(1024)S(1)}, f32[4096]{0:T(1024)}, u32[]{:S(2)}) copy-start(f32[4096]{0:T(1024)} %param.6) | copy-start | bytes 49156
  0.0 16.1 %slice-start.1 = ((s8[27262976]{0:T(1024)(128)(4,1)}), s8[4194304]{0:T(1024)(128)(4,1)S(1)}, s32[]{:S(2)}) async-start(s8[27262976]{0:T(1024)(128)(4,1)} %bitcast.3), calls=%async_computation.1 | async-start | bytes 8388608
  0.0 16.1 %slice-start.2 = ((s8[27262976]{0:T(1024)(128)(4,1)}), s8[4194304]{0:T(1024)(128)(4,1)S(1)}, s32[]{:S(2)}) async-start(s8[27262976]{0:T(1024)(128)(4,1)} %bitcast.3), calls=%async_computation.2 | async-start | bytes 8388608
  0.0 16.1 %slice-start.3 = ((s8[27262976]{0:T(1024)(128)(4,1)}), s8[4194304]{0:T(1024)(128)(4,1)S(1)}, s32[]{:S(2)}) async-start(s8[27262976]{0:T(1024)(128)(4,1)} %bitcast.3), calls=%async_computation.3 | async-start | bytes 8388608
  0.0 16.1 %slice-start.4 = ((s8[27262976]{0:T(1024)(128)(4,1)}), s8[4194304]{0:T(1024)(128)(4,1)S(1)}, s32[]{:S(2)}) async-start(s8[27262976]{0:T(1024)(128)(4,1)} %bitcast.3), calls=%async_computation.4 | async-start | bytes 8388608
  0.0 16.1 %slice-start.5 = ((s8[27262976]{0:T(1024)(128)(4,1)}), s8[4194304]{0:T(1024)(128)(4,1)S(1)}, s32[]{:S(2)}) async-start(s8[27262976]{0:T(1024)(128)(4,1)} %bitcast.3), calls=%async_computation.5 | async-start | bytes 8388608
  0.1 16.1 %slice-start.6 = ((s8[27262976]{0:T(1024)(128)(4,1)}), s8[2097152]{0:T(1024)(128)(4,1)S(1)}, s32[]{:S(2)}) async-start(s8[27262976]{0:T(1024)(128)(4,1)} %bitcast.3), calls=%async_computation.6 | async-start | bytes 4194304
  0.1 19.8 %slice-start.7 = ((s8[27262976]{0:T(1024)(128)(4,1)}), s8[2097152]{0:T(1024)(128)(4,1)S(1)}, s32[]{:S(2)}) async-start(s8[27262976]{0:T(1024)(128)(4,1)} %bitcast.5), calls=%async_computation.7 | async-start | bytes 4194304
  0.1 19.8 %slice-start.8 = ((s8[27262976]{0:T(1024)(128)(4,1)}), s8[4194304]{0:T(1024)(128)(4,1)S(1)}, s32[]{:S(2)}) async-start(s8[27262976]{0:T(1024)(128)(4,1)} %bitcast.5), calls=%async_computation.8 | async-start | bytes 8388608
  0.1 19.8 %slice-start.9 = ((s8[27262976]{0:T(1024)(128)(4,1)}), s8[4194304]{0:T(1024)(128)(4,1)S(1)}, s32[]{:S(2)}) async-start(s8[27262976]{0:T(1024)(128)(4,1)} %bitcast.5), calls=%async_computation.9 | async-start | bytes 8388608
  0.1 19.8 %slice-start.10 = ((s8[27262976]{0:T(1024)(128)(4,1)}), s8[4194304]{0:T(1024)(128)(4,1)S(1)}, s32[]{:S(2)}) async-start(s8[27262976]{0:T(1024)(128)(4,1)} %bitcast.5), calls=%async_computation.10 | async-start | bytes 8388608
  0.1 19.8 %slice-start.11 = ((s8[27262976]{0:T(1024)(128)(4,1)}), s8[4194304]{0:T(1024)(128)(4,1)S(1)}, s32[]{:S(2)}) async-start(s8[27262976]{0:T(1024)(128)(4,1)} %bitcast.5), calls=%async_computation.11 | async-start | bytes 8388608
  0.1 19.8 %slice-start.12 = ((s8[27262976]{0:T(1024)(128)(4,1)}), s8[4194304]{0:T(1024)(128)(4,1)S(1)}, s32[]{:S(2)}) async-start(s8[27262976]{0:T(1024)(128)(4,1)} %bitcast.5), calls=%async_computation.12 | async-start | bytes 8388608
  0.9 1.4 %collective-permute-start = (f32[3,4096]{1,0:T(4,128)S(1)}, f32[3,4096]{1,0:T(4,128)S(1)}, u32[]{:S(2)}, u32[]{:S(2)}) collective-permute-start(f32[3,4096]{1,0:T(4,128)S(1)} %shard_map.57.refs_0_), channel_id=1, source_target_pairs={{0,1},{1,0},{2,3},{3,2},{4,5},{5,4},{6,7},{7,6},{8,9},{9,8},{10,11... | collective-permute-start | bytes 147464 | tf_op jit(solution)/shard_map/ppermute | solution.py:139
  2.5 5.2 %collective-permute-start.1 = (bf16[2,4096]{1,0:T(2,128)(2,1)S(1)}, bf16[2,4096]{1,0:T(2,128)(2,1)S(1)}, u32[]{:S(2)}, u32[]{:S(2)}) collective-permute-start(bf16[2,4096]{1,0:T(2,128)(2,1)S(1)} %get-tuple-element.19), channel_id=1, source_target_pairs={{0,9},{1,8},{2,11},{3,10},{4,13},{5,12},{6,15},{7,14},{8,1},{9,0},... | collective-permute-start | bytes 49160 | tf_op jit(solution)/shard_map/ppermute | solution.py:133
  7.7 4.0 %collective-permute-start.2 = (bf16[4,4096]{1,0:T(4,128)(2,1)S(1)}, bf16[4,4096]{1,0:T(4,128)(2,1)S(1)}, u32[]{:S(2)}, u32[]{:S(2)}) collective-permute-start(bf16[4,4096]{1,0:T(4,128)(2,1)S(1)} %shard_map.59.refs_0_), channel_id=1, source_target_pairs={{0,4},{2,6},{4,0},{6,2},{8,12},{10,14},{12,8},{14,10},{1,5},{3,7},... | collective-permute-start | bytes 98312 | tf_op jit(solution)/shard_map/ppermute | solution.py:139
  11.7 4.3 %collective-permute-start.3 = (bf16[8,4096]{1,0:T(8,128)(2,1)S(1)}, bf16[8,4096]{1,0:T(8,128)(2,1)S(1)}, u32[]{:S(2)}, u32[]{:S(2)}) collective-permute-start(bf16[8,4096]{1,0:T(8,128)(2,1)S(1)} %shard_map.60.refs_0_), channel_id=1, source_target_pairs={{0,2},{2,0},{4,6},{6,4},{8,10},{10,8},{12,14},{14,12},{1,3},{3,1},... | collective-permute-start | bytes 196616 | tf_op jit(solution)/shard_map/ppermute | solution.py:139
  16.1 3.8 %slice-start.13 = ((s8[27262976]{0:T(1024)(128)(4,1)}), s8[4194304]{0:T(1024)(128)(4,1)S(1)}, s32[]{:S(2)}) async-start(s8[27262976]{0:T(1024)(128)(4,1)} %bitcast.5), calls=%async_computation.13 | async-start | bytes 8388608
  19.8 6.3 %collective-permute-start.5 = (f32[16,3328]{1,0:T(8,128)S(1)}, f32[16,3328]{1,0:T(8,128)S(1)}, u32[]{:S(2)}, u32[]{:S(2)}) collective-permute-start(f32[16,3328]{1,0:T(8,128)S(1)} %get-tuple-element.22.refs_2_), channel_id=1, source_target_pairs={{0,1},{1,0},{2,3},{3,2},{4,5},{5,4},{6,7},{7,6},{8,9},{9,8},{10,11... | collective-permute-start | bytes 638984 | tf_op jit(solution)/shard_map/ppermute | solution.py:139
  24.6 1.5 %collective-permute-start.4 = (bf16[16,3328]{1,0:T(8,128)(2,1)S(1)}, bf16[16,3328]{1,0:T(8,128)(2,1)S(1)}, u32[]{:S(2)}, u32[]{:S(2)}) collective-permute-start(bf16[16,3328]{1,0:T(8,128)(2,1)S(1)} %get-tuple-element.21), channel_id=1, source_target_pairs={{0,1},{1,0},{2,3},{3,2},{4,5},{5,4},{6,7},{7,6},{8,9},{9,8},{10,11... | collective-permute-start | bytes 319496 | tf_op jit(solution)/shard_map/ppermute | solution.py:139
  30.4 4.4 %collective-permute-start.6 = (bf16[8,4096]{1,0:T(8,128)(2,1)S(1)}, bf16[8,4096]{1,0:T(8,128)(2,1)S(1)}, u32[]{:S(2)}, u32[]{:S(2)}) collective-permute-start(bf16[8,4096]{1,0:T(8,128)(2,1)S(1)} %get-tuple-element.26), channel_id=1, source_target_pairs={{0,2},{2,0},{4,6},{6,4},{8,10},{10,8},{12,14},{14,12},{1,3},{3,1},... | collective-permute-start | bytes 196616 | tf_op jit(solution)/shard_map/ppermute | solution.py:139
  34.9 4.0 %collective-permute-start.7 = (bf16[4,4096]{1,0:T(4,128)(2,1)S(1)}, bf16[4,4096]{1,0:T(4,128)(2,1)S(1)}, u32[]{:S(2)}, u32[]{:S(2)}) collective-permute-start(bf16[4,4096]{1,0:T(4,128)(2,1)S(1)} %get-tuple-element.28), channel_id=1, source_target_pairs={{0,4},{2,6},{4,0},{6,2},{8,12},{10,14},{12,8},{14,10},{1,5},{3,7},... | collective-permute-start | bytes 98312 | tf_op jit(solution)/shard_map/ppermute | solution.py:139
  38.9 4.7 %collective-permute-start.8 = (bf16[2,4096]{1,0:T(2,128)(2,1)S(1)}, bf16[2,4096]{1,0:T(2,128)(2,1)S(1)}, u32[]{:S(2)}, u32[]{:S(2)}) collective-permute-start(bf16[2,4096]{1,0:T(2,128)(2,1)S(1)} %get-tuple-element.30), channel_id=1, source_target_pairs={{0,8},{2,10},{4,12},{6,14},{8,0},{10,2},{12,4},{14,6},{1,9},{3,11}... | collective-permute-start | bytes 49160 | tf_op jit(solution)/shard_map/ppermute | solution.py:139

commit v9 on v8

--- a/solution.py
+++ b/solution.py
@@ -16,8 +16,8 @@
 
 PAD = (512, 1024)
 PADS = 96
-UP_SHARE, GATE_SHARE = 2, 6
-DOWN_LIMIT = 13
+UP_SHARE, GATE_SHARE = 4, 11
+DOWN_LIMIT = 14
 
 
 def call(kernel, outs, *args, pads=(), specs=None, scratch=(), limit=0, flops=0):
@@ -158,9 +158,9 @@
     for mask in reversed(masks[:-1]):
         held = call(join_kernel, Shape((2 * held.shape[0], half), bf16), held, swap(held, "gx", groups, mask))
     down_weight = pltpu.with_memory_space_constraint(down_weight, pltpu.HBM)
-    chunk = max(c for c in range(16, 257, 16) if units % c == 0)
+    chunk = max(c for c in range(16, 129, 16) if units % c == 0)
     count = units // chunk
-    counts = (count * UP_SHARE // 13, count * GATE_SHARE // 13)
+    counts = (count * UP_SHARE // 26, count * GATE_SHARE // 26)
     counts = (*counts, count - sum(counts))
 
     def project(weight, first, ahead, narrow=None):

time: 44.4 us -> 44.7 us (level)
  no operation moved by 1% of the time
where the time goes in v9:
time: 44.7 us; the launch traced here: 44.5 us
  starting transfers between devices  15.3 us (34%)
  waiting for transfers between devices  14.4 us (32%)
  Pallas kernels  13.8 us (31%)
  local copies, waits for them, and re-layouts  0.77 us (2%)
    pallas_call x13, Pallas kernels, call(): pl.pallas_call(lambda *refs: kernel(*refs[skip:]), out_shape=outs, in_spe...  13.8 us
    ppermute x8, waiting for transfers between devices, swap(): return lax.ppermute(x, axis, [(i, i ^ mask) for i in range(size)])  12.9 us
    ppermute x8, starting transfers between devices, swap(): return lax.ppermute(x, axis, [(i, i ^ mask) for i in range(size)])  11.5 us
    ppermute x1, starting transfers between devices, cross(): lax.ppermute(x, ('gx', 'gy'), [(2 * i + c, 2 * (i ^ mask) + 1 - c) for i...  3.76 us
    ppermute x1, waiting for transfers between devices, cross(): lax.ppermute(x, ('gx', 'gy'), [(2 * i + c, 2 * (i ^ mask) + 1 - c) for i...  1.44 us
  transfers between devices with their start and end apart: 9, of which 8 were waited for; matrix products, arithmetic and copies ran while one was open for 0% of the time, Pallas kernels for 10%

profile of v9, /device:TPU:0, one launch (start us, length us, event | category | flops | bytes accessed | tf_op | source)
XLA Modules:
  0.0 44.5 jit_solution(5995690009427785514)
XLA Ops:
  0.1 0.0 slice-start.7
  0.1 0.0 slice-start.8
  0.1 0.0 slice-start.9
  0.1 0.0 slice-start.10
  0.1 0.0 slice-start.11
  0.1 0.0 slice-start.12
  0.1 0.1 shard_map.56.refs_0_
  0.2 0.7 %copy-done = bf16[2,1,4096]{2,0,1:T(2,128)(2,1)S(1)} copy-done((bf16[2,1,4096]{2,0,1:T(2,128)(2,1)S(1)}, bf16[2,1,4096]{2,0,1:T(2,128)(2,1)}, u32[]{:S(2)}) %copy-start) | copy-done | bytes 16408
  0.9 0.0 copy-done.1
  0.9 0.5 %collective-permute-start = (f32[3,4096]{1,0:T(4,128)S(1)}, f32[3,4096]{1,0:T(4,128)S(1)}, u32[]{:S(2)}, u32[]{:S(2)}) collective-permute-start(f32[3,4096]{1,0:T(4,128)S(1)} %shard_map.57.refs_0_), channel_id=1, source_target_pairs={{0,1},{1,0},{2,3},{3,2},{4,5},{5,4},{6,7},{7,6},{8,9},{9,8},{10,11... | collective-permute-start | bytes 147464 | tf_op jit(solution)/shard_map/ppermute | solution.py:139
  1.4 0.9 %collective-permute-done.refs_1_ = f32[3,4096]{1,0:T(4,128)S(1)} collective-permute-done((f32[3,4096]{1,0:T(4,128)S(1)}, f32[3,4096]{1,0:T(4,128)S(1)}, u32[]{:S(2)}, u32[]{:S(2)}) %collective-permute-start) | collective-permute-done | bytes 49184 | tf_op jit(solution)/shard_map/ppermute | solution.py:139
  2.3 0.2 shard_map.58
  2.5 3.8 %collective-permute-start.1 = (bf16[2,4096]{1,0:T(2,128)(2,1)S(1)}, bf16[2,4096]{1,0:T(2,128)(2,1)S(1)}, u32[]{:S(2)}, u32[]{:S(2)}) collective-permute-start(bf16[2,4096]{1,0:T(2,128)(2,1)S(1)} %get-tuple-element.19), channel_id=1, source_target_pairs={{0,9},{1,8},{2,11},{3,10},{4,13},{5,12},{6,15},{7,14},{8,1},{9,0},... | collective-permute-start | bytes 49160 | tf_op jit(solution)/shard_map/ppermute | solution.py:133
  6.2 1.4 %collective-permute-done.1.refs_1_ = bf16[2,4096]{1,0:T(2,128)(2,1)S(1)} collective-permute-done((bf16[2,4096]{1,0:T(2,128)(2,1)S(1)}, bf16[2,4096]{1,0:T(2,128)(2,1)S(1)}, u32[]{:S(2)}, u32[]{:S(2)}) %collective-permute-start.1) | collective-permute-done | bytes 16416 | tf_op jit(solution)/shard_map/ppermute | solution.py:133
  7.7 1.9 %collective-permute-start.2 = (bf16[4,4096]{1,0:T(4,128)(2,1)S(1)}, bf16[4,4096]{1,0:T(4,128)(2,1)S(1)}, u32[]{:S(2)}, u32[]{:S(2)}) collective-permute-start(bf16[4,4096]{1,0:T(4,128)(2,1)S(1)} %shard_map.59.refs_0_), channel_id=1, source_target_pairs={{0,4},{2,6},{4,0},{6,2},{8,12},{10,14},{12,8},{14,10},{1,5},{3,7},... | collective-permute-start | bytes 98312 | tf_op jit(solution)/shard_map/ppermute | solution.py:139
  9.6 2.1 %collective-permute-done.2.refs_1_ = bf16[4,4096]{1,0:T(4,128)(2,1)S(1)} collective-permute-done((bf16[4,4096]{1,0:T(4,128)(2,1)S(1)}, bf16[4,4096]{1,0:T(4,128)(2,1)S(1)}, u32[]{:S(2)}, u32[]{:S(2)}) %collective-permute-start.2) | collective-permute-done | bytes 32800 | tf_op jit(solution)/shard_map/ppermute | solution.py:139
  11.7 1.8 %collective-permute-start.3 = (bf16[8,4096]{1,0:T(8,128)(2,1)S(1)}, bf16[8,4096]{1,0:T(8,128)(2,1)S(1)}, u32[]{:S(2)}, u32[]{:S(2)}) collective-permute-start(bf16[8,4096]{1,0:T(8,128)(2,1)S(1)} %shard_map.60.refs_0_), channel_id=1, source_target_pairs={{0,2},{2,0},{4,6},{6,4},{8,10},{10,8},{12,14},{14,12},{1,3},{3,1},... | collective-permute-start | bytes 196616 | tf_op jit(solution)/shard_map/ppermute | solution.py:139
  13.5 2.5 %collective-permute-done.3.refs_1_ = bf16[8,4096]{1,0:T(8,128)(2,1)S(1)} collective-permute-done((bf16[8,4096]{1,0:T(8,128)(2,1)S(1)}, bf16[8,4096]{1,0:T(8,128)(2,1)S(1)}, u32[]{:S(2)}, u32[]{:S(2)}) %collective-permute-start.3) | collective-permute-done | bytes 65568 | tf_op jit(solution)/shard_map/ppermute | solution.py:139
  16.1 0.0 slice-start.13
  16.1 3.7 %shard_map.63 = (f32[16,3328]{1,0:T(8,128)S(1)}, bf16[512,4096]{1,0:T(8,128)(2,1)S(1)}) custom-call(bf16[16,4096]{1,0:T(8,128)(2,1)S(1)} %shard_map.61.refs_0_, bf16[4096,3328]{1,0:T(8,128)(2,1)S(1)} %bitcast.4, bf16[3328,4096]{1,0:T(8,128)(2,1)} %refs_4_.1), custom_call_target="tpu_custom_call" | custom-call | flops 436207616 | bytes 27262976 | tf_op jit(solution)/shard_map/pallas_call | solution.py:27
  19.8 0.1 collective-permute-start.5
  20.0 4.3 %shard_map.62 = (f32[16,3328]{1,0:T(8,128)S(1)}, bf16[16,3328]{1,0:T(8,128)(2,1)S(1)}, bf16[1408,4096]{1,0:T(8,128)(2,1)S(1)}) custom-call(bf16[16,4096]{1,0:T(8,128)(2,1)S(1)} %shard_map.61.refs_0_, bf16[4096,3328]{1,0:T(8,128)(2,1)S(1)} %bitcast.6, bf16[3328,4096]{1,0:T(8,128)(2,1)} %refs_4_.1), custom_call_target="tpu_custom_call" | custom-call | flops 436207616 | bytes 27262976 | tf_op jit(solution)/shard_map/pallas_call | solution.py:27
  24.3 0.5 %collective-permute-start.4 = (bf16[16,3328]{1,0:T(8,128)(2,1)S(1)}, bf16[16,3328]{1,0:T(8,128)(2,1)S(1)}, u32[]{:S(2)}, u32[]{:S(2)}) collective-permute-start(bf16[16,3328]{1,0:T(8,128)(2,1)S(1)} %get-tuple-element.21), channel_id=1, source_target_pairs={{0,1},{1,0},{2,3},{3,2},{4,5},{5,4},{6,7},{7,6},{8,9},{9,8},{10,11... | collective-permute-start | bytes 319496 | tf_op jit(solution)/shard_map/ppermute | solution.py:139
  24.8 1.0 %collective-permute-done.4.refs_1_ = bf16[16,3328]{1,0:T(8,128)(2,1)S(1)} collective-permute-done((bf16[16,3328]{1,0:T(8,128)(2,1)S(1)}, bf16[16,3328]{1,0:T(8,128)(2,1)S(1)}, u32[]{:S(2)}, u32[]{:S(2)}) %collective-permute-start.4) | collective-permute-done | bytes 106528 | tf_op jit(solution)/shard_map/ppermute | solution.py:139
  25.8 4.9 %shard_map.64 = (f32[8,4096]{1,0:T(8,128)S(1)}, bf16[8,4096]{1,0:T(8,128)(2,1)S(1)}) custom-call(f32[16,3328]{1,0:T(8,128)S(1)} %get-tuple-element.20.refs_0_, bf16[16,3328]{1,0:T(8,128)(2,1)S(1)} %collective-permute-done.4.refs_1_, f32[16,3328]{1,0:T(8,128)S(1)} %get-tuple-element.22.refs_2_, f32[16,3328]{1,0:T(8,128)S(1)} %collective-permute-done.5.refs_3_, ...), custom_call_target="tpu_custom_call" | custom-call | flops 436207616 | bytes 27262976 | tf_op jit(solution)/shard_map/pallas_call | solution.py:27
  30.7 1.8 %collective-permute-start.6 = (bf16[8,4096]{1,0:T(8,128)(2,1)S(1)}, bf16[8,4096]{1,0:T(8,128)(2,1)S(1)}, u32[]{:S(2)}, u32[]{:S(2)}) collective-permute-start(bf16[8,4096]{1,0:T(8,128)(2,1)S(1)} %get-tuple-element.26), channel_id=1, source_target_pairs={{0,2},{2,0},{4,6},{6,4},{8,10},{10,8},{12,14},{14,12},{1,3},{3,1},... | collective-permute-start | bytes 196616 | tf_op jit(solution)/shard_map/ppermute | solution.py:139
  32.6 2.6 %collective-permute-done.6.refs_1_ = bf16[8,4096]{1,0:T(8,128)(2,1)S(1)} collective-permute-done((bf16[8,4096]{1,0:T(8,128)(2,1)S(1)}, bf16[8,4096]{1,0:T(8,128)(2,1)S(1)}, u32[]{:S(2)}, u32[]{:S(2)}) %collective-permute-start.6) | collective-permute-done | bytes 65568 | tf_op jit(solution)/shard_map/ppermute | solution.py:139
  35.2 1.9 %collective-permute-start.7 = (bf16[4,4096]{1,0:T(4,128)(2,1)S(1)}, bf16[4,4096]{1,0:T(4,128)(2,1)S(1)}, u32[]{:S(2)}, u32[]{:S(2)}) collective-permute-start(bf16[4,4096]{1,0:T(4,128)(2,1)S(1)} %get-tuple-element.28), channel_id=1, source_target_pairs={{0,4},{2,6},{4,0},{6,2},{8,12},{10,14},{12,8},{14,10},{1,5},{3,7},... | collective-permute-start | bytes 98312 | tf_op jit(solution)/shard_map/ppermute | solution.py:139
  37.1 2.1 %collective-permute-done.7.refs_1_ = bf16[4,4096]{1,0:T(4,128)(2,1)S(1)} collective-permute-done((bf16[4,4096]{1,0:T(4,128)(2,1)S(1)}, bf16[4,4096]{1,0:T(4,128)(2,1)S(1)}, u32[]{:S(2)}, u32[]{:S(2)}) %collective-permute-start.7) | collective-permute-done | bytes 32800 | tf_op jit(solution)/shard_map/ppermute | solution.py:139
  39.2 2.9 %collective-permute-start.8 = (bf16[2,4096]{1,0:T(2,128)(2,1)S(1)}, bf16[2,4096]{1,0:T(2,128)(2,1)S(1)}, u32[]{:S(2)}, u32[]{:S(2)}) collective-permute-start(bf16[2,4096]{1,0:T(2,128)(2,1)S(1)} %get-tuple-element.30), channel_id=1, source_target_pairs={{0,8},{2,10},{4,12},{6,14},{8,0},{10,2},{12,4},{14,6},{1,9},{3,11}... | collective-permute-start | bytes 49160 | tf_op jit(solution)/shard_map/ppermute | solution.py:139
  42.1 1.8 %collective-permute-done.8.refs_1_ = bf16[2,4096]{1,0:T(2,128)(2,1)S(1)} collective-permute-done((bf16[2,4096]{1,0:T(2,128)(2,1)S(1)}, bf16[2,4096]{1,0:T(2,128)(2,1)S(1)}, u32[]{:S(2)}, u32[]{:S(2)}) %collective-permute-start.8) | collective-permute-done | bytes 16416 | tf_op jit(solution)/shard_map/ppermute | solution.py:139
  43.9 0.6 %shard_map.67 = bf16[2,4096]{1,0:T(2,128)(2,1)} custom-call(f32[2,4096]{1,0:T(2,128)S(1)} %get-tuple-element.29.refs_0_, bf16[2,4096]{1,0:T(2,128)(2,1)S(1)} %collective-permute-done.8.refs_1_), custom_call_target="tpu_custom_call" | custom-call | tf_op jit(solution)/shard_map/pallas_call | solution.py:27
  (33 shorter events, 0.1 us)
Async XLA Ops:
  0.0 16.1 %slice-start = ((s8[27262976]{0:T(1024)(128)(4,1)}), s8[4194304]{0:T(1024)(128)(4,1)S(1)}, s32[]{:S(2)}) async-start(s8[27262976]{0:T(1024)(128)(4,1)} %bitcast.3), calls=%async_computation | async-start | bytes 8388608
  0.0 0.9 %copy-start = (bf16[2,1,4096]{2,0,1:T(2,128)(2,1)S(1)}, bf16[2,1,4096]{2,0,1:T(2,128)(2,1)}, u32[]{:S(2)}) copy-start(bf16[2,1,4096]{2,0,1:T(2,128)(2,1)} %param.5) | copy-start | bytes 49156
  0.0 0.9 %copy-start.1 = (f32[4096]{0:T(1024)S(1)}, f32[4096]{0:T(1024)}, u32[]{:S(2)}) copy-start(f32[4096]{0:T(1024)} %param.6) | copy-start | bytes 49156
  0.0 16.1 %slice-start.1 = ((s8[27262976]{0:T(1024)(128)(4,1)}), s8[4194304]{0:T(1024)(128)(4,1)S(1)}, s32[]{:S(2)}) async-start(s8[27262976]{0:T(1024)(128)(4,1)} %bitcast.3), calls=%async_computation.1 | async-start | bytes 8388608
  0.0 16.1 %slice-start.2 = ((s8[27262976]{0:T(1024)(128)(4,1)}), s8[4194304]{0:T(1024)(128)(4,1)S(1)}, s32[]{:S(2)}) async-start(s8[27262976]{0:T(1024)(128)(4,1)} %bitcast.3), calls=%async_computation.2 | async-start | bytes 8388608
  0.0 16.1 %slice-start.3 = ((s8[27262976]{0:T(1024)(128)(4,1)}), s8[4194304]{0:T(1024)(128)(4,1)S(1)}, s32[]{:S(2)}) async-start(s8[27262976]{0:T(1024)(128)(4,1)} %bitcast.3), calls=%async_computation.3 | async-start | bytes 8388608
  0.0 16.1 %slice-start.4 = ((s8[27262976]{0:T(1024)(128)(4,1)}), s8[4194304]{0:T(1024)(128)(4,1)S(1)}, s32[]{:S(2)}) async-start(s8[27262976]{0:T(1024)(128)(4,1)} %bitcast.3), calls=%async_computation.4 | async-start | bytes 8388608
  0.0 16.1 %slice-start.5 = ((s8[27262976]{0:T(1024)(128)(4,1)}), s8[4194304]{0:T(1024)(128)(4,1)S(1)}, s32[]{:S(2)}) async-start(s8[27262976]{0:T(1024)(128)(4,1)} %bitcast.3), calls=%async_computation.5 | async-start | bytes 8388608
  0.1 16.1 %slice-start.6 = ((s8[27262976]{0:T(1024)(128)(4,1)}), s8[2097152]{0:T(1024)(128)(4,1)S(1)}, s32[]{:S(2)}) async-start(s8[27262976]{0:T(1024)(128)(4,1)} %bitcast.3), calls=%async_computation.6 | async-start | bytes 4194304
  0.1 19.8 %slice-start.7 = ((s8[27262976]{0:T(1024)(128)(4,1)}), s8[2097152]{0:T(1024)(128)(4,1)S(1)}, s32[]{:S(2)}) async-start(s8[27262976]{0:T(1024)(128)(4,1)} %bitcast.5), calls=%async_computation.7 | async-start | bytes 4194304
  0.1 19.8 %slice-start.8 = ((s8[27262976]{0:T(1024)(128)(4,1)}), s8[4194304]{0:T(1024)(128)(4,1)S(1)}, s32[]{:S(2)}) async-start(s8[27262976]{0:T(1024)(128)(4,1)} %bitcast.5), calls=%async_computation.8 | async-start | bytes 8388608
  0.1 19.8 %slice-start.9 = ((s8[27262976]{0:T(1024)(128)(4,1)}), s8[4194304]{0:T(1024)(128)(4,1)S(1)}, s32[]{:S(2)}) async-start(s8[27262976]{0:T(1024)(128)(4,1)} %bitcast.5), calls=%async_computation.9 | async-start | bytes 8388608
  0.1 19.8 %slice-start.10 = ((s8[27262976]{0:T(1024)(128)(4,1)}), s8[4194304]{0:T(1024)(128)(4,1)S(1)}, s32[]{:S(2)}) async-start(s8[27262976]{0:T(1024)(128)(4,1)} %bitcast.5), calls=%async_computation.10 | async-start | bytes 8388608
  0.1 19.8 %slice-start.11 = ((s8[27262976]{0:T(1024)(128)(4,1)}), s8[4194304]{0:T(1024)(128)(4,1)S(1)}, s32[]{:S(2)}) async-start(s8[27262976]{0:T(1024)(128)(4,1)} %bitcast.5), calls=%async_computation.11 | async-start | bytes 8388608
  0.1 19.8 %slice-start.12 = ((s8[27262976]{0:T(1024)(128)(4,1)}), s8[4194304]{0:T(1024)(128)(4,1)S(1)}, s32[]{:S(2)}) async-start(s8[27262976]{0:T(1024)(128)(4,1)} %bitcast.5), calls=%async_computation.12 | async-start | bytes 8388608
  0.9 1.4 %collective-permute-start = (f32[3,4096]{1,0:T(4,128)S(1)}, f32[3,4096]{1,0:T(4,128)S(1)}, u32[]{:S(2)}, u32[]{:S(2)}) collective-permute-start(f32[3,4096]{1,0:T(4,128)S(1)} %shard_map.57.refs_0_), channel_id=1, source_target_pairs={{0,1},{1,0},{2,3},{3,2},{4,5},{5,4},{6,7},{7,6},{8,9},{9,8},{10,11... | collective-permute-start | bytes 147464 | tf_op jit(solution)/shard_map/ppermute | solution.py:139
  2.5 5.2 %collective-permute-start.1 = (bf16[2,4096]{1,0:T(2,128)(2,1)S(1)}, bf16[2,4096]{1,0:T(2,128)(2,1)S(1)}, u32[]{:S(2)}, u32[]{:S(2)}) collective-permute-start(bf16[2,4096]{1,0:T(2,128)(2,1)S(1)} %get-tuple-element.19), channel_id=1, source_target_pairs={{0,9},{1,8},{2,11},{3,10},{4,13},{5,12},{6,15},{7,14},{8,1},{9,0},... | collective-permute-start | bytes 49160 | tf_op jit(solution)/shard_map/ppermute | solution.py:133
  7.7 4.0 %collective-permute-start.2 = (bf16[4,4096]{1,0:T(4,128)(2,1)S(1)}, bf16[4,4096]{1,0:T(4,128)(2,1)S(1)}, u32[]{:S(2)}, u32[]{:S(2)}) collective-permute-start(bf16[4,4096]{1,0:T(4,128)(2,1)S(1)} %shard_map.59.refs_0_), channel_id=1, source_target_pairs={{0,4},{2,6},{4,0},{6,2},{8,12},{10,14},{12,8},{14,10},{1,5},{3,7},... | collective-permute-start | bytes 98312 | tf_op jit(solution)/shard_map/ppermute | solution.py:139
  11.7 4.3 %collective-permute-start.3 = (bf16[8,4096]{1,0:T(8,128)(2,1)S(1)}, bf16[8,4096]{1,0:T(8,128)(2,1)S(1)}, u32[]{:S(2)}, u32[]{:S(2)}) collective-permute-start(bf16[8,4096]{1,0:T(8,128)(2,1)S(1)} %shard_map.60.refs_0_), channel_id=1, source_target_pairs={{0,2},{2,0},{4,6},{6,4},{8,10},{10,8},{12,14},{14,12},{1,3},{3,1},... | collective-permute-start | bytes 196616 | tf_op jit(solution)/shard_map/ppermute | solution.py:139
  16.1 3.8 %slice-start.13 = ((s8[27262976]{0:T(1024)(128)(4,1)}), s8[4194304]{0:T(1024)(128)(4,1)S(1)}, s32[]{:S(2)}) async-start(s8[27262976]{0:T(1024)(128)(4,1)} %bitcast.5), calls=%async_computation.13 | async-start | bytes 8388608
  19.8 6.0 %collective-permute-start.5 = (f32[16,3328]{1,0:T(8,128)S(1)}, f32[16,3328]{1,0:T(8,128)S(1)}, u32[]{:S(2)}, u32[]{:S(2)}) collective-permute-start(f32[16,3328]{1,0:T(8,128)S(1)} %get-tuple-element.22.refs_2_), channel_id=1, source_target_pairs={{0,1},{1,0},{2,3},{3,2},{4,5},{5,4},{6,7},{7,6},{8,9},{9,8},{10,11... | collective-permute-start | bytes 638984 | tf_op jit(solution)/shard_map/ppermute | solution.py:139
  24.3 1.5 %collective-permute-start.4 = (bf16[16,3328]{1,0:T(8,128)(2,1)S(1)}, bf16[16,3328]{1,0:T(8,128)(2,1)S(1)}, u32[]{:S(2)}, u32[]{:S(2)}) collective-permute-start(bf16[16,3328]{1,0:T(8,128)(2,1)S(1)} %get-tuple-element.21), channel_id=1, source_target_pairs={{0,1},{1,0},{2,3},{3,2},{4,5},{5,4},{6,7},{7,6},{8,9},{9,8},{10,11... | collective-permute-start | bytes 319496 | tf_op jit(solution)/shard_map/ppermute | solution.py:139
  30.7 4.4 %collective-permute-start.6 = (bf16[8,4096]{1,0:T(8,128)(2,1)S(1)}, bf16[8,4096]{1,0:T(8,128)(2,1)S(1)}, u32[]{:S(2)}, u32[]{:S(2)}) collective-permute-start(bf16[8,4096]{1,0:T(8,128)(2,1)S(1)} %get-tuple-element.26), channel_id=1, source_target_pairs={{0,2},{2,0},{4,6},{6,4},{8,10},{10,8},{12,14},{14,12},{1,3},{3,1},... | collective-permute-start | bytes 196616 | tf_op jit(solution)/shard_map/ppermute | solution.py:139
  35.2 4.0 %collective-permute-start.7 = (bf16[4,4096]{1,0:T(4,128)(2,1)S(1)}, bf16[4,4096]{1,0:T(4,128)(2,1)S(1)}, u32[]{:S(2)}, u32[]{:S(2)}) collective-permute-start(bf16[4,4096]{1,0:T(4,128)(2,1)S(1)} %get-tuple-element.28), channel_id=1, source_target_pairs={{0,4},{2,6},{4,0},{6,2},{8,12},{10,14},{12,8},{14,10},{1,5},{3,7},... | collective-permute-start | bytes 98312 | tf_op jit(solution)/shard_map/ppermute | solution.py:139
  39.2 4.7 %collective-permute-start.8 = (bf16[2,4096]{1,0:T(2,128)(2,1)S(1)}, bf16[2,4096]{1,0:T(2,128)(2,1)S(1)}, u32[]{:S(2)}, u32[]{:S(2)}) collective-permute-start(bf16[2,4096]{1,0:T(2,128)(2,1)S(1)} %get-tuple-element.30), channel_id=1, source_target_pairs={{0,8},{2,10},{4,12},{6,14},{8,0},{10,2},{12,4},{14,6},{1,9},{3,11}... | collective-permute-start | bytes 49160 | tf_op jit(solution)/shard_map/ppermute | solution.py:139

commit v10 on v7

--- a/solution.py
+++ b/solution.py
@@ -146,6 +146,7 @@
     own_rows = steps * local
     rows = own_rows * groups
     masks = [1 << k for k in range(groups.bit_length() - 1)]
+    masks = [*masks[1:2], *masks[:1], *masks[2:]]
     x = tokens.reshape(own_rows, half)
 
     pads = (call(empty_kernel, Shape(PAD, f32)),) * PADS

time: 44.4 us -> 44.5 us (level)
  no operation moved by 1% of the time
where the time goes in v10:
time: 44.5 us; the launch traced here: 44.3 us
  starting transfers between devices  15.2 us (34%)
  waiting for transfers between devices  14.5 us (33%)
  Pallas kernels  13.5 us (30%)
  local copies, waits for them, and re-layouts  0.77 us (2%)
    pallas_call x13, Pallas kernels, call(): pl.pallas_call(lambda *refs: kernel(*refs[skip:]), out_shape=outs, in_spe...  13.5 us
    ppermute x8, waiting for transfers between devices, swap(): return lax.ppermute(x, axis, [(i, i ^ mask) for i in range(size)])  13.1 us
    ppermute x8, starting transfers between devices, swap(): return lax.ppermute(x, axis, [(i, i ^ mask) for i in range(size)])  11.4 us
    ppermute x1, starting transfers between devices, cross(): lax.ppermute(x, ('gx', 'gy'), [(2 * i + c, 2 * (i ^ mask) + 1 - c) for i...  3.76 us
    ppermute x1, waiting for transfers between devices, cross(): lax.ppermute(x, ('gx', 'gy'), [(2 * i + c, 2 * (i ^ mask) + 1 - c) for i...  1.44 us
  transfers between devices with their start and end apart: 9, of which 8 were waited for; matrix products, arithmetic and copies ran while one was open for 0% of the time, Pallas kernels for 9%

profile of v10, /device:TPU:0, one launch (start us, length us, event | category | flops | bytes accessed | tf_op | source)
XLA Modules:
  0.0 44.3 jit_solution(13445853913754485694)
XLA Ops:
  0.1 0.0 slice-start.7
  0.1 0.0 slice-start.8
  0.1 0.0 slice-start.9
  0.1 0.0 slice-start.10
  0.1 0.0 slice-start.11
  0.1 0.0 slice-start.12
  0.1 0.1 shard_map.56.refs_0_
  0.2 0.7 %copy-done = bf16[2,1,4096]{2,0,1:T(2,128)(2,1)S(1)} copy-done((bf16[2,1,4096]{2,0,1:T(2,128)(2,1)S(1)}, bf16[2,1,4096]{2,0,1:T(2,128)(2,1)}, u32[]{:S(2)}) %copy-start) | copy-done | bytes 16408
  0.9 0.0 copy-done.1
  0.9 0.5 %collective-permute-start = (f32[3,4096]{1,0:T(4,128)S(1)}, f32[3,4096]{1,0:T(4,128)S(1)}, u32[]{:S(2)}, u32[]{:S(2)}) collective-permute-start(f32[3,4096]{1,0:T(4,128)S(1)} %shard_map.57.refs_0_), channel_id=1, source_target_pairs={{0,1},{1,0},{2,3},{3,2},{4,5},{5,4},{6,7},{7,6},{8,9},{9,8},{10,11... | collective-permute-start | bytes 147464 | tf_op jit(solution)/shard_map/ppermute | solution.py:139
  1.4 0.9 %collective-permute-done.refs_1_ = f32[3,4096]{1,0:T(4,128)S(1)} collective-permute-done((f32[3,4096]{1,0:T(4,128)S(1)}, f32[3,4096]{1,0:T(4,128)S(1)}, u32[]{:S(2)}, u32[]{:S(2)}) %collective-permute-start) | collective-permute-done | bytes 49184 | tf_op jit(solution)/shard_map/ppermute | solution.py:139
  2.3 0.2 shard_map.58
  2.5 3.8 %collective-permute-start.1 = (bf16[2,4096]{1,0:T(2,128)(2,1)S(1)}, bf16[2,4096]{1,0:T(2,128)(2,1)S(1)}, u32[]{:S(2)}, u32[]{:S(2)}) collective-permute-start(bf16[2,4096]{1,0:T(2,128)(2,1)S(1)} %get-tuple-element.19), channel_id=1, source_target_pairs={{0,9},{1,8},{2,11},{3,10},{4,13},{5,12},{6,15},{7,14},{8,1},{9,0},... | collective-permute-start | bytes 49160 | tf_op jit(solution)/shard_map/ppermute | solution.py:133
  6.2 1.4 %collective-permute-done.1.refs_1_ = bf16[2,4096]{1,0:T(2,128)(2,1)S(1)} collective-permute-done((bf16[2,4096]{1,0:T(2,128)(2,1)S(1)}, bf16[2,4096]{1,0:T(2,128)(2,1)S(1)}, u32[]{:S(2)}, u32[]{:S(2)}) %collective-permute-start.1) | collective-permute-done | bytes 16416 | tf_op jit(solution)/shard_map/ppermute | solution.py:133
  7.7 1.8 %collective-permute-start.2 = (bf16[4,4096]{1,0:T(4,128)(2,1)S(1)}, bf16[4,4096]{1,0:T(4,128)(2,1)S(1)}, u32[]{:S(2)}, u32[]{:S(2)}) collective-permute-start(bf16[4,4096]{1,0:T(4,128)(2,1)S(1)} %shard_map.59.refs_0_), channel_id=1, source_target_pairs={{0,2},{2,0},{4,6},{6,4},{8,10},{10,8},{12,14},{14,12},{1,3},{3,1},... | collective-permute-start | bytes 98312 | tf_op jit(solution)/shard_map/ppermute | solution.py:139
  9.5 2.2 %collective-permute-done.2.refs_1_ = bf16[4,4096]{1,0:T(4,128)(2,1)S(1)} collective-permute-done((bf16[4,4096]{1,0:T(4,128)(2,1)S(1)}, bf16[4,4096]{1,0:T(4,128)(2,1)S(1)}, u32[]{:S(2)}, u32[]{:S(2)}) %collective-permute-start.2) | collective-permute-done | bytes 32800 | tf_op jit(solution)/shard_map/ppermute | solution.py:139
  11.7 1.9 %collective-permute-start.3 = (bf16[8,4096]{1,0:T(8,128)(2,1)S(1)}, bf16[8,4096]{1,0:T(8,128)(2,1)S(1)}, u32[]{:S(2)}, u32[]{:S(2)}) collective-permute-start(bf16[8,4096]{1,0:T(8,128)(2,1)S(1)} %shard_map.60.refs_0_), channel_id=1, source_target_pairs={{0,4},{2,6},{4,0},{6,2},{8,12},{10,14},{12,8},{14,10},{1,5},{3,7},... | collective-permute-start | bytes 196616 | tf_op jit(solution)/shard_map/ppermute | solution.py:139
  13.6 2.4 %collective-permute-done.3.refs_1_ = bf16[8,4096]{1,0:T(8,128)(2,1)S(1)} collective-permute-done((bf16[8,4096]{1,0:T(8,128)(2,1)S(1)}, bf16[8,4096]{1,0:T(8,128)(2,1)S(1)}, u32[]{:S(2)}, u32[]{:S(2)}) %collective-permute-start.3) | collective-permute-done | bytes 65568 | tf_op jit(solution)/shard_map/ppermute | solution.py:139
  16.1 0.0 slice-start.13
  16.1 3.7 %shard_map.63 = (f32[16,3328]{1,0:T(8,128)S(1)}, bf16[512,4096]{1,0:T(8,128)(2,1)S(1)}) custom-call(bf16[16,4096]{1,0:T(8,128)(2,1)S(1)} %shard_map.61.refs_0_, bf16[4096,3328]{1,0:T(8,128)(2,1)S(1)} %bitcast.4, bf16[3328,4096]{1,0:T(8,128)(2,1)} %refs_4_.1), custom_call_target="tpu_custom_call" | custom-call | flops 436207616 | bytes 27262976 | tf_op jit(solution)/shard_map/pallas_call | solution.py:27
  19.8 0.1 collective-permute-start.5
  20.0 4.0 %shard_map.62 = (f32[16,3328]{1,0:T(8,128)S(1)}, bf16[16,3328]{1,0:T(8,128)(2,1)S(1)}, bf16[1280,4096]{1,0:T(8,128)(2,1)S(1)}) custom-call(bf16[16,4096]{1,0:T(8,128)(2,1)S(1)} %shard_map.61.refs_0_, bf16[4096,3328]{1,0:T(8,128)(2,1)S(1)} %bitcast.6, bf16[3328,4096]{1,0:T(8,128)(2,1)} %refs_4_.1), custom_call_target="tpu_custom_call" | custom-call | flops 436207616 | bytes 27262976 | tf_op jit(solution)/shard_map/pallas_call | solution.py:27
  24.0 0.5 %collective-permute-start.4 = (bf16[16,3328]{1,0:T(8,128)(2,1)S(1)}, bf16[16,3328]{1,0:T(8,128)(2,1)S(1)}, u32[]{:S(2)}, u32[]{:S(2)}) collective-permute-start(bf16[16,3328]{1,0:T(8,128)(2,1)S(1)} %get-tuple-element.21), channel_id=1, source_target_pairs={{0,1},{1,0},{2,3},{3,2},{4,5},{5,4},{6,7},{7,6},{8,9},{9,8},{10,11... | collective-permute-start | bytes 319496 | tf_op jit(solution)/shard_map/ppermute | solution.py:139
  24.5 1.0 %collective-permute-done.4.refs_1_ = bf16[16,3328]{1,0:T(8,128)(2,1)S(1)} collective-permute-done((bf16[16,3328]{1,0:T(8,128)(2,1)S(1)}, bf16[16,3328]{1,0:T(8,128)(2,1)S(1)}, u32[]{:S(2)}, u32[]{:S(2)}) %collective-permute-start.4) | collective-permute-done | bytes 106528 | tf_op jit(solution)/shard_map/ppermute | solution.py:139
  25.5 4.9 %shard_map.64 = (f32[8,4096]{1,0:T(8,128)S(1)}, bf16[8,4096]{1,0:T(8,128)(2,1)S(1)}) custom-call(f32[16,3328]{1,0:T(8,128)S(1)} %get-tuple-element.20.refs_0_, bf16[16,3328]{1,0:T(8,128)(2,1)S(1)} %collective-permute-done.4.refs_1_, f32[16,3328]{1,0:T(8,128)S(1)} %get-tuple-element.22.refs_2_, f32[16,3328]{1,0:T(8,128)S(1)} %collective-permute-done.5.refs_3_, ...), custom_call_target="tpu_custom_call" | custom-call | flops 436207616 | bytes 27262976 | tf_op jit(solution)/shard_map/pallas_call | solution.py:27
  30.4 1.9 %collective-permute-start.6 = (bf16[8,4096]{1,0:T(8,128)(2,1)S(1)}, bf16[8,4096]{1,0:T(8,128)(2,1)S(1)}, u32[]{:S(2)}, u32[]{:S(2)}) collective-permute-start(bf16[8,4096]{1,0:T(8,128)(2,1)S(1)} %get-tuple-element.26), channel_id=1, source_target_pairs={{0,4},{2,6},{4,0},{6,2},{8,12},{10,14},{12,8},{14,10},{1,5},{3,7},... | collective-permute-start | bytes 196616 | tf_op jit(solution)/shard_map/ppermute | solution.py:139
  32.3 2.6 %collective-permute-done.6.refs_1_ = bf16[8,4096]{1,0:T(8,128)(2,1)S(1)} collective-permute-done((bf16[8,4096]{1,0:T(8,128)(2,1)S(1)}, bf16[8,4096]{1,0:T(8,128)(2,1)S(1)}, u32[]{:S(2)}, u32[]{:S(2)}) %collective-permute-start.6) | collective-permute-done | bytes 65568 | tf_op jit(solution)/shard_map/ppermute | solution.py:139
  35.0 1.7 %collective-permute-start.7 = (bf16[4,4096]{1,0:T(4,128)(2,1)S(1)}, bf16[4,4096]{1,0:T(4,128)(2,1)S(1)}, u32[]{:S(2)}, u32[]{:S(2)}) collective-permute-start(bf16[4,4096]{1,0:T(4,128)(2,1)S(1)} %get-tuple-element.28), channel_id=1, source_target_pairs={{0,2},{2,0},{4,6},{6,4},{8,10},{10,8},{12,14},{14,12},{1,3},{3,1},... | collective-permute-start | bytes 98312 | tf_op jit(solution)/shard_map/ppermute | solution.py:139
  36.7 2.3 %collective-permute-done.7.refs_1_ = bf16[4,4096]{1,0:T(4,128)(2,1)S(1)} collective-permute-done((bf16[4,4096]{1,0:T(4,128)(2,1)S(1)}, bf16[4,4096]{1,0:T(4,128)(2,1)S(1)}, u32[]{:S(2)}, u32[]{:S(2)}) %collective-permute-start.7) | collective-permute-done | bytes 32800 | tf_op jit(solution)/shard_map/ppermute | solution.py:139
  39.0 2.9 %collective-permute-start.8 = (bf16[2,4096]{1,0:T(2,128)(2,1)S(1)}, bf16[2,4096]{1,0:T(2,128)(2,1)S(1)}, u32[]{:S(2)}, u32[]{:S(2)}) collective-permute-start(bf16[2,4096]{1,0:T(2,128)(2,1)S(1)} %get-tuple-element.30), channel_id=1, source_target_pairs={{0,8},{2,10},{4,12},{6,14},{8,0},{10,2},{12,4},{14,6},{1,9},{3,11}... | collective-permute-start | bytes 49160 | tf_op jit(solution)/shard_map/ppermute | solution.py:139
  41.9 1.8 %collective-permute-done.8.refs_1_ = bf16[2,4096]{1,0:T(2,128)(2,1)S(1)} collective-permute-done((bf16[2,4096]{1,0:T(2,128)(2,1)S(1)}, bf16[2,4096]{1,0:T(2,128)(2,1)S(1)}, u32[]{:S(2)}, u32[]{:S(2)}) %collective-permute-start.8) | collective-permute-done | bytes 16416 | tf_op jit(solution)/shard_map/ppermute | solution.py:139
  43.7 0.6 %shard_map.67 = bf16[2,4096]{1,0:T(2,128)(2,1)} custom-call(f32[2,4096]{1,0:T(2,128)S(1)} %get-tuple-element.29.refs_0_, bf16[2,4096]{1,0:T(2,128)(2,1)S(1)} %collective-permute-done.8.refs_1_), custom_call_target="tpu_custom_call" | custom-call | tf_op jit(solution)/shard_map/pallas_call | solution.py:27
  (33 shorter events, 0.1 us)
Async XLA Ops:
  0.0 16.1 %slice-start = ((s8[27262976]{0:T(1024)(128)(4,1)}), s8[4194304]{0:T(1024)(128)(4,1)S(1)}, s32[]{:S(2)}) async-start(s8[27262976]{0:T(1024)(128)(4,1)} %bitcast.3), calls=%async_computation | async-start | bytes 8388608
  0.0 0.9 %copy-start = (bf16[2,1,4096]{2,0,1:T(2,128)(2,1)S(1)}, bf16[2,1,4096]{2,0,1:T(2,128)(2,1)}, u32[]{:S(2)}) copy-start(bf16[2,1,4096]{2,0,1:T(2,128)(2,1)} %param.5) | copy-start | bytes 49156
  0.0 0.9 %copy-start.1 = (f32[4096]{0:T(1024)S(1)}, f32[4096]{0:T(1024)}, u32[]{:S(2)}) copy-start(f32[4096]{0:T(1024)} %param.6) | copy-start | bytes 49156
  0.0 16.1 %slice-start.1 = ((s8[27262976]{0:T(1024)(128)(4,1)}), s8[4194304]{0:T(1024)(128)(4,1)S(1)}, s32[]{:S(2)}) async-start(s8[27262976]{0:T(1024)(128)(4,1)} %bitcast.3), calls=%async_computation.1 | async-start | bytes 8388608
  0.0 16.1 %slice-start.2 = ((s8[27262976]{0:T(1024)(128)(4,1)}), s8[4194304]{0:T(1024)(128)(4,1)S(1)}, s32[]{:S(2)}) async-start(s8[27262976]{0:T(1024)(128)(4,1)} %bitcast.3), calls=%async_computation.2 | async-start | bytes 8388608
  0.0 16.1 %slice-start.3 = ((s8[27262976]{0:T(1024)(128)(4,1)}), s8[4194304]{0:T(1024)(128)(4,1)S(1)}, s32[]{:S(2)}) async-start(s8[27262976]{0:T(1024)(128)(4,1)} %bitcast.3), calls=%async_computation.3 | async-start | bytes 8388608
  0.0 16.1 %slice-start.4 = ((s8[27262976]{0:T(1024)(128)(4,1)}), s8[4194304]{0:T(1024)(128)(4,1)S(1)}, s32[]{:S(2)}) async-start(s8[27262976]{0:T(1024)(128)(4,1)} %bitcast.3), calls=%async_computation.4 | async-start | bytes 8388608
  0.0 16.1 %slice-start.5 = ((s8[27262976]{0:T(1024)(128)(4,1)}), s8[4194304]{0:T(1024)(128)(4,1)S(1)}, s32[]{:S(2)}) async-start(s8[27262976]{0:T(1024)(128)(4,1)} %bitcast.3), calls=%async_computation.5 | async-start | bytes 8388608
  0.1 16.1 %slice-start.6 = ((s8[27262976]{0:T(1024)(128)(4,1)}), s8[2097152]{0:T(1024)(128)(4,1)S(1)}, s32[]{:S(2)}) async-start(s8[27262976]{0:T(1024)(128)(4,1)} %bitcast.3), calls=%async_computation.6 | async-start | bytes 4194304
  0.1 19.8 %slice-start.7 = ((s8[27262976]{0:T(1024)(128)(4,1)}), s8[2097152]{0:T(1024)(128)(4,1)S(1)}, s32[]{:S(2)}) async-start(s8[27262976]{0:T(1024)(128)(4,1)} %bitcast.5), calls=%async_computation.7 | async-start | bytes 4194304
  0.1 19.8 %slice-start.8 = ((s8[27262976]{0:T(1024)(128)(4,1)}), s8[4194304]{0:T(1024)(128)(4,1)S(1)}, s32[]{:S(2)}) async-start(s8[27262976]{0:T(1024)(128)(4,1)} %bitcast.5), calls=%async_computation.8 | async-start | bytes 8388608
  0.1 19.8 %slice-start.9 = ((s8[27262976]{0:T(1024)(128)(4,1)}), s8[4194304]{0:T(1024)(128)(4,1)S(1)}, s32[]{:S(2)}) async-start(s8[27262976]{0:T(1024)(128)(4,1)} %bitcast.5), calls=%async_computation.9 | async-start | bytes 8388608
  0.1 19.8 %slice-start.10 = ((s8[27262976]{0:T(1024)(128)(4,1)}), s8[4194304]{0:T(1024)(128)(4,1)S(1)}, s32[]{:S(2)}) async-start(s8[27262976]{0:T(1024)(128)(4,1)} %bitcast.5), calls=%async_computation.10 | async-start | bytes 8388608
  0.1 19.8 %slice-start.11 = ((s8[27262976]{0:T(1024)(128)(4,1)}), s8[4194304]{0:T(1024)(128)(4,1)S(1)}, s32[]{:S(2)}) async-start(s8[27262976]{0:T(1024)(128)(4,1)} %bitcast.5), calls=%async_computation.11 | async-start | bytes 8388608
  0.1 19.8 %slice-start.12 = ((s8[27262976]{0:T(1024)(128)(4,1)}), s8[4194304]{0:T(1024)(128)(4,1)S(1)}, s32[]{:S(2)}) async-start(s8[27262976]{0:T(1024)(128)(4,1)} %bitcast.5), calls=%async_computation.12 | async-start | bytes 8388608
  0.9 1.4 %collective-permute-start = (f32[3,4096]{1,0:T(4,128)S(1)}, f32[3,4096]{1,0:T(4,128)S(1)}, u32[]{:S(2)}, u32[]{:S(2)}) collective-permute-start(f32[3,4096]{1,0:T(4,128)S(1)} %shard_map.57.refs_0_), channel_id=1, source_target_pairs={{0,1},{1,0},{2,3},{3,2},{4,5},{5,4},{6,7},{7,6},{8,9},{9,8},{10,11... | collective-permute-start | bytes 147464 | tf_op jit(solution)/shard_map/ppermute | solution.py:139
  2.5 5.2 %collective-permute-start.1 = (bf16[2,4096]{1,0:T(2,128)(2,1)S(1)}, bf16[2,4096]{1,0:T(2,128)(2,1)S(1)}, u32[]{:S(2)}, u32[]{:S(2)}) collective-permute-start(bf16[2,4096]{1,0:T(2,128)(2,1)S(1)} %get-tuple-element.19), channel_id=1, source_target_pairs={{0,9},{1,8},{2,11},{3,10},{4,13},{5,12},{6,15},{7,14},{8,1},{9,0},... | collective-permute-start | bytes 49160 | tf_op jit(solution)/shard_map/ppermute | solution.py:133
  7.7 4.0 %collective-permute-start.2 = (bf16[4,4096]{1,0:T(4,128)(2,1)S(1)}, bf16[4,4096]{1,0:T(4,128)(2,1)S(1)}, u32[]{:S(2)}, u32[]{:S(2)}) collective-permute-start(bf16[4,4096]{1,0:T(4,128)(2,1)S(1)} %shard_map.59.refs_0_), channel_id=1, source_target_pairs={{0,2},{2,0},{4,6},{6,4},{8,10},{10,8},{12,14},{14,12},{1,3},{3,1},... | collective-permute-start | bytes 98312 | tf_op jit(solution)/shard_map/ppermute | solution.py:139
  11.7 4.3 %collective-permute-start.3 = (bf16[8,4096]{1,0:T(8,128)(2,1)S(1)}, bf16[8,4096]{1,0:T(8,128)(2,1)S(1)}, u32[]{:S(2)}, u32[]{:S(2)}) collective-permute-start(bf16[8,4096]{1,0:T(8,128)(2,1)S(1)} %shard_map.60.refs_0_), channel_id=1, source_target_pairs={{0,4},{2,6},{4,0},{6,2},{8,12},{10,14},{12,8},{14,10},{1,5},{3,7},... | collective-permute-start | bytes 196616 | tf_op jit(solution)/shard_map/ppermute | solution.py:139
  16.1 3.8 %slice-start.13 = ((s8[27262976]{0:T(1024)(128)(4,1)}), s8[4194304]{0:T(1024)(128)(4,1)S(1)}, s32[]{:S(2)}) async-start(s8[27262976]{0:T(1024)(128)(4,1)} %bitcast.5), calls=%async_computation.13 | async-start | bytes 8388608
  19.8 5.7 %collective-permute-start.5 = (f32[16,3328]{1,0:T(8,128)S(1)}, f32[16,3328]{1,0:T(8,128)S(1)}, u32[]{:S(2)}, u32[]{:S(2)}) collective-permute-start(f32[16,3328]{1,0:T(8,128)S(1)} %get-tuple-element.22.refs_2_), channel_id=1, source_target_pairs={{0,1},{1,0},{2,3},{3,2},{4,5},{5,4},{6,7},{7,6},{8,9},{9,8},{10,11... | collective-permute-start | bytes 638984 | tf_op jit(solution)/shard_map/ppermute | solution.py:139
  24.0 1.5 %collective-permute-start.4 = (bf16[16,3328]{1,0:T(8,128)(2,1)S(1)}, bf16[16,3328]{1,0:T(8,128)(2,1)S(1)}, u32[]{:S(2)}, u32[]{:S(2)}) collective-permute-start(bf16[16,3328]{1,0:T(8,128)(2,1)S(1)} %get-tuple-element.21), channel_id=1, source_target_pairs={{0,1},{1,0},{2,3},{3,2},{4,5},{5,4},{6,7},{7,6},{8,9},{9,8},{10,11... | collective-permute-start | bytes 319496 | tf_op jit(solution)/shard_map/ppermute | solution.py:139
  30.4 4.5 %collective-permute-start.6 = (bf16[8,4096]{1,0:T(8,128)(2,1)S(1)}, bf16[8,4096]{1,0:T(8,128)(2,1)S(1)}, u32[]{:S(2)}, u32[]{:S(2)}) collective-permute-start(bf16[8,4096]{1,0:T(8,128)(2,1)S(1)} %get-tuple-element.26), channel_id=1, source_target_pairs={{0,4},{2,6},{4,0},{6,2},{8,12},{10,14},{12,8},{14,10},{1,5},{3,7},... | collective-permute-start | bytes 196616 | tf_op jit(solution)/shard_map/ppermute | solution.py:139
  35.0 4.0 %collective-permute-start.7 = (bf16[4,4096]{1,0:T(4,128)(2,1)S(1)}, bf16[4,4096]{1,0:T(4,128)(2,1)S(1)}, u32[]{:S(2)}, u32[]{:S(2)}) collective-permute-start(bf16[4,4096]{1,0:T(4,128)(2,1)S(1)} %get-tuple-element.28), channel_id=1, source_target_pairs={{0,2},{2,0},{4,6},{6,4},{8,10},{10,8},{12,14},{14,12},{1,3},{3,1},... | collective-permute-start | bytes 98312 | tf_op jit(solution)/shard_map/ppermute | solution.py:139
  39.0 4.7 %collective-permute-start.8 = (bf16[2,4096]{1,0:T(2,128)(2,1)S(1)}, bf16[2,4096]{1,0:T(2,128)(2,1)S(1)}, u32[]{:S(2)}, u32[]{:S(2)}) collective-permute-start(bf16[2,4096]{1,0:T(2,128)(2,1)S(1)} %get-tuple-element.30), channel_id=1, source_target_pairs={{0,8},{2,10},{4,12},{6,14},{8,0},{10,2},{12,4},{14,6},{1,9},{3,11}... | collective-permute-start | bytes 49160 | tf_op jit(solution)/shard_map/ppermute | solution.py:139

commit v11 on v7

--- a/solution.py
+++ b/solution.py
@@ -106,16 +106,16 @@
     for k, (copy, parts) in enumerate(passes):
         if copy is not None:
             copy.wait()
-        for c in range(0, width, 512):
-            total = acc_ref[:, c : c + 512] if k else None
+        for c in range(0, width, 1024):
+            total = acc_ref[:, c : c + 1024] if k else None
             for ref, at, a, b in parts:
-                part = jnp.dot(h_ref[:, a:b], ref[at : at + b - a, c : c + 512], preferred_element_type=f32)
+                part = jnp.dot(h_ref[:, a:b], ref[at : at + b - a, c : c + 1024], preferred_element_type=f32)
                 total = part if total is None else total + part
             if k < len(passes) - 1:
-                acc_ref[:, c : c + 512] = total
+                acc_ref[:, c : c + 1024] = total
             else:
-                keep_ref[:, c : c + 512] = total[:rows]
-                send_ref[:, c : c + 512] = total[rows:].astype(send_ref.dtype)
+                keep_ref[:, c : c + 1024] = total[:rows]
+                send_ref[:, c : c + 1024] = total[rows:].astype(send_ref.dtype)
 
 
 def add_kernel(a_ref, b_ref, keep_ref, send_ref):

time: 44.4 us -> 44.4 us (level)
  no operation moved by 1% of the time
where the time goes in v11:
time: 44.4 us; the launch traced here: 44.3 us
  starting transfers between devices  15.3 us (34%)
  waiting for transfers between devices  14.4 us (32%)
  Pallas kernels  13.6 us (31%)
  local copies, waits for them, and re-layouts  0.77 us (2%)
    pallas_call x13, Pallas kernels, call(): pl.pallas_call(lambda *refs: kernel(*refs[skip:]), out_shape=outs, in_spe...  13.6 us
    ppermute x8, waiting for transfers between devices, swap(): return lax.ppermute(x, axis, [(i, i ^ mask) for i in range(size)])  12.9 us
    ppermute x8, starting transfers between devices, swap(): return lax.ppermute(x, axis, [(i, i ^ mask) for i in range(size)])  11.5 us
    ppermute x1, starting transfers between devices, cross(): lax.ppermute(x, ('gx', 'gy'), [(2 * i + c, 2 * (i ^ mask) + 1 - c) for i...  3.76 us
    ppermute x1, waiting for transfers between devices, cross(): lax.ppermute(x, ('gx', 'gy'), [(2 * i + c, 2 * (i ^ mask) + 1 - c) for i...  1.44 us
  transfers between devices with their start and end apart: 9, of which 8 were waited for; matrix products, arithmetic and copies ran while one was open for 0% of the time, Pallas kernels for 9%

profile of v11, /device:TPU:0, one launch (start us, length us, event | category | flops | bytes accessed | tf_op | source)
XLA Modules:
  0.0 44.3 jit_solution(10146885461831134464)
XLA Ops:
  0.1 0.0 slice-start.7
  0.1 0.0 slice-start.8
  0.1 0.0 slice-start.9
  0.1 0.0 slice-start.10
  0.1 0.0 slice-start.11
  0.1 0.0 slice-start.12
  0.1 0.1 shard_map.56.refs_0_
  0.2 0.7 %copy-done = bf16[2,1,4096]{2,0,1:T(2,128)(2,1)S(1)} copy-done((bf16[2,1,4096]{2,0,1:T(2,128)(2,1)S(1)}, bf16[2,1,4096]{2,0,1:T(2,128)(2,1)}, u32[]{:S(2)}) %copy-start) | copy-done | bytes 16408
  0.9 0.0 copy-done.1
  0.9 0.5 %collective-permute-start = (f32[3,4096]{1,0:T(4,128)S(1)}, f32[3,4096]{1,0:T(4,128)S(1)}, u32[]{:S(2)}, u32[]{:S(2)}) collective-permute-start(f32[3,4096]{1,0:T(4,128)S(1)} %shard_map.57.refs_0_), channel_id=1, source_target_pairs={{0,1},{1,0},{2,3},{3,2},{4,5},{5,4},{6,7},{7,6},{8,9},{9,8},{10,11... | collective-permute-start | bytes 147464 | tf_op jit(solution)/shard_map/ppermute | solution.py:139
  1.4 0.9 %collective-permute-done.refs_1_ = f32[3,4096]{1,0:T(4,128)S(1)} collective-permute-done((f32[3,4096]{1,0:T(4,128)S(1)}, f32[3,4096]{1,0:T(4,128)S(1)}, u32[]{:S(2)}, u32[]{:S(2)}) %collective-permute-start) | collective-permute-done | bytes 49184 | tf_op jit(solution)/shard_map/ppermute | solution.py:139
  2.3 0.2 shard_map.58
  2.5 3.8 %collective-permute-start.1 = (bf16[2,4096]{1,0:T(2,128)(2,1)S(1)}, bf16[2,4096]{1,0:T(2,128)(2,1)S(1)}, u32[]{:S(2)}, u32[]{:S(2)}) collective-permute-start(bf16[2,4096]{1,0:T(2,128)(2,1)S(1)} %get-tuple-element.19), channel_id=1, source_target_pairs={{0,9},{1,8},{2,11},{3,10},{4,13},{5,12},{6,15},{7,14},{8,1},{9,0},... | collective-permute-start | bytes 49160 | tf_op jit(solution)/shard_map/ppermute | solution.py:133
  6.2 1.4 %collective-permute-done.1.refs_1_ = bf16[2,4096]{1,0:T(2,128)(2,1)S(1)} collective-permute-done((bf16[2,4096]{1,0:T(2,128)(2,1)S(1)}, bf16[2,4096]{1,0:T(2,128)(2,1)S(1)}, u32[]{:S(2)}, u32[]{:S(2)}) %collective-permute-start.1) | collective-permute-done | bytes 16416 | tf_op jit(solution)/shard_map/ppermute | solution.py:133
  7.7 1.9 %collective-permute-start.2 = (bf16[4,4096]{1,0:T(4,128)(2,1)S(1)}, bf16[4,4096]{1,0:T(4,128)(2,1)S(1)}, u32[]{:S(2)}, u32[]{:S(2)}) collective-permute-start(bf16[4,4096]{1,0:T(4,128)(2,1)S(1)} %shard_map.59.refs_0_), channel_id=1, source_target_pairs={{0,4},{2,6},{4,0},{6,2},{8,12},{10,14},{12,8},{14,10},{1,5},{3,7},... | collective-permute-start | bytes 98312 | tf_op jit(solution)/shard_map/ppermute | solution.py:139
  9.6 2.1 %collective-permute-done.2.refs_1_ = bf16[4,4096]{1,0:T(4,128)(2,1)S(1)} collective-permute-done((bf16[4,4096]{1,0:T(4,128)(2,1)S(1)}, bf16[4,4096]{1,0:T(4,128)(2,1)S(1)}, u32[]{:S(2)}, u32[]{:S(2)}) %collective-permute-start.2) | collective-permute-done | bytes 32800 | tf_op jit(solution)/shard_map/ppermute | solution.py:139
  11.7 1.8 %collective-permute-start.3 = (bf16[8,4096]{1,0:T(8,128)(2,1)S(1)}, bf16[8,4096]{1,0:T(8,128)(2,1)S(1)}, u32[]{:S(2)}, u32[]{:S(2)}) collective-permute-start(bf16[8,4096]{1,0:T(8,128)(2,1)S(1)} %shard_map.60.refs_0_), channel_id=1, source_target_pairs={{0,2},{2,0},{4,6},{6,4},{8,10},{10,8},{12,14},{14,12},{1,3},{3,1},... | collective-permute-start | bytes 196616 | tf_op jit(solution)/shard_map/ppermute | solution.py:139
  13.5 2.5 %collective-permute-done.3.refs_1_ = bf16[8,4096]{1,0:T(8,128)(2,1)S(1)} collective-permute-done((bf16[8,4096]{1,0:T(8,128)(2,1)S(1)}, bf16[8,4096]{1,0:T(8,128)(2,1)S(1)}, u32[]{:S(2)}, u32[]{:S(2)}) %collective-permute-start.3) | collective-permute-done | bytes 65568 | tf_op jit(solution)/shard_map/ppermute | solution.py:139
  16.1 0.0 slice-start.13
  16.1 3.7 %shard_map.63 = (f32[16,3328]{1,0:T(8,128)S(1)}, bf16[512,4096]{1,0:T(8,128)(2,1)S(1)}) custom-call(bf16[16,4096]{1,0:T(8,128)(2,1)S(1)} %shard_map.61.refs_0_, bf16[4096,3328]{1,0:T(8,128)(2,1)S(1)} %bitcast.4, bf16[3328,4096]{1,0:T(8,128)(2,1)} %refs_4_.1), custom_call_target="tpu_custom_call" | custom-call | flops 436207616 | bytes 27262976 | tf_op jit(solution)/shard_map/pallas_call | solution.py:27
  19.8 0.1 collective-permute-start.5
  20.0 4.0 %shard_map.62 = (f32[16,3328]{1,0:T(8,128)S(1)}, bf16[16,3328]{1,0:T(8,128)(2,1)S(1)}, bf16[1280,4096]{1,0:T(8,128)(2,1)S(1)}) custom-call(bf16[16,4096]{1,0:T(8,128)(2,1)S(1)} %shard_map.61.refs_0_, bf16[4096,3328]{1,0:T(8,128)(2,1)S(1)} %bitcast.6, bf16[3328,4096]{1,0:T(8,128)(2,1)} %refs_4_.1), custom_call_target="tpu_custom_call" | custom-call | flops 436207616 | bytes 27262976 | tf_op jit(solution)/shard_map/pallas_call | solution.py:27
  24.0 0.5 %collective-permute-start.4 = (bf16[16,3328]{1,0:T(8,128)(2,1)S(1)}, bf16[16,3328]{1,0:T(8,128)(2,1)S(1)}, u32[]{:S(2)}, u32[]{:S(2)}) collective-permute-start(bf16[16,3328]{1,0:T(8,128)(2,1)S(1)} %get-tuple-element.21), channel_id=1, source_target_pairs={{0,1},{1,0},{2,3},{3,2},{4,5},{5,4},{6,7},{7,6},{8,9},{9,8},{10,11... | collective-permute-start | bytes 319496 | tf_op jit(solution)/shard_map/ppermute | solution.py:139
  24.5 1.0 %collective-permute-done.4.refs_1_ = bf16[16,3328]{1,0:T(8,128)(2,1)S(1)} collective-permute-done((bf16[16,3328]{1,0:T(8,128)(2,1)S(1)}, bf16[16,3328]{1,0:T(8,128)(2,1)S(1)}, u32[]{:S(2)}, u32[]{:S(2)}) %collective-permute-start.4) | collective-permute-done | bytes 106528 | tf_op jit(solution)/shard_map/ppermute | solution.py:139
  25.5 5.0 %shard_map.64 = (f32[8,4096]{1,0:T(8,128)S(1)}, bf16[8,4096]{1,0:T(8,128)(2,1)S(1)}) custom-call(f32[16,3328]{1,0:T(8,128)S(1)} %get-tuple-element.20.refs_0_, bf16[16,3328]{1,0:T(8,128)(2,1)S(1)} %collective-permute-done.4.refs_1_, f32[16,3328]{1,0:T(8,128)S(1)} %get-tuple-element.22.refs_2_, f32[16,3328]{1,0:T(8,128)S(1)} %collective-permute-done.5.refs_3_, ...), custom_call_target="tpu_custom_call" | custom-call | flops 436207616 | bytes 27262976 | tf_op jit(solution)/shard_map/pallas_call | solution.py:27
  30.5 1.8 %collective-permute-start.6 = (bf16[8,4096]{1,0:T(8,128)(2,1)S(1)}, bf16[8,4096]{1,0:T(8,128)(2,1)S(1)}, u32[]{:S(2)}, u32[]{:S(2)}) collective-permute-start(bf16[8,4096]{1,0:T(8,128)(2,1)S(1)} %get-tuple-element.26), channel_id=1, source_target_pairs={{0,2},{2,0},{4,6},{6,4},{8,10},{10,8},{12,14},{14,12},{1,3},{3,1},... | collective-permute-start | bytes 196616 | tf_op jit(solution)/shard_map/ppermute | solution.py:139
  32.3 2.6 %collective-permute-done.6.refs_1_ = bf16[8,4096]{1,0:T(8,128)(2,1)S(1)} collective-permute-done((bf16[8,4096]{1,0:T(8,128)(2,1)S(1)}, bf16[8,4096]{1,0:T(8,128)(2,1)S(1)}, u32[]{:S(2)}, u32[]{:S(2)}) %collective-permute-start.6) | collective-permute-done | bytes 65568 | tf_op jit(solution)/shard_map/ppermute | solution.py:139
  34.9 1.9 %collective-permute-start.7 = (bf16[4,4096]{1,0:T(4,128)(2,1)S(1)}, bf16[4,4096]{1,0:T(4,128)(2,1)S(1)}, u32[]{:S(2)}, u32[]{:S(2)}) collective-permute-start(bf16[4,4096]{1,0:T(4,128)(2,1)S(1)} %get-tuple-element.28), channel_id=1, source_target_pairs={{0,4},{2,6},{4,0},{6,2},{8,12},{10,14},{12,8},{14,10},{1,5},{3,7},... | collective-permute-start | bytes 98312 | tf_op jit(solution)/shard_map/ppermute | solution.py:139
  36.8 2.1 %collective-permute-done.7.refs_1_ = bf16[4,4096]{1,0:T(4,128)(2,1)S(1)} collective-permute-done((bf16[4,4096]{1,0:T(4,128)(2,1)S(1)}, bf16[4,4096]{1,0:T(4,128)(2,1)S(1)}, u32[]{:S(2)}, u32[]{:S(2)}) %collective-permute-start.7) | collective-permute-done | bytes 32800 | tf_op jit(solution)/shard_map/ppermute | solution.py:139
  38.9 2.9 %collective-permute-start.8 = (bf16[2,4096]{1,0:T(2,128)(2,1)S(1)}, bf16[2,4096]{1,0:T(2,128)(2,1)S(1)}, u32[]{:S(2)}, u32[]{:S(2)}) collective-permute-start(bf16[2,4096]{1,0:T(2,128)(2,1)S(1)} %get-tuple-element.30), channel_id=1, source_target_pairs={{0,8},{2,10},{4,12},{6,14},{8,0},{10,2},{12,4},{14,6},{1,9},{3,11}... | collective-permute-start | bytes 49160 | tf_op jit(solution)/shard_map/ppermute | solution.py:139
  41.8 1.8 %collective-permute-done.8.refs_1_ = bf16[2,4096]{1,0:T(2,128)(2,1)S(1)} collective-permute-done((bf16[2,4096]{1,0:T(2,128)(2,1)S(1)}, bf16[2,4096]{1,0:T(2,128)(2,1)S(1)}, u32[]{:S(2)}, u32[]{:S(2)}) %collective-permute-start.8) | collective-permute-done | bytes 16416 | tf_op jit(solution)/shard_map/ppermute | solution.py:139
  43.6 0.6 %shard_map.67 = bf16[2,4096]{1,0:T(2,128)(2,1)} custom-call(f32[2,4096]{1,0:T(2,128)S(1)} %get-tuple-element.29.refs_0_, bf16[2,4096]{1,0:T(2,128)(2,1)S(1)} %collective-permute-done.8.refs_1_), custom_call_target="tpu_custom_call" | custom-call | tf_op jit(solution)/shard_map/pallas_call | solution.py:27
  (33 shorter events, 0.1 us)
Async XLA Ops:
  0.0 16.1 %slice-start = ((s8[27262976]{0:T(1024)(128)(4,1)}), s8[4194304]{0:T(1024)(128)(4,1)S(1)}, s32[]{:S(2)}) async-start(s8[27262976]{0:T(1024)(128)(4,1)} %bitcast.3), calls=%async_computation | async-start | bytes 8388608
  0.0 0.9 %copy-start = (bf16[2,1,4096]{2,0,1:T(2,128)(2,1)S(1)}, bf16[2,1,4096]{2,0,1:T(2,128)(2,1)}, u32[]{:S(2)}) copy-start(bf16[2,1,4096]{2,0,1:T(2,128)(2,1)} %param.5) | copy-start | bytes 49156
  0.0 0.9 %copy-start.1 = (f32[4096]{0:T(1024)S(1)}, f32[4096]{0:T(1024)}, u32[]{:S(2)}) copy-start(f32[4096]{0:T(1024)} %param.6) | copy-start | bytes 49156
  0.0 16.1 %slice-start.1 = ((s8[27262976]{0:T(1024)(128)(4,1)}), s8[4194304]{0:T(1024)(128)(4,1)S(1)}, s32[]{:S(2)}) async-start(s8[27262976]{0:T(1024)(128)(4,1)} %bitcast.3), calls=%async_computation.1 | async-start | bytes 8388608
  0.0 16.1 %slice-start.2 = ((s8[27262976]{0:T(1024)(128)(4,1)}), s8[4194304]{0:T(1024)(128)(4,1)S(1)}, s32[]{:S(2)}) async-start(s8[27262976]{0:T(1024)(128)(4,1)} %bitcast.3), calls=%async_computation.2 | async-start | bytes 8388608
  0.0 16.1 %slice-start.3 = ((s8[27262976]{0:T(1024)(128)(4,1)}), s8[4194304]{0:T(1024)(128)(4,1)S(1)}, s32[]{:S(2)}) async-start(s8[27262976]{0:T(1024)(128)(4,1)} %bitcast.3), calls=%async_computation.3 | async-start | bytes 8388608
  0.0 16.1 %slice-start.4 = ((s8[27262976]{0:T(1024)(128)(4,1)}), s8[4194304]{0:T(1024)(128)(4,1)S(1)}, s32[]{:S(2)}) async-start(s8[27262976]{0:T(1024)(128)(4,1)} %bitcast.3), calls=%async_computation.4 | async-start | bytes 8388608
  0.0 16.1 %slice-start.5 = ((s8[27262976]{0:T(1024)(128)(4,1)}), s8[4194304]{0:T(1024)(128)(4,1)S(1)}, s32[]{:S(2)}) async-start(s8[27262976]{0:T(1024)(128)(4,1)} %bitcast.3), calls=%async_computation.5 | async-start | bytes 8388608
  0.1 16.1 %slice-start.6 = ((s8[27262976]{0:T(1024)(128)(4,1)}), s8[2097152]{0:T(1024)(128)(4,1)S(1)}, s32[]{:S(2)}) async-start(s8[27262976]{0:T(1024)(128)(4,1)} %bitcast.3), calls=%async_computation.6 | async-start | bytes 4194304
  0.1 19.8 %slice-start.7 = ((s8[27262976]{0:T(1024)(128)(4,1)}), s8[2097152]{0:T(1024)(128)(4,1)S(1)}, s32[]{:S(2)}) async-start(s8[27262976]{0:T(1024)(128)(4,1)} %bitcast.5), calls=%async_computation.7 | async-start | bytes 4194304
  0.1 19.8 %slice-start.8 = ((s8[27262976]{0:T(1024)(128)(4,1)}), s8[4194304]{0:T(1024)(128)(4,1)S(1)}, s32[]{:S(2)}) async-start(s8[27262976]{0:T(1024)(128)(4,1)} %bitcast.5), calls=%async_computation.8 | async-start | bytes 8388608
  0.1 19.8 %slice-start.9 = ((s8[27262976]{0:T(1024)(128)(4,1)}), s8[4194304]{0:T(1024)(128)(4,1)S(1)}, s32[]{:S(2)}) async-start(s8[27262976]{0:T(1024)(128)(4,1)} %bitcast.5), calls=%async_computation.9 | async-start | bytes 8388608
  0.1 19.8 %slice-start.10 = ((s8[27262976]{0:T(1024)(128)(4,1)}), s8[4194304]{0:T(1024)(128)(4,1)S(1)}, s32[]{:S(2)}) async-start(s8[27262976]{0:T(1024)(128)(4,1)} %bitcast.5), calls=%async_computation.10 | async-start | bytes 8388608
  0.1 19.8 %slice-start.11 = ((s8[27262976]{0:T(1024)(128)(4,1)}), s8[4194304]{0:T(1024)(128)(4,1)S(1)}, s32[]{:S(2)}) async-start(s8[27262976]{0:T(1024)(128)(4,1)} %bitcast.5), calls=%async_computation.11 | async-start | bytes 8388608
  0.1 19.8 %slice-start.12 = ((s8[27262976]{0:T(1024)(128)(4,1)}), s8[4194304]{0:T(1024)(128)(4,1)S(1)}, s32[]{:S(2)}) async-start(s8[27262976]{0:T(1024)(128)(4,1)} %bitcast.5), calls=%async_computation.12 | async-start | bytes 8388608
  0.9 1.4 %collective-permute-start = (f32[3,4096]{1,0:T(4,128)S(1)}, f32[3,4096]{1,0:T(4,128)S(1)}, u32[]{:S(2)}, u32[]{:S(2)}) collective-permute-start(f32[3,4096]{1,0:T(4,128)S(1)} %shard_map.57.refs_0_), channel_id=1, source_target_pairs={{0,1},{1,0},{2,3},{3,2},{4,5},{5,4},{6,7},{7,6},{8,9},{9,8},{10,11... | collective-permute-start | bytes 147464 | tf_op jit(solution)/shard_map/ppermute | solution.py:139
  2.5 5.2 %collective-permute-start.1 = (bf16[2,4096]{1,0:T(2,128)(2,1)S(1)}, bf16[2,4096]{1,0:T(2,128)(2,1)S(1)}, u32[]{:S(2)}, u32[]{:S(2)}) collective-permute-start(bf16[2,4096]{1,0:T(2,128)(2,1)S(1)} %get-tuple-element.19), channel_id=1, source_target_pairs={{0,9},{1,8},{2,11},{3,10},{4,13},{5,12},{6,15},{7,14},{8,1},{9,0},... | collective-permute-start | bytes 49160 | tf_op jit(solution)/shard_map/ppermute | solution.py:133
  7.7 4.0 %collective-permute-start.2 = (bf16[4,4096]{1,0:T(4,128)(2,1)S(1)}, bf16[4,4096]{1,0:T(4,128)(2,1)S(1)}, u32[]{:S(2)}, u32[]{:S(2)}) collective-permute-start(bf16[4,4096]{1,0:T(4,128)(2,1)S(1)} %shard_map.59.refs_0_), channel_id=1, source_target_pairs={{0,4},{2,6},{4,0},{6,2},{8,12},{10,14},{12,8},{14,10},{1,5},{3,7},... | collective-permute-start | bytes 98312 | tf_op jit(solution)/shard_map/ppermute | solution.py:139
  11.7 4.3 %collective-permute-start.3 = (bf16[8,4096]{1,0:T(8,128)(2,1)S(1)}, bf16[8,4096]{1,0:T(8,128)(2,1)S(1)}, u32[]{:S(2)}, u32[]{:S(2)}) collective-permute-start(bf16[8,4096]{1,0:T(8,128)(2,1)S(1)} %shard_map.60.refs_0_), channel_id=1, source_target_pairs={{0,2},{2,0},{4,6},{6,4},{8,10},{10,8},{12,14},{14,12},{1,3},{3,1},... | collective-permute-start | bytes 196616 | tf_op jit(solution)/shard_map/ppermute | solution.py:139
  16.1 3.8 %slice-start.13 = ((s8[27262976]{0:T(1024)(128)(4,1)}), s8[4194304]{0:T(1024)(128)(4,1)S(1)}, s32[]{:S(2)}) async-start(s8[27262976]{0:T(1024)(128)(4,1)} %bitcast.5), calls=%async_computation.13 | async-start | bytes 8388608
  19.8 5.7 %collective-permute-start.5 = (f32[16,3328]{1,0:T(8,128)S(1)}, f32[16,3328]{1,0:T(8,128)S(1)}, u32[]{:S(2)}, u32[]{:S(2)}) collective-permute-start(f32[16,3328]{1,0:T(8,128)S(1)} %get-tuple-element.22.refs_2_), channel_id=1, source_target_pairs={{0,1},{1,0},{2,3},{3,2},{4,5},{5,4},{6,7},{7,6},{8,9},{9,8},{10,11... | collective-permute-start | bytes 638984 | tf_op jit(solution)/shard_map/ppermute | solution.py:139
  24.0 1.5 %collective-permute-start.4 = (bf16[16,3328]{1,0:T(8,128)(2,1)S(1)}, bf16[16,3328]{1,0:T(8,128)(2,1)S(1)}, u32[]{:S(2)}, u32[]{:S(2)}) collective-permute-start(bf16[16,3328]{1,0:T(8,128)(2,1)S(1)} %get-tuple-element.21), channel_id=1, source_target_pairs={{0,1},{1,0},{2,3},{3,2},{4,5},{5,4},{6,7},{7,6},{8,9},{9,8},{10,11... | collective-permute-start | bytes 319496 | tf_op jit(solution)/shard_map/ppermute | solution.py:139
  30.5 4.4 %collective-permute-start.6 = (bf16[8,4096]{1,0:T(8,128)(2,1)S(1)}, bf16[8,4096]{1,0:T(8,128)(2,1)S(1)}, u32[]{:S(2)}, u32[]{:S(2)}) collective-permute-start(bf16[8,4096]{1,0:T(8,128)(2,1)S(1)} %get-tuple-element.26), channel_id=1, source_target_pairs={{0,2},{2,0},{4,6},{6,4},{8,10},{10,8},{12,14},{14,12},{1,3},{3,1},... | collective-permute-start | bytes 196616 | tf_op jit(solution)/shard_map/ppermute | solution.py:139
  34.9 4.0 %collective-permute-start.7 = (bf16[4,4096]{1,0:T(4,128)(2,1)S(1)}, bf16[4,4096]{1,0:T(4,128)(2,1)S(1)}, u32[]{:S(2)}, u32[]{:S(2)}) collective-permute-start(bf16[4,4096]{1,0:T(4,128)(2,1)S(1)} %get-tuple-element.28), channel_id=1, source_target_pairs={{0,4},{2,6},{4,0},{6,2},{8,12},{10,14},{12,8},{14,10},{1,5},{3,7},... | collective-permute-start | bytes 98312 | tf_op jit(solution)/shard_map/ppermute | solution.py:139
  38.9 4.7 %collective-permute-start.8 = (bf16[2,4096]{1,0:T(2,128)(2,1)S(1)}, bf16[2,4096]{1,0:T(2,128)(2,1)S(1)}, u32[]{:S(2)}, u32[]{:S(2)}) collective-permute-start(bf16[2,4096]{1,0:T(2,128)(2,1)S(1)} %get-tuple-element.30), channel_id=1, source_target_pairs={{0,8},{2,10},{4,12},{6,14},{8,0},{10,2},{12,4},{14,6},{1,9},{3,11}... | collective-permute-start | bytes 49160 | tf_op jit(solution)/shard_map/ppermute | solution.py:139
